TPU v7x, 256 devices: a whole 4x4x8 slice. The times are simulated.
256 devices in a mesh: vocab: 16 (over y_lo, x, core), dp: 16 (over z, y_hi).
Axes of the slice: x: 4, y: 4 (y_hi: 2, y_lo: 2; y = y_hi * 2 + y_lo), z: 8, core: 2. Of those that a mesh axis runs over, the one named last changes fastest.
Arguments:
- features: bfloat16 [4096, 4096], P('dp'), may hold values from -6 to 6
- token_ids: int32 [4096], P('dp'), may hold values from 0 to 16383
- positions: int32 [4096], replicated, may hold values from 0 to 4095, each once
- target_buffer: bfloat16 [4096, 16384], P(None, ('vocab', 'dp')), may hold values from -96 to 320
- norm_gain: float32 [4096], replicated, may hold values from 0.25 to 1.75
- final_gain: float32 [4096], replicated, may hold values from 0.25 to 1.75
- w_in: bfloat16 [4096, 7168], P(None, 'vocab'), may hold values from -0.09375 to 0.09375
- w_out: bfloat16 [7168, 4096], P('vocab'), may hold values from -0.0625 to 0.0625
- head_weight: bfloat16 [4096, 16384], P('dp', 'vocab'), may hold values from -4 to 4
Outputs:
- grad_head: float32 [4096, 16384], P('dp', 'vocab')
- grad_in: float32 [4096, 7168], P('dp', 'vocab')
- grad_out: float32 [7168, 4096], P('vocab', 'dp')
All inputs are finite; a program needn't handle non-finite values.
Results may differ from a plain program's by a relative error of at most 0.04.
Values may be sent and summed in bfloat16 or wider, within the bound.
A program may use at most 128 MiB of HBM per device.

v0:
```python
import jax
import jax.numpy as jnp
from jax import lax
from jax.sharding import PartitionSpec as P

EPS = 1e-05
HARD = 0.5


def body(
    features, token_ids, positions, target_buffer, norm_gain, final_gain, w_in, w_out, head_weight
):
    groups = lax.axis_size("dp")
    tok = features.shape[0]
    vwidth = target_buffer.shape[1] * groups
    ordered = target_buffer[positions].reshape(groups, tok, target_buffer.shape[1])
    target = lax.all_to_all(ordered, "dp", split_axis=0, concat_axis=2, tiled=True)[0]
    xfloat = features.astype(jnp.float32)
    rinput = lax.rsqrt(jnp.mean(xfloat * xfloat, -1, keepdims=True) + EPS)
    normed = (xfloat * rinput * norm_gain).astype(jnp.bfloat16)
    pre = jnp.dot(normed, w_in, preferred_element_type=jnp.float32)
    act = jax.nn.silu(pre).astype(jnp.bfloat16)
    hidden = lax.psum(
        jnp.dot(act, w_out, preferred_element_type=jnp.float32).astype(jnp.bfloat16), "vocab"
    ).astype(jnp.float32)
    resid = xfloat + hidden
    rscale = lax.rsqrt(jnp.mean(resid * resid, -1, keepdims=True) + EPS)
    final = (resid * rscale * final_gain).astype(jnp.bfloat16)
    backward = (((1,), (1,)), ((), ()))
    contract = (((0,), (0,)), ((), ()))
    full_head = lax.all_gather(head_weight, "dp", axis=0, tiled=True)
    logits = jnp.dot(final, full_head, preferred_element_type=jnp.float32)
    tfloat = target.astype(jnp.float32)
    top_q, top_p = lax.pmax((jnp.max(logits, -1), jnp.max(tfloat, -1)), "vocab")
    qexp = jnp.exp(logits - top_q[:, None])
    pexp = jnp.exp(tfloat - top_p[:, None])
    sum_q, sum_p = lax.psum((jnp.sum(qexp, -1), jnp.sum(pexp, -1)), "vocab")
    qprob = qexp / sum_q[:, None]
    pprob = pexp / sum_p[:, None]
    columns_here = lax.axis_index("vocab") * vwidth + jnp.arange(vwidth, dtype=jnp.int32)
    onehot = (columns_here[None, :] == token_ids[:, None]).astype(jnp.float32)
    dlogits = (qprob - pprob + HARD * (qprob - onehot)).astype(jnp.bfloat16)
    partial_final = lax.dot_general(
        dlogits, full_head, backward, preferred_element_type=jnp.float32
    )
    dfinal = lax.psum(partial_final.astype(jnp.bfloat16), "vocab").astype(jnp.float32)
    inner = jnp.sum(dfinal * final_gain * resid, -1, keepdims=True)
    width = features.shape[1]
    dresid = (rscale * final_gain * dfinal - resid * rscale**3 / width * inner).astype(jnp.bfloat16)
    dact = lax.dot_general(dresid, w_out, backward, preferred_element_type=jnp.float32)
    sig = jax.nn.sigmoid(pre)
    dpre = (dact * sig * (1.0 + pre * (1.0 - sig))).astype(jnp.bfloat16)
    hwidth = w_in.shape[1]
    summed = lax.psum_scatter(
        jnp.concatenate(
            [
                lax.dot_general(final, dlogits, contract, preferred_element_type=jnp.float32),
                jnp.concatenate(
                    [
                        lax.dot_general(normed, dpre, contract, preferred_element_type=jnp.float32),
                        lax.dot_general(dresid, act, contract, preferred_element_type=jnp.float32),
                    ],
                    1,
                ),
            ],
            1,
        ).astype(jnp.bfloat16),
        "dp",
        scatter_dimension=0,
        tiled=True,
    ).astype(jnp.float32)
    grad_head = summed[:, :vwidth]
    grad_in = summed[:, vwidth : vwidth + hwidth]
    grad_out = summed[:, vwidth + hwidth :].T
    return (grad_head, grad_in, grad_out)


def solution(mesh):
    return jax.shard_map(
        body,
        mesh=mesh,
        in_specs=(
            P("dp", None),
            P("dp"),
            P(),
            P(None, ("vocab", "dp")),
            P(),
            P(),
            P(None, "vocab"),
            P("vocab", None),
            P("dp", "vocab"),
        ),
        out_specs=(P("dp", "vocab"), P("dp", "vocab"), P("vocab", "dp")),
        check_vma=False,
    )
```

profile of v0, /device:TPU:1, one launch (start us, length us, event | category | flops | bytes accessed | tf_op | source)
XLA Modules:
  0.0 695.0 jit_solution(14237104393546704227)
XLA Ops:
  8.0 2.1 fusion.4
  10.1 4.1 fusion.11
  15.0 2.6 convolution_convert_fusion.4
  18.7 12.1 %gather_fusion = bf16[4096,64]{1,0:T(8,128)(2,1)S(1)} fusion(bf16[4096,64]{1,0:T(8,128)(2,1)S(1)} %copy.15, s32[4096]{0:T(1024)S(1)} %fusion.17), kind=kCustom, calls=%fused_computation | custom fusion | bytes 1064960 | tf_op jit(solution)/shard_map/gather | solution.py:16
  32.0 11.7 %all-to-all-start = ((bf16[16,256,64]{1,2,0:T(8,128)(2,1)}), bf16[16,256,64]{1,2,0:T(8,128)(2,1)S(1)}, u32[]{:S(2)}, u32[]{:S(2)}) async-start(bf16[16,256,64]{1,2,0:T(8,128)(2,1)} %copy.16), calls=%async_computation | async-start | bytes 1048576 | tf_op jit(solution)/shard_map/all_to_all | solution.py:17
  43.9 20.4 %all-to-all-done = bf16[16,256,64]{1,2,0:T(8,128)(2,1)S(1)} async-done(((bf16[16,256,64]{1,2,0:T(8,128)(2,1)}), bf16[16,256,64]{1,2,0:T(8,128)(2,1)S(1)}, u32[]{:S(2)}, u32[]{:S(2)}) %all-to-all-start) | async-done | bytes 524320 | tf_op jit(solution)/shard_map/all_to_all | solution.py:17
  65.4 2.5 copy.17
  67.9 83.9 %all-reduce.5.cloned.1.call-done = bf16[256,4096]{1,0:T(8,128)(2,1)} async-done(((bf16[256,4096]{1,0:T(8,128)(2,1)}), bf16[256,4096]{1,0:T(8,128)(2,1)}) %all-reduce.5.cloned.1.call-update) | async-done | bytes 2097168 | tf_op jit(solution)/shard_map/psum | solution.py:23
  151.8 2.4 multiply_reduce_fusion
  154.2 23.0 %all-gather.2.cloned.1.call-done = bf16[4096,1024]{1,0:T(8,128)(2,1)} async-done(((bf16[256,1024]{1,0:T(8,128)(2,1)}), bf16[4096,1024]{1,0:T(8,128)(2,1)}) %all-gather.2.cloned.1.call-update) | async-done | bytes 8388624 | tf_op jit(solution)/shard_map/all_gather | solution.py:31
  177.3 7.4 %fusion.21 = (f32[256]{0:T(256)S(1)}, f32[256,1024]{1,0:T(8,128)}) fusion(bf16[4096,1024]{1,0:T(8,128)(2,1)} %all-gather.2.cloned.1.call-done, bf16[256,4096]{1,0:T(8,128)(2,1)} %all-reduce.5.cloned.1.call-done, bf16[256,4096]{1,0:T(8,128)(2,1)S(1)} %copy-done, f32[4096]{0:T(1024)S(1)} %copy-done.9, f32[256]{0:T(256)S(1)} %get-tuple-element.16), kind=kOutput, calls=%fused_computation.47 | convolution fusion | flops 2154036992 | bytes 13649920 | tf_op jit(solution)/shard_map/dot_general | solution.py:32
  184.6 28.3 %all-reduce.1 = (f32[256]{0:T(256)S(1)}, f32[256]{0:T(256)S(1)}) all-reduce(bf16[256]{0:T(256)(128)(2,1)S(1)} %get-tuple-element.13, f32[256]{0:T(256)S(1)} %get-tuple-element.17), channel_id=1, replica_groups=mesh['vocab'=16,'dp'=16] {'vocab'}, use_global_device_ids=true, to_apply=%region_8.9 | all-reduce | flops 512 | bytes 3584 | tf_op jit(solution)/shard_map/pmax | solution.py:34
  213.0 1.5 fusion.9
  214.7 28.9 %all-reduce = (f32[256]{0:T(256)S(1)}, f32[256]{0:T(256)S(1)}) all-reduce(f32[256]{0:T(256)S(1)} %exponential_reduce_fusion, f32[256]{0:T(256)S(1)} %fusion.9), channel_id=1, replica_groups=mesh['vocab'=16,'dp'=16] {'vocab'}, use_global_device_ids=true, to_apply=%region_10.11 | all-reduce | flops 512 | bytes 4096 | tf_op jit(solution)/shard_map/psum | solution.py:37
  243.6 8.3 %convolution_convert_fusion.3 = bf16[256,4096]{1,0:T(8,128)(2,1)} fusion(bf16[4096,1024]{1,0:T(8,128)(2,1)} %all-gather.2.cloned.1.call-done, f32[256,1024]{1,0:T(8,128)} %copy.17, f32[256,1024]{1,0:T(8,128)} %get-tuple-element.18, s32[1024]{0:T(1024)S(1)} %iota_add_fusion, f32[256]{0:T(256)S(1)} %get-tuple-element.9, f32[256]{0:T(256)S(1)} %get-tuple-element.11, ...), kind=kOutput, calls=%fused_computation.10 | convolution fusion | flops 2151415808 | bytes 12592128 | tf_op jit(solution)/shard_map/dot_general | solution.py:43
  252.1 8.2 %convolution_convert_fusion = bf16[4096,1024]{0,1:T(8,128)(2,1)} fusion(bf16[256,4096]{1,0:T(8,128)(2,1)} %all-reduce.5.cloned.1.call-done, bf16[256,4096]{1,0:T(8,128)(2,1)S(1)} %copy-done, f32[4096]{0:T(1024)S(1)} %copy-done.9, f32[256]{0:T(256)S(1)} %get-tuple-element.16, f32[256,1024]{1,0:T(8,128)S(1)} %copy-done.5, f32[256,1024]{1,0:T(8,128)} %get-tuple-element.18, ...), kind=kOutput, calls=%fused_computation.2 | convolution fusion | flops 2160852992 | bytes 14706688 | tf_op jit(solution)/shard_map/dot_general | solution.py:57
  260.4 114.5 %all-reduce.7.cloned.1.call-done = bf16[256,4096]{1,0:T(8,128)(2,1)} async-done(((bf16[256,4096]{1,0:T(8,128)(2,1)}), bf16[256,4096]{1,0:T(8,128)(2,1)}) %all-reduce.7.cloned.1.call-update) | async-done | bytes 2097168 | tf_op jit(solution)/shard_map/psum | solution.py:46
  374.9 3.4 fusion.3
  378.4 3.3 fusion.1
  381.7 8.5 %convolution_convert_fusion.2 = bf16[4096,448]{0,1:T(8,128)(2,1)} fusion(bf16[256,4096]{1,0:T(8,128)(2,1)} %fusion.1, bf16[448,4096]{1,0:T(8,128)(2,1)} %param.16, bf16[256,4096]{1,0:T(8,128)(2,1)S(1)} %copy-done, f32[4096]{0:T(1024)S(1)} %copy-done.12, f32[256]{0:T(256)S(1)} %add_rsqrt_fusion.1, f32[256,448]{0,1:T(8,128)S(1)} %copy-done.7), kind=kOutput, calls=%fused_computation.7 | convolution fusion | flops 1886109696 | bytes 12010496 | tf_op jit(solution)/shard_map/dot_general | solution.py:60
  390.2 2.9 convolution_convert_fusion.1
  393.0 10.5 %pad_maximum_fusion = bf16[4096,1920]{0,1:T(8,128)(2,1)} fusion(bf16[4096,448]{0,1:T(8,128)(2,1)S(1)} %convolution_convert_fusion.1, bf16[4096,448]{0,1:T(8,128)(2,1)S(1)} %copy-done.4, bf16[4096,1024]{0,1:T(8,128)(2,1)} %convolution_convert_fusion), kind=kLoop, calls=%fused_computation.1 | loop fusion | flops 47185920 | bytes 31457280 | tf_op jit(solution)/shard_map/concatenate | solution.py:55
  403.6 279.8 %reduce-scatter.2.cloned.1.call-done = bf16[256,1920]{0,1:T(8,128)(2,1)} async-done(((bf16[4096,1920]{0,1:T(8,128)(2,1)}), bf16[256,1920]{0,1:T(8,128)(2,1)}) %reduce-scatter.2.cloned.1.call-update) | async-done | bytes 983056 | tf_op jit(solution)/shard_map/reduce_scatter | solution.py:54
  684.6 1.3 copy.18
  (49 shorter events, 7.7 us)
Async XLA Ops:
  8.0 143.8 %all-reduce.5.cloned.1.call-start = ((), (), s32[]{:S(2)}) async-start(), calls=%async_computation.2 | async-start | bytes 4194304 | tf_op jit(solution)/shard_map/psum | solution.py:23
  10.1 4.8 copy-start.11
  14.2 0.8 copy-start.6
  15.0 3.2 copy-start.8
  15.0 3.7 copy-start.10
  17.6 159.6 %all-gather.2.cloned.1.call-start = ((), (), s32[]{:S(2)}) async-start(), calls=%async_computation.3 | async-start | bytes 8912896 | tf_op jit(solution)/shard_map/all_gather | solution.py:31
  30.9 120.9 %copy-start = (bf16[256,4096]{1,0:T(8,128)(2,1)S(1)}, bf16[256,4096]{1,0:T(8,128)(2,1)}, u32[]{:S(2)}) copy-start(bf16[256,4096]{1,0:T(8,128)(2,1)} %param.9) | copy-start | bytes 6291460
  32.0 32.3 %all-to-all-start = ((bf16[16,256,64]{1,2,0:T(8,128)(2,1)}), bf16[16,256,64]{1,2,0:T(8,128)(2,1)S(1)}, u32[]{:S(2)}, u32[]{:S(2)}) async-start(bf16[16,256,64]{1,2,0:T(8,128)(2,1)} %copy.16), calls=%async_computation | async-start | bytes 1048576 | tf_op jit(solution)/shard_map/all_to_all | solution.py:17
  43.8 133.5 %copy-start.9 = (f32[4096]{0:T(1024)S(1)}, f32[4096]{0:T(1024)}, u32[]{:S(2)}) copy-start(f32[4096]{0:T(1024)} %param.14) | copy-start | bytes 49156
  43.8 331.1 %all-reduce.7.cloned.1.call-start = ((), (), s32[]{:S(2)}) async-start(), calls=%async_computation.4 | async-start | bytes 4194304 | tf_op jit(solution)/shard_map/psum | solution.py:46
  177.3 66.3 %copy-start.13 = (s32[256]{0:T(256)S(1)}, s32[256]{0:T(256)}, u32[]{:S(2)}) copy-start(s32[256]{0:T(256)} %param.10) | copy-start | bytes 3076
  243.6 8.5 %copy-start.5 = (f32[256,1024]{1,0:T(8,128)S(1)}, f32[256,1024]{1,0:T(8,128)}, u32[]{:S(2)}) copy-start(f32[256,1024]{1,0:T(8,128)} %copy.17) | copy-start | bytes 3145732
  251.9 431.4 %reduce-scatter.2.cloned.1.call-start = ((), (), s32[]{:S(2)}) async-start(), calls=%async_computation.5 | async-start | bytes 16711680 | tf_op jit(solution)/shard_map/reduce_scatter | solution.py:54
  374.9 3.4 copy-start.1
  374.9 3.5 copy-start.2
  378.4 3.3 copy-start.7
  378.4 3.3 copy-start.12
  390.2 2.9 copy-start.4
  683.3 2.5 copy-start.3
Sparse Core Ops, SparseCore 0:
  17.8 134.0 all-reduce.4
  252.0 122.8 all-reduce.6
Sparse Core Ops, SparseCore 1:
  20.7 156.5 all-gather.1
  403.6 279.6 reduce-scatter.1
where the time goes:
time: 696 us; the launch traced here: 695 us
  waiting for transfers between devices  522 us (75%)
  blocking collectives  57.2 us (8%)
  matrix products  41.9 us (6%)
  other arithmetic  24.7 us (4%)
  local copies, waits for them, and re-layouts  21.3 us (3%)
  between operations  15.7 us (2%)
  starting transfers between devices  12.1 us (2%)
    reduce_scatter x1, waiting for transfers between devices, body(): lax.psum_scatter(jnp.concatenate([lax.dot_general(final, dlogits, contrac...  280 us
    psum x1, waiting for transfers between devices, body(): lax.psum(partial_final.astype(jnp.bfloat16), 'vocab').astype(jnp.float32)  115 us
    psum x1, waiting for transfers between devices, body(): lax.psum(jnp.dot(act, w_out, preferred_element_type=jnp.float32).astype(j...  83.9 us
    psum x1, blocking collectives, body(): sum_q, sum_p = lax.psum((jnp.sum(qexp, -1), jnp.sum(pexp, -1)), 'vocab')  28.9 us
    pmax x1, blocking collectives, body(): top_q, top_p = lax.pmax((jnp.max(logits, -1), jnp.max(tfloat, -1)), 'vocab')  28.3 us
    all_gather x1, waiting for transfers between devices, body(): full_head = lax.all_gather(head_weight, 'dp', axis=0, tiled=True)  23 us
    all_to_all x1, waiting for transfers between devices, body(): lax.all_to_all(ordered, 'dp', split_axis=0, concat_axis=2, tiled=True)[0]  20.4 us
  transfers between devices with their start and end apart: 5, of which 5 were waited for; matrix products, arithmetic and copies ran while one was open for 4% of the time, Pallas kernels for 0%

commit v1 on v0

v1 whole, which is shorter than its diff:
```python
import jax
import jax.numpy as jnp
from jax import lax
from jax.sharding import Mesh, PartitionSpec as P

EPS = 1e-05
HARD = 0.5
PLANE = ("yhi", "ylo", "x", "core")


def body(
    features, token_ids, positions, target_buffer, norm_gain, final_gain, w_in, w_out, head_weight
):
    yhi = lax.axis_index("yhi")
    vocab = lax.axis_index(("ylo", "x", "core"))
    plane = lax.axis_index(PLANE)
    f32 = jnp.float32
    bf16 = jnp.bfloat16
    backward = (((1,), (1,)), ((), ()))
    contract = (((0,), (0,)), ((), ()))

    rows, cols = head_weight.shape
    hw = head_weight.reshape(rows, 8, 2, cols // 16)
    hw = lax.all_to_all(hw, "yhi", split_axis=2, concat_axis=0, tiled=True)
    hw = hw.reshape(rows * 2, cols // 2)
    full_head = lax.all_gather(hw, "z", axis=0, tiled=True)

    tw = target_buffer.shape[1]
    ordered = target_buffer[positions].reshape(8, -1, tw)
    target = lax.all_to_all(ordered, "z", split_axis=0, concat_axis=2, tiled=True)[0]

    feats = lax.all_gather(features, "yhi", axis=0, tiled=True)
    toks = lax.all_gather(token_ids, "yhi", axis=0, tiled=True)
    n_tok, width = feats.shape
    xfloat = feats.astype(f32)
    rinput = lax.rsqrt(jnp.mean(xfloat * xfloat, -1, keepdims=True) + EPS)
    normed = (xfloat * rinput * norm_gain).astype(bf16)
    fw = w_in.shape[1] // 2
    win = lax.dynamic_slice_in_dim(w_in, yhi * fw, fw, 1)
    wout = lax.dynamic_slice_in_dim(w_out, yhi * fw, fw, 0)
    pre = jnp.dot(normed, win, preferred_element_type=f32)
    act = jax.nn.silu(pre).astype(bf16)
    part = jnp.dot(act, wout, preferred_element_type=f32).astype(bf16)
    hidden = lax.psum_scatter(part, PLANE, scatter_dimension=0, tiled=True).astype(f32)
    own = hidden.shape[0]
    xown = lax.dynamic_slice_in_dim(feats, plane * own, own, 0).astype(f32)
    resid = xown + hidden
    rscale = lax.rsqrt(jnp.mean(resid * resid, -1, keepdims=True) + EPS)
    final = (resid * rscale * final_gain).astype(bf16)
    final = lax.all_gather(final, PLANE, axis=0, tiled=True)

    logits = jnp.dot(final, full_head, preferred_element_type=f32)
    tfloat = target.astype(f32)
    top_q = jnp.max(logits, -1)
    top_p = jnp.max(tfloat, -1)
    qexp = jnp.exp(logits - top_q[:, None])
    pexp = jnp.exp(tfloat - top_p[:, None])
    stats = jnp.stack([top_q, jnp.sum(qexp, -1), top_p, jnp.sum(pexp, -1)])
    every = lax.all_gather(stats, PLANE, axis=0)
    all_q = jnp.max(every[:, 0], 0)
    all_p = jnp.max(every[:, 2], 0)
    sum_q = jnp.sum(every[:, 1] * jnp.exp(every[:, 0] - all_q), 0)
    sum_p = jnp.sum(every[:, 3] * jnp.exp(every[:, 2] - all_p), 0)
    qprob = qexp * (jnp.exp(top_q - all_q) / sum_q)[:, None]
    pprob = pexp * (jnp.exp(top_p - all_p) / sum_p)[:, None]
    lane = jnp.arange(cols // 2, dtype=jnp.int32)
    columns_here = vocab * cols + (lane // tw) * (2 * tw) + yhi * tw + lane % tw
    onehot = (columns_here[None, :] == toks[:, None]).astype(f32)
    dlogits = (qprob - pprob + HARD * (qprob - onehot)).astype(bf16)

    part = lax.dot_general(dlogits, full_head, backward, preferred_element_type=f32).astype(bf16)
    dfinal = lax.psum_scatter(part, PLANE, scatter_dimension=0, tiled=True).astype(f32)
    inner = jnp.sum(dfinal * final_gain * resid, -1, keepdims=True)
    dresid = (rscale * final_gain * dfinal - resid * rscale**3 / width * inner).astype(bf16)
    dresid = lax.all_gather(dresid, PLANE, axis=0, tiled=True)

    gh = lax.dot_general(final, dlogits, contract, preferred_element_type=f32).astype(bf16)
    gh = lax.psum_scatter(gh, "z", scatter_dimension=0, tiled=True)
    gh = lax.all_to_all(
        gh.reshape(rows * 2, 8, 1, tw), "yhi", split_axis=0, concat_axis=2, tiled=True
    ).reshape(rows, cols).astype(f32)

    dact = lax.dot_general(dresid, wout, backward, preferred_element_type=f32)
    sig = jax.nn.sigmoid(pre)
    dpre = (dact * sig * (1.0 + pre * (1.0 - sig))).astype(bf16)
    gf = jnp.concatenate(
        [
            lax.dot_general(normed, dpre, contract, preferred_element_type=f32),
            lax.dot_general(dresid, act, contract, preferred_element_type=f32),
        ],
        1,
    ).astype(bf16)
    gf = lax.psum_scatter(gf, "z", scatter_dimension=0, tiled=True)
    gf = lax.all_to_all(
        gf.reshape(rows * 2, 2, fw), "yhi", split_axis=0, concat_axis=2, tiled=True
    ).astype(f32)
    return (gh, gf[:, 0], gf[:, 1].T)


def solution(mesh):
    names = ("ylo", "x", "core", "z", "yhi")
    fine = Mesh(mesh.devices.reshape(2, 4, 2, 8, 2), names)
    v = ("ylo", "x", "core")
    d = ("z", "yhi")
    return jax.shard_map(
        body,
        mesh=fine,
        in_specs=(
            P(d, None),
            P(d),
            P(),
            P(None, v + d),
            P(),
            P(),
            P(None, v),
            P(v, None),
            P(d, v),
        ),
        out_specs=(P(d, v), P(d, v), P(v, d)),
        check_vma=False,
    )
```

time: 696 us -> 542 us (0.78)
  waiting for transfers between devices: 522 us -> 394 us
  blocking collectives: 57.2 us -> 40.5 us
  other arithmetic: 24.7 us -> 14.4 us
  matrix products: 41.9 us -> 34.4 us
    psum x2 -> x0, waiting for transfers between devices: 198 us -> none  [the longest x1 115 us: body(): lax.psum(partial_final.astype(jnp.bfloat16), 'vocab').astype(jnp.float32)]
    all_gather x1 -> x4, waiting for transfers between devices: 23 us -> 132 us  [the longest x1 69 us: body(): feats = lax.all_gather(features, 'yhi', axis=0, tiled=True)]
    reduce_scatter x1 -> x4, waiting for transfers between devices: 280 us -> 246 us  [the longest x2 160 us: body(): lax.psum_scatter(part, PLANE, scatter_dimension=0, tiled=True).astype(f32)]
    all_gather x0 -> x2, blocking collectives: none -> 29.2 us  [the longest x1 24.6 us: body(): every = lax.all_gather(stats, PLANE, axis=0)]
    psum x1 -> x0, blocking collectives: 28.9 us -> none  [body(): sum_q, sum_p = lax.psum((jnp.sum(qexp, -1), jnp.sum(pexp, -1)), 'vocab')]
    pmax x1 -> x0, blocking collectives: 28.3 us -> none  [body(): top_q, top_p = lax.pmax((jnp.max(logits, -1), jnp.max(tfloat, -1)), 'vocab')]
    all_to_all x0 -> x1, blocking collectives: none -> 11.3 us  [body(): hw = lax.all_to_all(hw, 'yhi', split_axis=2, concat_axis=0, tiled=True)]
    dot_general x7, matrix products: 41.9 us -> 34.4 us  [the longest x1 7.89 us: body(): lax.dot_general(normed, dpre, contract, preferred_element_type=f32)]
  transfers between devices with their start and end apart: 5 -> 11, of which waited for: 5 -> 9; matrix products, arithmetic and copies ran while one was open for 4% -> 9% of each run, Pallas kernels for 0% -> 0%
where the time goes in v1:
time: 542 us; the launch traced here: 541 us
  waiting for transfers between devices  394 us (73%)
  blocking collectives  40.5 us (7%)
  matrix products  34.4 us (6%)
  local copies, waits for them, and re-layouts  26.2 us (5%)
  between operations  15.8 us (3%)
  starting transfers between devices  15.3 us (3%)
  other arithmetic  14.4 us (3%)
    reduce_scatter x2, waiting for transfers between devices, body(): lax.psum_scatter(part, PLANE, scatter_dimension=0, tiled=True).astype(f32)  160 us
    all_gather x1, waiting for transfers between devices, body(): feats = lax.all_gather(features, 'yhi', axis=0, tiled=True)  69 us
    all_gather x1, waiting for transfers between devices, body(): dresid = lax.all_gather(dresid, PLANE, axis=0, tiled=True)  45.9 us
    reduce_scatter x1, waiting for transfers between devices, body(): gf = lax.psum_scatter(gf, 'z', scatter_dimension=0, tiled=True)  43.9 us
    reduce_scatter x1, waiting for transfers between devices, body(): gh = lax.psum_scatter(gh, 'z', scatter_dimension=0, tiled=True)  41.9 us
    all_gather x1, blocking collectives, body(): every = lax.all_gather(stats, PLANE, axis=0)  24.6 us
    all_gather x1, waiting for transfers between devices, body(): final = lax.all_gather(final, PLANE, axis=0, tiled=True)  17 us
    gather x1, local copies, waits for them, and re-layouts, body(): ordered = target_buffer[positions].reshape(8, -1, tw)  12.1 us
  transfers between devices with their start and end apart: 11, of which 9 were waited for; matrix products, arithmetic and copies ran while one was open for 9% of the time, Pallas kernels for 0%

profile of v1, /device:TPU:1, one launch (start us, length us, event | category | flops | bytes accessed | tf_op | source)
XLA Modules:
  0.0 540.7 jit_solution(8305544254634356896)
XLA Ops:
  8.8 69.0 %all-gather.8.cloned.1.call-done = bf16[512,4096]{1,0:T(8,128)(2,1)} async-done(((bf16[256,4096]{1,0:T(8,128)(2,1)}), bf16[512,4096]{1,0:T(8,128)(2,1)}) %all-gather.8.cloned.1.call-update) | async-done | bytes 4194320 | tf_op jit(solution)/shard_map/all_gather | solution.py:32
  81.3 3.2 fusion.3
  84.6 3.3 convolution_convert_fusion
  88.2 11.3 %all_to_all.42 = bf16[256,8,2,64]{0,3,1,2:T(8,128)(2,1)S(1)} all-to-all(bf16[256,8,2,64]{0,3,1,2:T(8,128)(2,1)S(1)} %copy.55), channel_id=1, replica_groups=mesh['ylo'=2,'x'=4,'core'=2,'z'=8,'yhi'=2] {'yhi'}, dimensions={2} | all-to-all | bytes 1048576 | tf_op jit(solution)/shard_map/all_to_all | solution.py:24
  101.1 74.3 %reduce-scatter.5.cloned.1.call-done = bf16[16,4096]{1,0:T(8,128)(2,1)} async-done(((bf16[512,4096]{1,0:T(8,128)(2,1)}), bf16[16,4096]{1,0:T(8,128)(2,1)}) %reduce-scatter.5.cloned.1.call-update) | async-done | bytes 131088 | tf_op jit(solution)/shard_map/reduce_scatter | solution.py:44
  178.8 12.1 %gather_fusion = bf16[4096,64]{1,0:T(8,128)(2,1)S(1)} fusion(bf16[4096,64]{1,0:T(8,128)(2,1)S(1)} %copy.57, s32[4096]{0:T(1024)S(1)} %fusion.42), kind=kCustom, calls=%fused_computation | custom fusion | bytes 1064960 | tf_op jit(solution)/shard_map/gather | solution.py:29
  192.0 6.7 %all-to-all-start.1 = ((bf16[8,512,64]{1,2,0:T(8,128)(2,1)}), bf16[8,512,64]{1,2,0:T(8,128)(2,1)S(1)}, u32[]{:S(2)}, u32[]{:S(2)}) async-start(bf16[8,512,64]{1,2,0:T(8,128)(2,1)} %copy.58), calls=%async_computation.2 | async-start | bytes 1048576 | tf_op jit(solution)/shard_map/all_to_all | solution.py:30
  198.8 4.6 all-gather.2
  203.4 10.2 %all-to-all-done.1 = bf16[8,512,64]{1,2,0:T(8,128)(2,1)S(1)} async-done(((bf16[8,512,64]{1,2,0:T(8,128)(2,1)}), bf16[8,512,64]{1,2,0:T(8,128)(2,1)S(1)}, u32[]{:S(2)}, u32[]{:S(2)}) %all-to-all-start.1) | async-done | bytes 524320 | tf_op jit(solution)/shard_map/all_to_all | solution.py:30
  214.1 17.0 %all-gather.10.cloned.1.call-done = bf16[512,4096]{1,0:T(8,128)(2,1)} async-done(((bf16[16,4096]{1,0:T(8,128)(2,1)}), bf16[512,4096]{1,0:T(8,128)(2,1)}) %all-gather.10.cloned.1.call-update) | async-done | bytes 4194320 | tf_op jit(solution)/shard_map/all_gather | solution.py:50
  231.1 5.8 %fusion.60 = (f32[512]{0:T(512)S(1)}, f32[512,512]{0,1:T(8,128)S(1)}) fusion(bf16[512,4096]{1,0:T(8,128)(2,1)} %all-gather.10.cloned.1.call-done, bf16[4096,512]{0,1:T(8,128)(2,1)} %all-gather.12.cloned.1.call-done), kind=kOutput, calls=%fused_computation.89 | convolution fusion | flops 2147745280 | bytes 9439232 | tf_op jit(solution)/shard_map/dot_general | solution.py:52
  237.1 24.6 %all-gather.1 = f32[32,4,512]{2,1,0:T(4,128)S(1)} all-gather(f32[1,4,512]{2,1,0:T(4,128)S(1)} %maximum_bitcast_fusion), channel_id=2, replica_groups=mesh['ylo'=2,'x'=4,'core'=2,'z'=8,'yhi'=2] {'yhi','ylo','x','core'}, dimensions={0}, use_global_device_ids=true | all-gather | bytes 270336 | tf_op jit(solution)/shard_map/all_gather | solution.py:59
  262.6 4.3 convolution_convert_fusion.1
  267.0 86.1 %reduce-scatter.9.cloned.1.call-done = bf16[16,4096]{1,0:T(8,128)(2,1)} async-done(((bf16[512,4096]{1,0:T(8,128)(2,1)}), bf16[16,4096]{1,0:T(8,128)(2,1)}) %reduce-scatter.9.cloned.1.call-update) | async-done | bytes 131088 | tf_op jit(solution)/shard_map/reduce_scatter | solution.py:72
  356.1 6.6 %convolution_convert_fusion.2 = bf16[4096,512]{1,0:T(8,128)(2,1)} fusion(bf16[512,4096]{1,0:T(8,128)(2,1)} %all-gather.10.cloned.1.call-done, bf16[512,512]{0,1:T(8,128)(2,1)S(1)} %fusion.23), kind=kOutput, calls=%fused_computation.8 | convolution fusion | flops 2149580800 | bytes 8912896 | tf_op jit(solution)/shard_map/dot_general | solution.py:77
  362.9 45.9 %all-gather.14.cloned.1.call-done = bf16[512,4096]{1,0:T(8,128)(2,1)} async-done(((bf16[16,4096]{1,0:T(8,128)(2,1)}), bf16[512,4096]{1,0:T(8,128)(2,1)}) %all-gather.14.cloned.1.call-update) | async-done | bytes 4194320 | tf_op jit(solution)/shard_map/all_gather | solution.py:75
  408.8 3.3 convolution_convert_fusion.3
  412.1 7.9 %convolution_convert_fusion.4 = bf16[4096,224]{0,1:T(8,128)(2,1)} fusion(bf16[512,4096]{1,0:T(8,128)(2,1)} %all-gather.8.cloned.1.call-done, f32[4096]{0:T(1024)S(1)} %copy-done.9, f32[512]{0:T(512)S(1)} %add_rsqrt_fusion, bf16[512,4096]{1,0:T(8,128)(2,1)} %all-gather.14.cloned.1.call-done, bf16[448,4096]{1,0:T(8,128)(2,1)} %param.16, s32[]{:T(128)S(6)} %select_n.31, ...), kind=kOutput, calls=%fused_computation.10 | convolution fusion | flops 1889386496 | bytes 12535812 | tf_op jit(solution)/shard_map/dot_general | solution.py:88
  420.0 3.6 pad_maximum_fusion
  423.7 41.9 %reduce-scatter.7.cloned.1.call-done = bf16[512,512]{1,0:T(8,128)(2,1)} async-done(((bf16[4096,512]{1,0:T(8,128)(2,1)}), bf16[512,512]{1,0:T(8,128)(2,1)}) %reduce-scatter.7.cloned.1.call-update) | async-done | bytes 524304 | tf_op jit(solution)/shard_map/reduce_scatter | solution.py:78
  469.2 4.0 all-to-all-start.2
  473.2 43.9 %reduce-scatter.11.cloned.1.call-done = bf16[512,448]{0,1:T(8,128)(2,1)} async-done(((bf16[4096,448]{0,1:T(8,128)(2,1)}), bf16[512,448]{0,1:T(8,128)(2,1)}) %reduce-scatter.11.cloned.1.call-update) | async-done | bytes 458768 | tf_op jit(solution)/shard_map/reduce_scatter | solution.py:93
  519.1 4.0 all-to-all-start.3
  526.6 5.0 all-to-all-done.3
  (76 shorter events, 26.3 us)
Async XLA Ops:
  8.0 73.1 %copy-start.9 = (f32[4096]{0:T(1024)S(1)}, f32[4096]{0:T(1024)}, u32[]{:S(2)}) copy-start(f32[4096]{0:T(1024)} %param.13) | copy-start | bytes 49156
  8.0 69.8 %all-gather.8.cloned.1.call-start = ((), (), s32[]{:S(2)}) async-start(), calls=%async_computation.8 | async-start | bytes 6291456 | tf_op jit(solution)/shard_map/all_gather | solution.py:32
  8.7 166.6 %reduce-scatter.5.cloned.1.call-start = ((), (), s32[]{:S(2)}) async-start(), calls=%async_computation.9 | async-start | bytes 4325376 | tf_op jit(solution)/shard_map/reduce_scatter | solution.py:44
  77.8 3.4 copy-start
  81.3 3.2 copy-start.3
  84.5 3.4 copy-start.5
  87.8 88.6 %copy-start.6 = (f32[4096]{0:T(1024)S(1)}, f32[4096]{0:T(1024)}, u32[]{:S(2)}) copy-start(f32[4096]{0:T(1024)} %param.14) | copy-start | bytes 49156
  87.9 90.4 %copy-start.4 = (bf16[4096,64]{0,1:T(8,128)(2,1)S(1)}, bf16[4096,64]{0,1:T(8,128)(2,1)}, u32[]{:S(2)}) copy-start(bf16[4096,64]{0,1:T(8,128)(2,1)} %param.12) | copy-start | bytes 1572868
  87.9 90.8 %copy-start.7 = (s32[4096]{0:T(1024)S(1)}, s32[4096]{0:T(1024)}, u32[]{:S(2)}) copy-start(s32[4096]{0:T(1024)} %param.11) | copy-start | bytes 49156
  87.9 126.2 %all-gather.12.cloned.1.call-start = ((), (), s32[]{:S(2)}) async-start(), calls=%async_computation.11 | async-start | bytes 4718592 | tf_op jit(solution)/shard_map/all_gather | solution.py:26
  101.0 130.1 %all-gather.10.cloned.1.call-start = ((), (), s32[]{:S(2)}) async-start(), calls=%async_computation.10 | async-start | bytes 4325376 | tf_op jit(solution)/shard_map/all_gather | solution.py:50
  178.7 20.1 %copy-start.8 = (s32[256]{0:T(256)S(1)}, s32[256]{0:T(256)}, u32[]{:S(2)}) copy-start(s32[256]{0:T(256)} %param.10) | copy-start | bytes 3076
  192.0 21.6 %all-to-all-start.1 = ((bf16[8,512,64]{1,2,0:T(8,128)(2,1)}), bf16[8,512,64]{1,2,0:T(8,128)(2,1)S(1)}, u32[]{:S(2)}, u32[]{:S(2)}) async-start(bf16[8,512,64]{1,2,0:T(8,128)(2,1)} %copy.58), calls=%async_computation.2 | async-start | bytes 1048576 | tf_op jit(solution)/shard_map/all_to_all | solution.py:30
  198.7 154.3 %reduce-scatter.9.cloned.1.call-start = ((), (), s32[]{:S(2)}) async-start(), calls=%async_computation.13 | async-start | bytes 4325376 | tf_op jit(solution)/shard_map/reduce_scatter | solution.py:72
  236.9 25.7 %copy-start.1 = (bf16[4096,512]{0,1:T(8,128)(2,1)S(1)}, bf16[4096,512]{0,1:T(8,128)(2,1)}, u32[]{:S(2)}) copy-start(bf16[4096,512]{0,1:T(8,128)(2,1)} %all-gather.12.cloned.1.call-done) | copy-start | bytes 12582916
  266.9 86.1 %copy-start.2 = (bf16[16,4096]{1,0:T(8,128)(2,1)S(1)}, bf16[16,4096]{1,0:T(8,128)(2,1)}, u32[]{:S(2)}) copy-start(bf16[16,4096]{1,0:T(8,128)(2,1)} %reduce-scatter.5.cloned.1.call-done) | copy-start | bytes 393220
  267.0 141.8 %all-gather.14.cloned.1.call-start = ((), (), s32[]{:S(2)}) async-start(), calls=%async_computation.14 | async-start | bytes 4325376 | tf_op jit(solution)/shard_map/all_gather | solution.py:75
  356.0 109.6 %reduce-scatter.7.cloned.1.call-start = ((), (), s32[]{:S(2)}) async-start(), calls=%async_computation.12 | async-start | bytes 4718592 | tf_op jit(solution)/shard_map/reduce_scatter | solution.py:78
  362.6 154.4 %reduce-scatter.11.cloned.1.call-start = ((), (), s32[]{:S(2)}) async-start(), calls=%async_computation.15 | async-start | bytes 4128768 | tf_op jit(solution)/shard_map/reduce_scatter | solution.py:93
  469.2 49.9 %all-to-all-start.2 = ((bf16[2,2,65536]{2,1,0:T(2,128)(2,1)}), bf16[2,2,65536]{2,1,0:T(2,128)(2,1)S(1)}, u32[]{:S(2)}, u32[]{:S(2)}) async-start(bf16[2,2,65536]{2,1,0:T(2,128)(2,1)} %reshape.157), calls=%async_computation.4 | async-start | bytes 1048576 | tf_op jit(solution)/shard_map/all_to_all | solution.py:79
  519.1 12.5 %all-to-all-start.3 = ((bf16[512,2,224]{2,1,0:T(2,128)(2,1)}), bf16[512,2,224]{2,1,0:T(2,128)(2,1)S(1)}, u32[]{:S(2)}, u32[]{:S(2)}) async-start(bf16[512,2,224]{2,1,0:T(2,128)(2,1)} %copy.65), calls=%async_computation.7 | async-start | bytes 1048576 | tf_op jit(solution)/shard_map/all_to_all | solution.py:94
Sparse Core Ops, SparseCore 0:
  10.6 67.1 all-gather.7
  88.0 87.3 reduce-scatter.4
  267.1 85.9 reduce-scatter.8
Sparse Core Ops, SparseCore 1:
  101.1 54.4 all-gather.11
  178.3 52.7 all-gather.9
  356.1 52.7 all-gather.13
  411.4 54.2 reduce-scatter.6
  468.2 48.9 reduce-scatter.10

commit v2 on v1

v2 whole, which is shorter than its diff:
```python
import functools
import jax
import jax.numpy as jnp
from jax import lax
from jax.experimental import pallas as pl
from jax.experimental.pallas import tpu as pltpu
from jax.sharding import Mesh, PartitionSpec as P

EPS = 1e-05
HARD = 0.5
MESH = pl.DeviceIdType.MESH
LEAD = ("YB", "core", "XA", "YA", "XB")
BLK = 16


def place():
    x, ylo, yhi, core = (lax.axis_index(n) for n in ("x", "ylo", "yhi", "core"))
    y = 2 * yhi + ylo
    odd = lax.rem(x, 2)
    bits = {
        "core": core,
        "XA": lax.rem(lax.div(x + 1, 2), 2),
        "XB": lax.div(x, 2),
        "YA": lax.rem(lax.div(y + 1, 2), 2),
        "YB": yhi,
    }
    to = {
        "core": {"core": 1 - core},
        "XA": {"x": x + 1 - 2 * odd},
        "XB": {"x": lax.rem(x + 3 + 2 * odd, 4)},
        "YA": {"ylo": 1 - ylo},
        "YB": {"ylo": 1 - ylo, "yhi": 1 - yhi},
    }
    return bits, to


def at(names, fixed, cols=None):
    where = tuple(fixed.get(n, slice(None)) for n in names)
    return where + (slice(None), slice(None) if cols is None else pl.ds(*cols))


def corners(names):
    out = [{}]
    for n in names:
        out = [dict(o, **{n: v}) for o in out for v in (0, 1)]
    return out


class Sender:
    def __init__(self, send_sem, recv_sem, to):
        self.send_sem, self.recv_sem, self.to = send_sem, recv_sem, to
        self.n = 0
        self.all = []

    def go(self, src, dst, dim):
        c = pltpu.make_async_remote_copy(
            src_ref=src,
            dst_ref=dst,
            send_sem=self.send_sem.at[self.n],
            recv_sem=self.recv_sem.at[self.n],
            device_id=self.to[dim],
            device_id_type=MESH,
        )
        c.start()
        self.n += 1
        self.all.append(c)
        return c

    def drain(self):
        for c in self.all:
            c.wait_send()


def colours(n, width):
    tiles = width // 128
    edges = [128 * (tiles * k // n) for k in range(n + 1)]
    return [(edges[k], edges[k + 1] - edges[k]) for k in range(n)]


def meet(to):
    barrier = pltpu.get_barrier_semaphore()
    for d in LEAD:
        pl.semaphore_signal(barrier, inc=1, device_id=to[d], device_id_type=MESH)
    pl.semaphore_wait(barrier, len(LEAD))


def reduce_cube(send, bits, names, dims, width, part, total, landed):
    rest = tuple(n for n in names if n != "core")
    n = len(dims)
    cuts = colours(n, width)
    first, second = [], []
    for keep, held in ((1, first), (0, second)):
        for k in range(n):
            d = dims[k]
            bit = 1 - bits[d] if keep else bits[d]
            src = part.at[at(names, {"core": 1 - bits["core"], d: bit}, cuts[k])]
            dst = total.at[at(rest, {d: bit}, cuts[k])]
            held.append(send.go(src, dst, "core"))

    def merge(k, bit):
        d = dims[k]
        for f in corners([m for m in rest if m != d]):
            f = dict(f, **{d: bit})
            w = at(rest, f, cuts[k])
            total[w] = total[w] + part[at(names, dict(f, core=bits["core"]), cuts[k])]

    def start(k, j):
        d = dims[(k + j) % n]
        fixed = {dims[(k + i) % n]: bits[dims[(k + i) % n]] for i in range(j)}
        fixed[d] = 1 - bits[d]
        return send.go(total.at[at(rest, fixed, cuts[k])], landed[k * n + j], d)

    flying = []
    for k in range(n):
        first[k].wait_recv()
        merge(k, 1 - bits[dims[k]])
        flying.append(start(k, 0))
    for k in range(n):
        second[k].wait_recv()
        merge(k, bits[dims[k]])
    for j in range(n):
        for k in range(n):
            flying[k].wait_recv()
            done = [dims[(k + i) % n] for i in range(j + 1)]
            fixed = {m: bits[m] for m in done}
            left = [m for m in rest if m not in done]
            for f in corners(left):
                w = at(rest, dict(f, **fixed), cuts[k])
                total[w] = total[w] + landed[k * n + j][tuple(f[m] for m in left)]
            if j + 1 < n:
                flying[k] = start(k, j + 1)


def gather_cube(send, bits, dims, width, full):
    n = len(dims)
    cuts = colours(n, width)
    arriving = [send.go(full.at[at(LEAD, bits)], full.at[at(LEAD, bits)], "core")]
    for j in range(n):
        flying = []
        for k in range(n):
            d = dims[(k + j) % n]
            done = [dims[(k + i) % n] for i in range(j)]
            piece = full.at[at(LEAD, {m: bits[m] for m in LEAD if m not in done}, cuts[k])]
            flying.append(send.go(piece, piece, d))
        for k in range(n):
            flying[k].wait_recv()
            d = dims[(k + j) % n]
            done = [dims[(k + i) % n] for i in range(j)]
            fixed = {m: bits[m] for m in LEAD if m not in done}
            fixed[d] = 1 - bits[d]
            piece = full.at[at(LEAD, fixed, cuts[k])]
            arriving.append(send.go(piece, piece, "core"))
    for c in arriving:
        c.wait_recv()


ICI3 = ("XA", "YA", "XB")
ICI4 = ("XA", "YA", "XB", "YB")


def landing(dims, width):
    n = len(dims)
    cuts = colours(n, width)
    return [
        pltpu.VMEM((2,) * (n - 1 - j) + (BLK, cuts[k][1]), jnp.bfloat16)
        for k in range(n)
        for j in range(n)
    ]


def forward_kernel(
    width, run, part, feats, gain, final_own, final_pair, resid_out, scale_out,
    total, full, xown, send_sem, recv_sem, local_sem, *landed,
):
    bits, to = place()
    names = LEAD[1:]
    mine = at(names, bits)
    fetch = pltpu.make_async_copy(feats.at[mine], xown, local_sem.at[0])
    fetch.start()
    meet(to)
    send = Sender(send_sem, recv_sem, to)
    reduce_cube(send, bits, names, ICI3, width, part, total, landed)
    fetch.wait()
    hidden = total[at(ICI3, bits)].astype(jnp.float32)
    resid = xown[...].astype(jnp.float32) + hidden
    rscale = lax.rsqrt(jnp.mean(resid * resid, -1, keepdims=True) + EPS)
    resid_out[...] = resid
    scale_out[...] = jnp.broadcast_to(rscale, scale_out.shape)
    full[at(LEAD, bits)] = (resid * rscale * gain[...]).astype(jnp.bfloat16)
    gather_cube(send, bits, ICI4, width, full)
    out = []
    for b in range(width // (2 * run)):
        for s, ref in ((bits["YB"], final_own), (1 - bits["YB"], final_pair)):
            c = pltpu.make_async_copy(
                full.at[at(LEAD, {}, (pl.multiple_of((2 * b + s) * run, run), run))],
                ref.at[at(LEAD, {}, (b * run, run))],
                local_sem.at[1 + len(out)],
            )
            c.start()
            out.append(c)
    for c in out:
        c.wait()
    send.drain()


def backward_kernel(
    width, run, part_own, part_pair, resid, scale, gain, grad_own, grad_half,
    part, total, full, send_sem, recv_sem, local_sem, *landed,
):
    bits, to = place()
    runs = width // (2 * run)
    fetch = []
    for b in range(runs):
        for s, ref in ((bits["YB"], part_own), (1 - bits["YB"], part_pair)):
            c = pltpu.make_async_copy(
                ref.at[at(LEAD, {}, (b * run, run))],
                part.at[at(LEAD, {}, (pl.multiple_of((2 * b + s) * run, run), run))],
                local_sem.at[len(fetch)],
            )
            c.start()
            fetch.append(c)
    meet(to)
    for c in fetch:
        c.wait()
    send = Sender(send_sem, recv_sem, to)
    reduce_cube(send, bits, LEAD, ICI4, width, part, total, landed)
    rest = tuple(n for n in LEAD if n != "core")
    dfinal = total[at(rest, bits)].astype(jnp.float32)
    r = resid[...]
    rscale = scale[...][:, :1]
    scaled = dfinal * gain[...]
    inner = jnp.sum(scaled * r, -1, keepdims=True)
    full[at(LEAD, bits)] = (rscale * scaled - r * (rscale * rscale * rscale / width * inner)).astype(
        jnp.bfloat16
    )
    gather_cube(send, bits, ICI4, width, full)
    out = [
        pltpu.make_async_copy(full.at[at(LEAD, {"YB": bits["YB"]})], grad_own, local_sem.at[2 * runs])
    ]
    for b in range(runs):
        for s, slot in ((bits["YB"], 0), (1 - bits["YB"], 1)):
            col = pl.multiple_of((2 * b + bits["YB"]) * run, run)
            out.append(
                pltpu.make_async_copy(
                    full.at[at(LEAD, {"YB": s}, (col, run))],
                    grad_half.at[at(LEAD, {"YB": slot}, (b * run, run))],
                    local_sem.at[len(out) - 1],
                )
            )
    for c in out:
        c.start()
    for c in out:
        c.wait()
    send.drain()


def stats_kernel(stats, out, near, far, held, send_sem, recv_sem):
    x, ylo, yhi, core = (lax.axis_index(n) for n in ("x", "ylo", "yhi", "core"))
    row = [
        {"x": lax.rem(x + i, 4), "core": lax.rem(core + c, 2)}
        for i in range(4) for c in range(2) if i or c
    ]
    column = [
        {"ylo": lax.rem(ylo + a, 2), "yhi": lax.rem(yhi + b, 2)}
        for a in range(2) for b in range(2) if a or b
    ]
    barrier = pltpu.get_barrier_semaphore()
    for d in row + column:
        pl.semaphore_signal(barrier, inc=1, device_id=d, device_id_type=MESH)
    pl.semaphore_wait(barrier, len(row) + len(column))

    def exchange(src, slots, peers, base):
        flying = []
        for i, d in enumerate(peers):
            c = pltpu.make_async_remote_copy(
                src_ref=src,
                dst_ref=slots.at[i],
                send_sem=send_sem.at[base + i],
                recv_sem=recv_sem.at[base + i],
                device_id=d,
                device_id_type=MESH,
            )
            c.start()
            flying.append(c)
        for c in flying:
            c.wait_recv()
        parts = [src[...]] + [slots[i] for i in range(len(peers))]
        tops = [p[0:2] for p in parts]
        top = functools.reduce(jnp.maximum, tops)
        total = functools.reduce(
            jnp.add, [p[2:4] * jnp.exp(t - top) for p, t in zip(parts, tops)]
        )
        return flying, top, total

    one, top, total = exchange(stats, near, row, 0)
    held[0:2] = top
    held[2:4] = total
    held[4:8] = jnp.zeros((4, held.shape[1]), jnp.float32)
    two, top, total = exchange(held, far, column, len(row))
    out[0:2] = top
    out[2:4] = total
    out[4:8] = jnp.zeros((4, out.shape[1]), jnp.float32)
    for c in one + two:
        c.wait_send()


VM = pl.BlockSpec(memory_space=pltpu.VMEM)
ANY = pl.BlockSpec(memory_space=pl.ANY)
CUBE = (2,) * 5


def params(cid):
    return pltpu.CompilerParams(
        collective_id=cid, has_side_effects=True, vmem_limit_bytes=40 * 1024 * 1024
    )


def call_forward(part, feats, gain, run):
    width = part.shape[1]
    sd = jax.ShapeDtypeStruct
    bf16, f32 = jnp.bfloat16, jnp.float32
    n_sem = 6 + 9 + 1 + 32
    own, pair, resid, scale = pl.pallas_call(
        functools.partial(forward_kernel, width, run),
        out_shape=(
            sd(CUBE + (BLK, width // 2), bf16),
            sd(CUBE + (BLK, width // 2), bf16),
            sd((BLK, width), f32),
            sd((BLK, 128), f32),
        ),
        in_specs=[VM, ANY, VM],
        out_specs=(ANY, ANY, VM, VM),
        scratch_shapes=[
            pltpu.VMEM((2,) * 3 + (BLK, width), bf16),
            pltpu.VMEM(CUBE + (BLK, width), bf16),
            pltpu.VMEM((BLK, width), bf16),
            pltpu.SemaphoreType.DMA((n_sem,)),
            pltpu.SemaphoreType.DMA((n_sem,)),
            pltpu.SemaphoreType.DMA((1 + width // run,)),
        ]
        + landing(ICI3, width),
        compiler_params=params(1),
        cost_estimate=pl.CostEstimate(flops=10**6, bytes_accessed=10**8, transcendentals=0),
        name="forward_plane",
    )(part.reshape(CUBE[1:] + (BLK, width)), feats.reshape(CUBE[1:] + (BLK, width)), gain[None])
    return own.reshape(-1, width // 2), pair.reshape(-1, width // 2), resid, scale


def call_backward(part_own, part_pair, resid, scale, gain, run):
    width = resid.shape[1]
    sd = jax.ShapeDtypeStruct
    bf16 = jnp.bfloat16
    n_sem = 8 + 16 + 1 + 32
    half = CUBE + (BLK, width // 2)
    own, halves = pl.pallas_call(
        functools.partial(backward_kernel, width, run),
        out_shape=(sd(CUBE[1:] + (BLK, width), bf16), sd(half, bf16)),
        in_specs=[ANY, ANY, VM, VM, VM],
        out_specs=(ANY, ANY),
        scratch_shapes=[
            pltpu.VMEM(CUBE + (BLK, width), bf16),
            pltpu.VMEM((2,) * 4 + (BLK, width), bf16),
            pltpu.VMEM(CUBE + (BLK, width), bf16),
            pltpu.SemaphoreType.DMA((n_sem,)),
            pltpu.SemaphoreType.DMA((n_sem,)),
            pltpu.SemaphoreType.DMA((1 + width // run,)),
        ]
        + landing(ICI4, width),
        compiler_params=params(3),
        cost_estimate=pl.CostEstimate(flops=10**6, bytes_accessed=10**8, transcendentals=0),
        name="backward_plane",
    )(part_own.reshape(half), part_pair.reshape(half), resid, scale, gain[None])
    return own.reshape(-1, width), halves.reshape(-1, width // 2)


def call_stats(stats):
    f32 = jnp.float32
    n = stats.shape[1]
    return pl.pallas_call(
        stats_kernel,
        out_shape=jax.ShapeDtypeStruct((8, n), f32),
        in_specs=[VM],
        out_specs=VM,
        scratch_shapes=[
            pltpu.VMEM((7, 8, n), f32),
            pltpu.VMEM((3, 8, n), f32),
            pltpu.VMEM((8, n), f32),
            pltpu.SemaphoreType.DMA((10,)),
            pltpu.SemaphoreType.DMA((10,)),
        ],
        compiler_params=params(2),
        name="softmax_stats",
    )(stats)


def body(
    features, token_ids, positions, target_buffer, norm_gain, final_gain, w_in, w_out, head_weight
):
    yhi = lax.axis_index("yhi")
    vocab = lax.axis_index(("ylo", "x", "core"))
    f32 = jnp.float32
    bf16 = jnp.bfloat16
    backward = (((1,), (1,)), ((), ()))
    contract = (((0,), (0,)), ((), ()))
    swap = functools.partial(lax.ppermute, axis_name="yhi", perm=[(0, 1), (1, 0)])
    gather = functools.partial(lax.all_gather, axis_name="z", axis=0, tiled=True)
    scatter = functools.partial(lax.psum_scatter, axis_name="z", scatter_dimension=0, tiled=True)

    def pick(array, axis, index):
        return lax.dynamic_index_in_dim(array, index, axis, keepdims=False)

    rows, cols = head_weight.shape
    hw = head_weight.reshape(rows, 8, 2, cols // 16)
    head_pair = swap(pick(hw, 2, 1 - yhi).reshape(rows, cols // 2))
    head_own = gather(pick(hw, 2, yhi).reshape(rows, cols // 2))
    head_pair = gather(head_pair)

    tok, width = features.shape
    xfloat = features.astype(f32)
    rinput = lax.rsqrt(jnp.mean(xfloat * xfloat, -1, keepdims=True) + EPS)
    normed = (xfloat * rinput * norm_gain).astype(bf16)
    pre = jnp.dot(normed, w_in, preferred_element_type=f32)
    act = jax.nn.silu(pre).astype(bf16)
    part = jnp.dot(act, w_out, preferred_element_type=f32).astype(bf16)
    final_own, final_pair, resid, scale = call_forward(part, features, final_gain, rows)

    split = normed.reshape(tok, 8, 2, rows)
    normed_own = pick(split, 2, yhi).reshape(tok, width // 2)
    normed_pair = swap(pick(split, 2, 1 - yhi).reshape(tok, width // 2))
    normed2 = jnp.concatenate([normed_own, normed_pair], 0)
    act2 = jnp.concatenate([act, swap(act)], 0)

    tw = target_buffer.shape[1]
    ordered = target_buffer[positions].reshape(8, -1, tw)
    target = lax.all_to_all(ordered, "z", split_axis=0, concat_axis=2, tiled=True)[0]
    toks = lax.all_gather(token_ids, "yhi", axis=0, tiled=True)

    logits = jnp.dot(final_own, head_own, preferred_element_type=f32) + jnp.dot(
        final_pair, head_pair, preferred_element_type=f32
    )
    tfloat = target.astype(f32)
    top_q = jnp.max(logits, -1)
    top_p = jnp.max(tfloat, -1)
    qexp = jnp.exp(logits - top_q[:, None])
    pexp = jnp.exp(tfloat - top_p[:, None])
    zero = jnp.zeros_like(top_q)
    stats = jnp.stack([top_q, top_p, jnp.sum(qexp, -1), jnp.sum(pexp, -1), zero, zero, zero, zero])
    every = call_stats(stats)
    qprob = qexp * (jnp.exp(top_q - every[0]) / every[2])[:, None]
    pprob = pexp * (jnp.exp(top_p - every[1]) / every[3])[:, None]
    lane = jnp.arange(cols // 2, dtype=jnp.int32)
    columns_here = vocab * cols + (lane // tw) * (2 * tw) + yhi * tw + lane % tw
    onehot = (columns_here[None, :] == toks[:, None]).astype(f32)
    dlogits = (qprob - pprob + HARD * (qprob - onehot)).astype(bf16)

    gh_pair = lax.dot_general(final_pair, dlogits, contract, preferred_element_type=f32).astype(bf16)
    gh_pair = scatter(gh_pair)
    gh_own = lax.dot_general(final_own, dlogits, contract, preferred_element_type=f32).astype(bf16)
    gh_own = scatter(gh_own)
    gh_other = swap(gh_pair)
    both = jnp.stack([gh_own, gh_other]).reshape(2, rows, 8, tw)
    both = jnp.where(yhi == 0, both, both[::-1])
    grad_head = both.transpose(1, 2, 0, 3).reshape(rows, cols).astype(f32)

    part_own = lax.dot_general(dlogits, head_own, backward, preferred_element_type=f32).astype(bf16)
    part_pair = lax.dot_general(dlogits, head_pair, backward, preferred_element_type=f32).astype(bf16)
    dresid, dresid2 = call_backward(part_own, part_pair, resid, scale, final_gain, rows)

    go = lax.dot_general(dresid2, act2, contract, preferred_element_type=f32).astype(bf16)
    go = scatter(go).astype(f32)
    dact = lax.dot_general(dresid, w_out, backward, preferred_element_type=f32)
    sig = jax.nn.sigmoid(pre)
    dpre = (dact * sig * (1.0 + pre * (1.0 - sig))).astype(bf16)
    dpre2 = jnp.concatenate([dpre, swap(dpre)], 0)
    gi = lax.dot_general(normed2, dpre2, contract, preferred_element_type=f32).astype(bf16)
    gi = scatter(gi).astype(f32)
    return (grad_head, gi, go.T)


def solution(mesh):
    names = ("ylo", "x", "core", "z", "yhi")
    fine = Mesh(mesh.devices.reshape(2, 4, 2, 8, 2), names)
    v = ("ylo", "x", "core")
    d = ("z", "yhi")
    return jax.shard_map(
        body,
        mesh=fine,
        in_specs=(
            P(d, None),
            P(d),
            P(),
            P(None, v + d),
            P(),
            P(),
            P(None, v),
            P(v, None),
            P(d, v),
        ),
        out_specs=(P(d, v), P(d, v), P(v, d)),
        check_vma=False,
    )
```

time: 542 us -> 331 us (0.61)
  waiting for transfers between devices: 394 us -> 110 us
  Pallas kernels: 0 us -> 106 us
  blocking collectives: 40.5 us -> 5.02 us
  local copies, waits for them, and re-layouts: 26.2 us -> 35.4 us
  matrix products: 34.4 us -> 26.5 us
    reduce_scatter x4, waiting for transfers between devices: 246 us -> 76.1 us  [the longest x1 41.2 us: body(): gh_own = scatter(gh_own)]
    all_gather x4 -> x2, waiting for transfers between devices: 132 us -> 1.35 us  [the longest x1 1.34 us: body(): head_pair = gather(head_pair)]
    pallas_call x0 -> x3, Pallas kernels: none -> 106 us  [the longest x1 48.4 us: call_backward(): pl.pallas_call(functools.partial(backward_kernel, width, run), out_shape=...]
    ppermute x0 -> x5, waiting for transfers between devices: none -> 32.3 us  [the longest x1 22.4 us: body(): normed_pair = swap(pick(split, 2, 1 - yhi).reshape(tok, width // 2))]
    all_gather x1 -> x0, blocking collectives: 24.6 us -> none  [body(): every = lax.all_gather(stats, PLANE, axis=0)]
    all_to_all x1 -> x0, blocking collectives: 11.3 us -> none  [body(): hw = lax.all_to_all(hw, 'yhi', split_axis=2, concat_axis=0, tiled=True)]
    ppermute x0 -> x5, starting transfers between devices: none -> 10.5 us  [the longest x1 3.83 us: body(): head_pair = swap(pick(hw, 2, 1 - yhi).reshape(rows, cols // 2))]
    all_to_all x1, waiting for transfers between devices: 10.2 us -> 0.01 us  [body(): lax.all_to_all(ordered, 'z', split_axis=0, concat_axis=2, tiled=True)[0]]
  transfers between devices with their start and end apart: 11 -> 12, of which waited for: 9 -> 6; matrix products, arithmetic and copies ran while one was open for 9% -> 16% of each run, Pallas kernels for 0% -> 28%
where the time goes in v2:
time: 331 us; the launch traced here: 327 us
  waiting for transfers between devices  110 us (33%)
  Pallas kernels  106 us (32%)
  local copies, waits for them, and re-layouts  35.4 us (11%)
  matrix products  26.5 us (8%)
  starting transfers between devices  19.7 us (6%)
  between operations  14.5 us (4%)
  other arithmetic  10.1 us (3%)
  blocking collectives  5.02 us (2%)
    pallas_call x1, Pallas kernels, call_backward(): pl.pallas_call(functools.partial(backward_kernel, width, run), out_shape=...  48.4 us
    pallas_call x1, Pallas kernels, call_forward(): pl.pallas_call(functools.partial(forward_kernel, width, run), out_shape=(...  42.8 us
    reduce_scatter x1, waiting for transfers between devices, body(): gh_own = scatter(gh_own)  41.2 us
    reduce_scatter x1, waiting for transfers between devices, body(): gi = scatter(gi).astype(f32)  34.9 us
    ppermute x1, waiting for transfers between devices, body(): normed_pair = swap(pick(split, 2, 1 - yhi).reshape(tok, width // 2))  22.4 us
    gather x1, local copies, waits for them, and re-layouts, body(): ordered = target_buffer[positions].reshape(8, -1, tw)  15 us
    pallas_call x1, Pallas kernels, call_stats(): pl.pallas_call(stats_kernel, out_shape=jax.ShapeDtypeStruct((8, n), f32),...  14.7 us
    unnamed x54, local copies, waits for them, and re-layouts  13.9 us
  transfers between devices with their start and end apart: 12, of which 6 were waited for; matrix products, arithmetic and copies ran while one was open for 16% of the time, Pallas kernels for 28%

profile of v2, /device:TPU:1, one launch (start us, length us, event | category | flops | bytes accessed | tf_op | source)
XLA Modules:
  0.0 327.0 jit_solution(2458669070515123714)
XLA Ops:
  9.4 3.8 %collective-permute-start = (bf16[256,512]{0,1:T(8,128)(2,1)S(1)}, bf16[256,512]{0,1:T(8,128)(2,1)S(1)}, u32[]{:S(2)}, u32[]{:S(2)}) collective-permute-start(bf16[256,512]{0,1:T(8,128)(2,1)S(1)} %bitcast.92), channel_id=1, source_target_pairs={{0,1},{1,0},{2,3},{3,2},{4,5},{5,4},{6,7},{7,6},{8,9},{9,8},{10,11... | collective-permute-start | bytes 786440 | tf_op jit(solution)/shard_map/ppermute | solution.py:414
  13.2 5.0 %collective-permute-done = bf16[256,512]{0,1:T(8,128)(2,1)S(1)} collective-permute-done((bf16[256,512]{0,1:T(8,128)(2,1)S(1)}, bf16[256,512]{0,1:T(8,128)(2,1)S(1)}, u32[]{:S(2)}, u32[]{:S(2)}) %collective-permute-start) | collective-permute-done | bytes 262176 | tf_op jit(solution)/shard_map/ppermute | solution.py:414
  19.4 15.0 %gather_fusion = bf16[4096,64]{1,0:T(8,128)(2,1)} fusion(bf16[4096,64]{1,0:T(8,128)(2,1)S(1)} %copy.32, s32[4096]{0:T(1024)S(1)} %fusion.20), kind=kCustom, calls=%fused_computation | custom fusion | bytes 1064960 | tf_op jit(solution)/shard_map/gather | solution.py:434
  34.4 2.5 copy.33
  36.9 9.0 %all-to-all-start = ((bf16[8,512,64]{1,2,0:T(8,128)(2,1)}), bf16[8,512,64]{1,2,0:T(8,128)(2,1)S(1)}, u32[]{:S(2)}, u32[]{:S(2)}) async-start(bf16[8,512,64]{1,2,0:T(8,128)(2,1)} %copy.33), calls=%async_computation | async-start | bytes 1048576 | tf_op jit(solution)/shard_map/all_to_all | solution.py:435
  46.0 2.5 copy.30
  48.5 2.4 fusion
  52.9 1.9 multiply_convert_fusion
  57.3 42.8 %forward_plane.1 = (bf16[2,2,2,2,2,16,2048]{6,5,4,3,2,1,0:T(8,128)(2,1)S(1)}, bf16[2,2,2,2,2,16,2048]{6,5,4,3,2,1,0:T(8,128)(2,1)S(1)}, f32[16,4096]{1,0:T(8,128)S(1)}, f32[16,128]{1,0:T(8,128)S(1)}) custom-call(bf16[2,2,2,2,16,4096]{5,4,3,2,1,0:T(8,128)(2,1)S(1)} %bitcast.71, bf16[2,2,2,2,16,4096]{5,4,3,2,1,0:T(8,128)(2,1)S(1)} %bitcast.72, ...), custom_call_target="tpu_custom_call" | custom-call | flops 1000000 | bytes 100000000 | tf_op jit(solution)/shard_map/forward_plane/pallas_call | solution.py:323
  102.9 5.0 %all-gather = s32[2,1,256]{2,1,0:T(1,128)S(1)} all-gather(s32[1,1,256]{2,1,0:T(1,128)S(1)} %bitcast.102), channel_id=1, replica_groups=mesh['ylo'=2,'x'=4,'core'=2,'z'=8,'yhi'=2] {'yhi'}, dimensions={0}, use_global_device_ids=true | all-gather | bytes 3072 | tf_op jit(solution)/shard_map/all_gather | solution.py:436
  109.3 3.9 %fusion.37 = f32[512,512]{0,1:T(8,128)} fusion(bf16[512,2048]{1,0:T(8,128)(2,1)S(1)} %bitcast.77, bf16[2048,512]{0,1:T(8,128)(2,1)} %all-gather.4.cloned.1.call-done), kind=kOutput, calls=%fused_computation.71 | convolution fusion | flops 1073741824 | bytes 5242880 | tf_op jit(solution)/shard_map/dot_general | solution.py:438
  114.5 3.9 %fusion.36 = (f32[512]{0:T(512)S(1)}, f32[512,512]{0,1:T(8,128)S(1)}) fusion(f32[512,512]{0,1:T(8,128)} %fusion.37, bf16[512,2048]{1,0:T(8,128)(2,1)} %bitcast.79, bf16[2048,512]{0,1:T(8,128)(2,1)} %all-gather.6.cloned.1.call-done), kind=kOutput, calls=%fused_computation.70 | convolution fusion | flops 1074265600 | bytes 6293504 | tf_op jit(solution)/shard_map/dot_general | solution.py:438
  119.4 14.7 %softmax_stats.1 = f32[8,512]{1,0:T(8,128)S(1)} custom-call(f32[8,512]{1,0:T(8,128)S(1)} %stack.29.stats), custom_call_target="tpu_custom_call" | custom-call | tf_op jit(solution)/shard_map/softmax_stats/pallas_call | solution.py:379
  136.8 2.7 convolution_convert_fusion.3
  140.4 1.9 collective-permute-start.4
  142.4 2.9 convolution_convert_fusion.2
  146.5 48.4 %backward_plane.1 = (bf16[2,2,2,2,16,4096]{5,4,3,2,1,0:T(8,128)(2,1)S(1)}, bf16[2,2,2,2,2,16,2048]{6,5,4,3,2,1,0:T(8,128)(2,1)S(1)}) custom-call(bf16[2,2,2,2,2,16,2048]{6,5,4,3,2,1,0:T(8,128)(2,1)S(1)} %bitcast.73, bf16[2,2,2,2,2,16,2048]{6,5,4,3,2,1,0:T(8,128)(2,1)S(1)} %bitcast.74, f32[16,4096]{1,0:T(8,128)S(1)} %get-tuple-element.11.resid, ...), custom_call_target="tpu_custom_call" | custom-call | flops 1000000 | bytes 100000000 | tf_op jit(solution)/shard_map/backward_plane/pallas_call | solution.py:355
  195.0 2.4 convolution_convert_fusion.5
  203.9 22.4 %collective-permute-done.2 = bf16[256,2048]{0,1:T(8,128)(2,1)S(1)} collective-permute-done((bf16[256,2048]{0,1:T(8,128)(2,1)S(1)}, bf16[256,2048]{0,1:T(8,128)(2,1)S(1)}, u32[]{:S(2)}, u32[]{:S(2)}) %collective-permute-start.2) | collective-permute-done | bytes 1048608 | tf_op jit(solution)/shard_map/ppermute | solution.py:429
  226.3 4.9 %collective-permute-done.3 = bf16[256,448]{0,1:T(8,128)(2,1)S(1)} collective-permute-done((bf16[256,448]{0,1:T(8,128)(2,1)S(1)}, bf16[256,448]{0,1:T(8,128)(2,1)S(1)}, u32[]{:S(2)}, u32[]{:S(2)}) %collective-permute-start.3) | collective-permute-done | bytes 229408 | tf_op jit(solution)/shard_map/ppermute | solution.py:474
  231.2 2.4 convolution_convert_fusion.6
  233.7 2.7 convolution_convert_fusion.4
  239.5 34.9 %reduce-scatter.9.cloned.1.call-done = bf16[256,448]{0,1:T(8,128)(2,1)} async-done(((bf16[2048,448]{0,1:T(8,128)(2,1)}), bf16[256,448]{0,1:T(8,128)(2,1)}) %reduce-scatter.9.cloned.1.call-update) | async-done | bytes 229392 | tf_op jit(solution)/shard_map/reduce_scatter | solution.py:476
  276.1 41.2 %reduce-scatter.5.cloned.1.call-done = bf16[256,512]{1,0:T(8,128)(2,1)} async-done(((bf16[2048,512]{1,0:T(8,128)(2,1)}), bf16[256,512]{1,0:T(8,128)(2,1)}) %reduce-scatter.5.cloned.1.call-update) | async-done | bytes 262160 | tf_op jit(solution)/shard_map/reduce_scatter | solution.py:459
  (100 shorter events, 33.3 us)
Async XLA Ops:
  7.2 11.7 %copy-start.13 = (bf16[4096,64]{0,1:T(8,128)(2,1)S(1)}, bf16[4096,64]{0,1:T(8,128)(2,1)}, u32[]{:S(2)}) copy-start(bf16[4096,64]{0,1:T(8,128)(2,1)} %param.12) | copy-start | bytes 1572868
  7.2 102.1 %all-gather.4.cloned.1.call-start = ((), (), s32[]{:S(2)}) async-start(), calls=%async_computation.5 | async-start | bytes 2359296 | tf_op jit(solution)/shard_map/all_gather | solution.py:415
  7.2 12.2 %copy-start.20 = (s32[4096]{0:T(1024)S(1)}, s32[4096]{0:T(1024)}, u32[]{:S(2)}) copy-start(s32[4096]{0:T(1024)} %param.11) | copy-start | bytes 49156
  9.3 105.2 %all-gather.6.cloned.1.call-start = ((), (), s32[]{:S(2)}) async-start(), calls=%async_computation.6 | async-start | bytes 2359296 | tf_op jit(solution)/shard_map/all_gather | solution.py:416
  9.4 8.8 %collective-permute-start = (bf16[256,512]{0,1:T(8,128)(2,1)S(1)}, bf16[256,512]{0,1:T(8,128)(2,1)S(1)}, u32[]{:S(2)}, u32[]{:S(2)}) collective-permute-start(bf16[256,512]{0,1:T(8,128)(2,1)S(1)} %bitcast.92), channel_id=1, source_target_pairs={{0,1},{1,0},{2,3},{3,2},{4,5},{5,4},{6,7},{7,6},{8,9},{9,8},{10,11... | collective-permute-start | bytes 786440 | tf_op jit(solution)/shard_map/ppermute | solution.py:414
  34.4 11.5 %copy-start = (bf16[256,4096]{1,0:T(8,128)(2,1)S(1)}, bf16[256,4096]{1,0:T(8,128)(2,1)}, u32[]{:S(2)}) copy-start(bf16[256,4096]{1,0:T(8,128)(2,1)} %param.9) | copy-start | bytes 6291460
  36.9 71.0 %all-to-all-start = ((bf16[8,512,64]{1,2,0:T(8,128)(2,1)}), bf16[8,512,64]{1,2,0:T(8,128)(2,1)S(1)}, u32[]{:S(2)}, u32[]{:S(2)}) async-start(bf16[8,512,64]{1,2,0:T(8,128)(2,1)} %copy.33), calls=%async_computation | async-start | bytes 1048576 | tf_op jit(solution)/shard_map/all_to_all | solution.py:435
  45.9 190.5 %reduce-scatter.7.cloned.1.call-start = ((), (), s32[]{:S(2)}) async-start(), calls=%async_computation.8 | async-start | bytes 2359296 | tf_op jit(solution)/shard_map/reduce_scatter | solution.py:457
  52.9 3.0 copy-start.11
  57.3 45.6 %copy-start.21 = (s32[256]{0:T(256)S(1)}, s32[256]{0:T(256)}, u32[]{:S(2)}) copy-start(s32[256]{0:T(256)} %param.10) | copy-start | bytes 3076
  102.9 6.4 %copy-start.3 = (bf16[2,2,2,2,2,16,2048]{6,5,4,3,2,1,0:T(8,128)(2,1)S(1)}, bf16[2,2,2,2,2,16,2048]{6,5,4,3,2,1,0:T(8,128)(2,1)}, u32[]{:S(2)}) copy-start(bf16[2,2,2,2,2,16,2048]{6,5,4,3,2,1,0:T(8,128)(2,1)} %copy-done.2) | copy-start | bytes 6291460
  114.5 19.6 %copy-start.9 = (f32[8,1,512,64]{2,3,0,1:T(8,128)S(1)}, f32[8,1,512,64]{2,3,0,1:T(8,128)}, u32[]{:S(2)}) copy-start(f32[8,1,512,64]{2,3,0,1:T(8,128)} %get-tuple-element.27) | copy-start | bytes 3145732
  118.4 18.4 %copy-start.6 = (bf16[2,2,2,2,2,16,2048]{6,5,4,3,2,1,0:T(8,128)(2,1)S(1)}, bf16[2,2,2,2,2,16,2048]{6,5,4,3,2,1,0:T(8,128)(2,1)}, u32[]{:S(2)}) copy-start(bf16[2,2,2,2,2,16,2048]{6,5,4,3,2,1,0:T(8,128)(2,1)} %copy-done.5) | copy-start | bytes 6291460
  139.5 2.9 copy-start.15
  139.5 5.7 %copy-start.23 = (bf16[2048,512]{0,1:T(8,128)(2,1)S(1)}, bf16[2048,512]{0,1:T(8,128)(2,1)}, u32[]{:S(2)}) copy-start(bf16[2048,512]{0,1:T(8,128)(2,1)} %all-gather.6.cloned.1.call-done) | copy-start | bytes 6291460
  139.5 98.2 %reduce-scatter.11.cloned.1.call-start = ((), (), s32[]{:S(2)}) async-start(), calls=%async_computation.10 | async-start | bytes 2064384 | tf_op jit(solution)/shard_map/reduce_scatter | solution.py:470
  140.4 54.6 %collective-permute-start.4 = (bf16[256,448]{0,1:T(8,128)(2,1)S(1)}, bf16[256,448]{0,1:T(8,128)(2,1)S(1)}, u32[]{:S(2)}, u32[]{:S(2)}) collective-permute-start(bf16[256,448]{0,1:T(8,128)(2,1)S(1)} %copy-done.18), channel_id=1, source_target_pairs={{0,1},{1,0},{2,3},{3,2},{4,5},{5,4},{6,7},{7,6},{8,9},{9,8},{10,11... | collective-permute-start | bytes 688136 | tf_op jit(solution)/shard_map/ppermute | solution.py:431
  197.4 77.0 %reduce-scatter.9.cloned.1.call-start = ((), (), s32[]{:S(2)}) async-start(), calls=%async_computation.9 | async-start | bytes 2064384 | tf_op jit(solution)/shard_map/reduce_scatter | solution.py:476
  197.5 3.5 %copy-start.12 = (bf16[448,4096]{1,0:T(8,128)(2,1)S(1)}, bf16[448,4096]{1,0:T(8,128)(2,1)}, u32[]{:S(2)}) copy-start(bf16[448,4096]{1,0:T(8,128)(2,1)} %param.16) | copy-start | bytes 11010052
  197.5 3.5 %copy-start.24 = (f32[256,448]{0,1:T(8,128)S(1)}, f32[256,448]{0,1:T(8,128)}, u32[]{:S(2)}) copy-start(f32[256,448]{0,1:T(8,128)} %get-tuple-element.35) | copy-start | bytes 1376260
  199.3 27.0 %collective-permute-start.2 = (bf16[256,2048]{0,1:T(8,128)(2,1)S(1)}, bf16[256,2048]{0,1:T(8,128)(2,1)S(1)}, u32[]{:S(2)}, u32[]{:S(2)}) collective-permute-start(bf16[256,2048]{0,1:T(8,128)(2,1)S(1)} %bitcast.88), channel_id=1, source_target_pairs={{0,1},{1,0},{2,3},{3,2},{4,5},{5,4},{6,7},{7,6},{8,9},{9,8},{10,11... | collective-permute-start | bytes 3145736 | tf_op jit(solution)/shard_map/ppermute | solution.py:429
  202.1 29.1 %collective-permute-start.3 = (bf16[256,448]{0,1:T(8,128)(2,1)S(1)}, bf16[256,448]{0,1:T(8,128)(2,1)S(1)}, u32[]{:S(2)}, u32[]{:S(2)}) collective-permute-start(bf16[256,448]{0,1:T(8,128)(2,1)S(1)} %fusion.7), channel_id=1, source_target_pairs={{0,1},{1,0},{2,3},{3,2},{4,5},{5,4},{6,7},{7,6},{8,9},{9,8},{10,11... | collective-permute-start | bytes 688136 | tf_op jit(solution)/shard_map/ppermute | solution.py:474
  233.6 83.7 %reduce-scatter.5.cloned.1.call-start = ((), (), s32[]{:S(2)}) async-start(), calls=%async_computation.7 | async-start | bytes 2359296 | tf_op jit(solution)/shard_map/reduce_scatter | solution.py:459
  236.4 82.0 %collective-permute-start.1 = (bf16[256,512]{1,0:T(8,128)(2,1)}, bf16[256,512]{1,0:T(8,128)(2,1)S(1)}, u32[]{:S(2)}, u32[]{:S(2)}) collective-permute-start(bf16[256,512]{1,0:T(8,128)(2,1)} %reduce-scatter.7.cloned.1.call-done), channel_id=1, source_target_pairs={{0,1},{1,0},{2,3},{3,2},{4,5},{5,4},{6,7},{7,6},{8,9},{9,8},{10,11... | collective-permute-start | bytes 786440 | tf_op jit(solution)/shard_map/ppermute | solution.py:460
  (13 other events, 21.1 us)
Sparse Core Ops, SparseCore 0:
  10.3 55.6 all-gather.3
  67.7 46.7 all-gather.5
  139.6 35.6 reduce-scatter.6
  197.5 34.4 reduce-scatter.10
  234.4 39.9 reduce-scatter.8
  276.8 40.5 reduce-scatter.4

commit v3 on v2

--- a/solution.py
+++ b/solution.py
@@ -169,7 +169,7 @@
 
 
 def forward_kernel(
-    width, run, part, feats, gain, final_own, final_pair, resid_out, scale_out,
+    width, part, feats, gain, final_out, resid_out, scale_out,
     total, full, xown, send_sem, recv_sem, local_sem, *landed,
 ):
     bits, to = place()
@@ -188,40 +188,19 @@
     scale_out[...] = jnp.broadcast_to(rscale, scale_out.shape)
     full[at(LEAD, bits)] = (resid * rscale * gain[...]).astype(jnp.bfloat16)
     gather_cube(send, bits, ICI4, width, full)
-    out = []
-    for b in range(width // (2 * run)):
-        for s, ref in ((bits["YB"], final_own), (1 - bits["YB"], final_pair)):
-            c = pltpu.make_async_copy(
-                full.at[at(LEAD, {}, (pl.multiple_of((2 * b + s) * run, run), run))],
-                ref.at[at(LEAD, {}, (b * run, run))],
-                local_sem.at[1 + len(out)],
-            )
-            c.start()
-            out.append(c)
-    for c in out:
-        c.wait()
+    put = pltpu.make_async_copy(full, final_out, local_sem.at[1])
+    put.start()
+    put.wait()
     send.drain()
 
 
 def backward_kernel(
-    width, run, part_own, part_pair, resid, scale, gain, grad_own, grad_half,
-    part, total, full, send_sem, recv_sem, local_sem, *landed,
+    width, run, part, resid, scale, gain, grad_own, grad_half,
+    total, full, send_sem, recv_sem, local_sem, *landed,
 ):
     bits, to = place()
     runs = width // (2 * run)
-    fetch = []
-    for b in range(runs):
-        for s, ref in ((bits["YB"], part_own), (1 - bits["YB"], part_pair)):
-            c = pltpu.make_async_copy(
-                ref.at[at(LEAD, {}, (b * run, run))],
-                part.at[at(LEAD, {}, (pl.multiple_of((2 * b + s) * run, run), run))],
-                local_sem.at[len(fetch)],
-            )
-            c.start()
-            fetch.append(c)
     meet(to)
-    for c in fetch:
-        c.wait()
     send = Sender(send_sem, recv_sem, to)
     reduce_cube(send, bits, LEAD, ICI4, width, part, total, landed)
     rest = tuple(n for n in LEAD if n != "core")
@@ -315,50 +294,50 @@
     )
 
 
-def call_forward(part, feats, gain, run):
+def call_forward(part, feats, gain):
     width = part.shape[1]
     sd = jax.ShapeDtypeStruct
     bf16, f32 = jnp.bfloat16, jnp.float32
     n_sem = 6 + 9 + 1 + 32
-    own, pair, resid, scale = pl.pallas_call(
-        functools.partial(forward_kernel, width, run),
+    final, resid, scale = pl.pallas_call(
+        functools.partial(forward_kernel, width),
         out_shape=(
-            sd(CUBE + (BLK, width // 2), bf16),
-            sd(CUBE + (BLK, width // 2), bf16),
+            sd(CUBE + (BLK, width), bf16),
             sd((BLK, width), f32),
             sd((BLK, 128), f32),
         ),
         in_specs=[VM, ANY, VM],
-        out_specs=(ANY, ANY, VM, VM),
+        out_specs=(ANY, VM, VM),
         scratch_shapes=[
             pltpu.VMEM((2,) * 3 + (BLK, width), bf16),
             pltpu.VMEM(CUBE + (BLK, width), bf16),
             pltpu.VMEM((BLK, width), bf16),
             pltpu.SemaphoreType.DMA((n_sem,)),
             pltpu.SemaphoreType.DMA((n_sem,)),
-            pltpu.SemaphoreType.DMA((1 + width // run,)),
+            pltpu.SemaphoreType.DMA((2,)),
         ]
         + landing(ICI3, width),
         compiler_params=params(1),
         cost_estimate=pl.CostEstimate(flops=10**6, bytes_accessed=10**8, transcendentals=0),
         name="forward_plane",
     )(part.reshape(CUBE[1:] + (BLK, width)), feats.reshape(CUBE[1:] + (BLK, width)), gain[None])
-    return own.reshape(-1, width // 2), pair.reshape(-1, width // 2), resid, scale
-
-
-def call_backward(part_own, part_pair, resid, scale, gain, run):
+    return final.reshape(-1, width), resid, scale
+
+
+def call_backward(part, resid, scale, gain, run):
     width = resid.shape[1]
     sd = jax.ShapeDtypeStruct
     bf16 = jnp.bfloat16
     n_sem = 8 + 16 + 1 + 32
-    half = CUBE + (BLK, width // 2)
     own, halves = pl.pallas_call(
         functools.partial(backward_kernel, width, run),
-        out_shape=(sd(CUBE[1:] + (BLK, width), bf16), sd(half, bf16)),
-        in_specs=[ANY, ANY, VM, VM, VM],
+        out_shape=(
+            sd(CUBE[1:] + (BLK, width), bf16),
+            sd(CUBE + (BLK, width // 2), bf16),
+        ),
+        in_specs=[VM, VM, VM, VM],
         out_specs=(ANY, ANY),
         scratch_shapes=[
-            pltpu.VMEM(CUBE + (BLK, width), bf16),
             pltpu.VMEM((2,) * 4 + (BLK, width), bf16),
             pltpu.VMEM(CUBE + (BLK, width), bf16),
             pltpu.SemaphoreType.DMA((n_sem,)),
@@ -369,7 +348,7 @@
         compiler_params=params(3),
         cost_estimate=pl.CostEstimate(flops=10**6, bytes_accessed=10**8, transcendentals=0),
         name="backward_plane",
-    )(part_own.reshape(half), part_pair.reshape(half), resid, scale, gain[None])
+    )(part.reshape(CUBE + (BLK, width)), resid, scale, gain[None])
     return own.reshape(-1, width), halves.reshape(-1, width // 2)
 
 
@@ -409,11 +388,13 @@
     def pick(array, axis, index):
         return lax.dynamic_index_in_dim(array, index, axis, keepdims=False)
 
+    def in_order(own, pair):
+        return jnp.where(yhi == 0, jnp.concatenate([own, pair], 0), jnp.concatenate([pair, own], 0))
+
     rows, cols = head_weight.shape
     hw = head_weight.reshape(rows, 8, 2, cols // 16)
     head_pair = swap(pick(hw, 2, 1 - yhi).reshape(rows, cols // 2))
-    head_own = gather(pick(hw, 2, yhi).reshape(rows, cols // 2))
-    head_pair = gather(head_pair)
+    head = gather(in_order(pick(hw, 2, yhi).reshape(rows, cols // 2), head_pair))
 
     tok, width = features.shape
     xfloat = features.astype(f32)
@@ -422,22 +403,25 @@
     pre = jnp.dot(normed, w_in, preferred_element_type=f32)
     act = jax.nn.silu(pre).astype(bf16)
     part = jnp.dot(act, w_out, preferred_element_type=f32).astype(bf16)
-    final_own, final_pair, resid, scale = call_forward(part, features, final_gain, rows)
+    final, resid, scale = call_forward(part, features, final_gain)
 
     split = normed.reshape(tok, 8, 2, rows)
     normed_own = pick(split, 2, yhi).reshape(tok, width // 2)
     normed_pair = swap(pick(split, 2, 1 - yhi).reshape(tok, width // 2))
-    normed2 = jnp.concatenate([normed_own, normed_pair], 0)
-    act2 = jnp.concatenate([act, swap(act)], 0)
+    act_pair = swap(act)
 
     tw = target_buffer.shape[1]
     ordered = target_buffer[positions].reshape(8, -1, tw)
     target = lax.all_to_all(ordered, "z", split_axis=0, concat_axis=2, tiled=True)[0]
-    toks = lax.all_gather(token_ids, "yhi", axis=0, tiled=True)
-
-    logits = jnp.dot(final_own, head_own, preferred_element_type=f32) + jnp.dot(
-        final_pair, head_pair, preferred_element_type=f32
+    toks = in_order(token_ids, swap(token_ids))
+
+    final, normed_pair, act_pair, target, toks = lax.optimization_barrier(
+        (final, normed_pair, act_pair, target, toks)
     )
+    normed2 = jnp.concatenate([normed_own, normed_pair], 0)
+    act2 = jnp.concatenate([act, act_pair], 0)
+
+    logits = jnp.dot(final, head, preferred_element_type=f32)
     tfloat = target.astype(f32)
     top_q = jnp.max(logits, -1)
     top_p = jnp.max(tfloat, -1)
@@ -453,28 +437,30 @@
     onehot = (columns_here[None, :] == toks[:, None]).astype(f32)
     dlogits = (qprob - pprob + HARD * (qprob - onehot)).astype(bf16)
 
-    gh_pair = lax.dot_general(final_pair, dlogits, contract, preferred_element_type=f32).astype(bf16)
-    gh_pair = scatter(gh_pair)
-    gh_own = lax.dot_general(final_own, dlogits, contract, preferred_element_type=f32).astype(bf16)
-    gh_own = scatter(gh_own)
-    gh_other = swap(gh_pair)
-    both = jnp.stack([gh_own, gh_other]).reshape(2, rows, 8, tw)
+    gh = lax.dot_general(final, dlogits, contract, preferred_element_type=f32).astype(bf16)
+    gh, dlogits = lax.optimization_barrier((gh, dlogits))
+    gh = scatter(gh).reshape(2, rows, cols // 2)
+    both = jnp.stack([pick(gh, 0, yhi), swap(pick(gh, 0, 1 - yhi))]).reshape(2, rows, 8, tw)
     both = jnp.where(yhi == 0, both, both[::-1])
     grad_head = both.transpose(1, 2, 0, 3).reshape(rows, cols).astype(f32)
 
-    part_own = lax.dot_general(dlogits, head_own, backward, preferred_element_type=f32).astype(bf16)
-    part_pair = lax.dot_general(dlogits, head_pair, backward, preferred_element_type=f32).astype(bf16)
-    dresid, dresid2 = call_backward(part_own, part_pair, resid, scale, final_gain, rows)
-
-    go = lax.dot_general(dresid2, act2, contract, preferred_element_type=f32).astype(bf16)
-    go = scatter(go).astype(f32)
+    part = lax.dot_general(dlogits, head, backward, preferred_element_type=f32).astype(bf16)
+    dresid, dresid2 = call_backward(part, resid, scale, final_gain, rows)
+
     dact = lax.dot_general(dresid, w_out, backward, preferred_element_type=f32)
     sig = jax.nn.sigmoid(pre)
     dpre = (dact * sig * (1.0 + pre * (1.0 - sig))).astype(bf16)
     dpre2 = jnp.concatenate([dpre, swap(dpre)], 0)
-    gi = lax.dot_general(normed2, dpre2, contract, preferred_element_type=f32).astype(bf16)
-    gi = scatter(gi).astype(f32)
-    return (grad_head, gi, go.T)
+    gf = jnp.concatenate(
+        [
+            lax.dot_general(normed2, dpre2, contract, preferred_element_type=f32),
+            lax.dot_general(dresid2, act2, contract, preferred_element_type=f32),
+        ],
+        1,
+    ).astype(bf16)
+    gf = scatter(gf).astype(f32)
+    units = act.shape[1]
+    return (grad_head, gf[:, :units], gf[:, units:].T)
 
 
 def solution(mesh):

time: 331 us -> 273 us (0.82); the launches traced: 327 us -> 273 us
  waiting for transfers between devices: 110 us -> 60.4 us
  Pallas kernels: 106 us -> 114 us
  local copies, waits for them, and re-layouts: 35.4 us -> 28 us
  blocking collectives: 5.02 us -> 0 us
    reduce_scatter x4 -> x2, waiting for transfers between devices: 76.1 us -> 48.8 us  [the longest x1 48.8 us: body(): gf = scatter(gf).astype(f32)]
    ppermute x1, waiting for transfers between devices: 22.4 us -> 0.01 us  [body(): normed_pair = swap(pick(split, 2, 1 - yhi).reshape(tok, width // 2))]
    pallas_call x1, Pallas kernels: 42.8 us -> 58 us  [call_forward(): pl.pallas_call(functools.partial(forward_kernel, width), out_shape=(sd(CU...]
    pallas_call x1, Pallas kernels: 14.7 us -> 9.16 us  [call_stats(): pl.pallas_call(stats_kernel, out_shape=jax.ShapeDtypeStruct((8, n), f32),...]
    all_gather x1 -> x0, blocking collectives: 5.02 us -> none  [body(): toks = lax.all_gather(token_ids, 'yhi', axis=0, tiled=True)]
    ppermute x2 -> x3, starting transfers between devices: 3.27 us -> 8.16 us  [the longest x1 3.79 us: body(): toks = in_order(token_ids, swap(token_ids))]
    unnamed x54 -> x31, local copies, waits for them, and re-layouts: 13.9 us -> 9.32 us
    dot_general x6 -> x3, matrix products: 17.3 us -> 17 us  [the longest x1 6.58 us: body(): lax.dot_general(final, dlogits, contract, preferred_element_type=f32)]
  transfers between devices with their start and end apart: 12 -> 10, of which waited for: 6 -> 3; matrix products, arithmetic and copies ran while one was open for 16% -> 15% of each run, Pallas kernels for 28% -> 38%
where the time goes in v3:
time: 273 us
  Pallas kernels  114 us (42%)
  waiting for transfers between devices  60.4 us (22%)
  local copies, waits for them, and re-layouts  28 us (10%)
  matrix products  24.8 us (9%)
  starting transfers between devices  22.2 us (8%)
  between operations  14.1 us (5%)
  other arithmetic  9.79 us (4%)
    pallas_call x1, Pallas kernels, call_forward(): pl.pallas_call(functools.partial(forward_kernel, width), out_shape=(sd(CU...  58 us
    reduce_scatter x1, waiting for transfers between devices, body(): gf = scatter(gf).astype(f32)  48.8 us
    pallas_call x1, Pallas kernels, call_backward(): pl.pallas_call(functools.partial(backward_kernel, width, run), out_shape=...  46.5 us
    gather x1, local copies, waits for them, and re-layouts, body(): ordered = target_buffer[positions].reshape(8, -1, tw)  12.1 us
    unnamed x31, local copies, waits for them, and re-layouts  9.32 us
    pallas_call x1, Pallas kernels, call_stats(): pl.pallas_call(stats_kernel, out_shape=jax.ShapeDtypeStruct((8, n), f32),...  9.16 us
    all_to_all x1, starting transfers between devices, body(): lax.all_to_all(ordered, 'z', split_axis=0, concat_axis=2, tiled=True)[0]  8.32 us
    dot_general x1, matrix products, body(): lax.dot_general(final, dlogits, contract, preferred_element_type=f32)  6.58 us
  transfers between devices with their start and end apart: 10, of which 3 were waited for; matrix products, arithmetic and copies ran while one was open for 15% of the time, Pallas kernels for 38%

profile of v3, /device:TPU:1, one launch (start us, length us, event | category | flops | bytes accessed | tf_op | source)
XLA Modules:
  0.0 273.0 jit_solution(3178166139475248207)
XLA Ops:
  8.6 3.8 %collective-permute-start.3 = (bf16[256,512]{0,1:T(8,128)(2,1)S(1)}, bf16[256,512]{0,1:T(8,128)(2,1)S(1)}, u32[]{:S(2)}, u32[]{:S(2)}) collective-permute-start(bf16[256,512]{0,1:T(8,128)(2,1)S(1)} %bitcast.69), channel_id=1, source_target_pairs={{0,1},{1,0},{2,3},{3,2},{4,5},{5,4},{6,7},{7,6},{8,9},{9,8},{10,11... | collective-permute-start | bytes 786440 | tf_op jit(solution)/shard_map/ppermute | solution.py:396
  12.4 5.0 %collective-permute-done.3 = bf16[256,512]{0,1:T(8,128)(2,1)S(1)} collective-permute-done((bf16[256,512]{0,1:T(8,128)(2,1)S(1)}, bf16[256,512]{0,1:T(8,128)(2,1)S(1)}, u32[]{:S(2)}, u32[]{:S(2)}) %collective-permute-start.3) | collective-permute-done | bytes 262176 | tf_op jit(solution)/shard_map/ppermute | solution.py:396
  18.4 3.8 %collective-permute-start.2 = (s32[256]{0:T(256)S(1)}, s32[256]{0:T(256)S(1)}, u32[]{:S(2)}, u32[]{:S(2)}) collective-permute-start(s32[256]{0:T(256)S(1)} %copy-done.10), channel_id=1, source_target_pairs={{0,1},{1,0},{2,3},{3,2},{4,5},{5,4},{6,7},{7,6},{8,9},{9,8},{10,11... | collective-permute-start | bytes 3080 | tf_op jit(solution)/shard_map/ppermute | solution.py:416
  22.7 12.1 %gather_fusion = bf16[4096,64]{1,0:T(8,128)(2,1)S(1)} fusion(bf16[4096,64]{1,0:T(8,128)(2,1)S(1)} %copy.22, s32[4096]{0:T(1024)S(1)} %fusion.16), kind=kCustom, calls=%fused_computation | custom fusion | bytes 1064960 | tf_op jit(solution)/shard_map/gather | solution.py:414
  35.9 8.3 %all-to-all-start = ((bf16[8,512,64]{1,2,0:T(8,128)(2,1)}), bf16[8,512,64]{1,2,0:T(8,128)(2,1)S(1)}, u32[]{:S(2)}, u32[]{:S(2)}) async-start(bf16[8,512,64]{1,2,0:T(8,128)(2,1)} %copy.23), calls=%async_computation | async-start | bytes 1048576 | tf_op jit(solution)/shard_map/all_to_all | solution.py:415
  44.3 2.5 copy.21
  46.8 2.2 fusion
  49.1 2.1 fusion.2
  51.2 1.5 constant_dynamic-slice_fusion
  52.7 1.9 multiply_convert_fusion
  54.6 2.9 %collective-permute-start.1 = (bf16[256,448]{0,1:T(8,128)(2,1)S(1)}, bf16[256,448]{0,1:T(8,128)(2,1)S(1)}, u32[]{:S(2)}, u32[]{:S(2)}) collective-permute-start(bf16[256,448]{0,1:T(8,128)(2,1)S(1)} %get-tuple-element.43), channel_id=1, source_target_pairs={{0,1},{1,0},{2,3},{3,2},{4,5},{5,4},{6,7},{7,6},{8,9},{9,8},{10,11... | collective-permute-start | bytes 688136 | tf_op jit(solution)/shard_map/ppermute | solution.py:411
  58.8 1.6 copy-done.1
  60.4 58.0 %forward_plane.1 = (bf16[2,2,2,2,2,16,4096]{6,5,4,3,2,1,0:T(8,128)(2,1)S(1)}, f32[16,4096]{1,0:T(8,128)S(1)}, f32[16,128]{1,0:T(8,128)S(1)}) custom-call(bf16[2,2,2,2,16,4096]{5,4,3,2,1,0:T(8,128)(2,1)S(1)} %bitcast.50, bf16[2,2,2,2,16,4096]{5,4,3,2,1,0:T(8,128)(2,1)S(1)} %bitcast.51, f32[1,4096]{1,0:T(1,128)S(1)} %bitcast.52), custom_call_target="tpu_custom_call" | custom-call | flops 1000000 | bytes 100000000 | tf_op jit(solution)/shard_map/forward_plane/pallas_call | solution.py:302
  118.5 2.0 copy-done.3
  120.8 5.8 %fusion.31 = (f32[512]{0:T(512)S(1)}, f32[512,512]{0,1:T(8,128)S(1)}) fusion(bf16[512,4096]{1,0:T(8,128)(2,1)} %bitcast.54, bf16[4096,512]{0,1:T(8,128)(2,1)} %all-gather.2.cloned.1.call-done), kind=kOutput, calls=%fused_computation.66 | convolution fusion | flops 2147745280 | bytes 9439232 | tf_op jit(solution)/shard_map/dot_general | solution.py:424
  126.9 9.2 %softmax_stats.1 = f32[8,512]{1,0:T(8,128)S(1)} custom-call(f32[8,512]{1,0:T(8,128)S(1)} %stack.29.stats), custom_call_target="tpu_custom_call" | custom-call | tf_op jit(solution)/shard_map/softmax_stats/pallas_call | solution.py:358
  136.7 6.6 %convolution_convert_fusion.1 = bf16[4096,512]{1,0:T(8,128)(2,1)} fusion(bf16[512,4096]{1,0:T(8,128)(2,1)} %bitcast.55, bf16[512,512]{0,1:T(8,128)(2,1)S(1)} %add_convert_fusion), kind=kOutput, calls=%fused_computation.2 | convolution fusion | flops 2149580800 | bytes 8912896 | tf_op jit(solution)/shard_map/dot_general | solution.py:440
  143.5 4.6 %convolution_convert_fusion = bf16[512,4096]{1,0:T(8,128)(2,1)S(1)} fusion(bf16[512,512]{0,1:T(8,128)(2,1)S(1)} %add_convert_fusion, bf16[4096,512]{0,1:T(8,128)(2,1)} %all-gather.2.cloned.1.call-done), kind=kOutput, calls=%fused_computation.1 | convolution fusion | flops 2149580800 | bytes 8912896 | tf_op jit(solution)/shard_map/dot_general | solution.py:447
  148.1 46.5 %backward_plane.1 = (bf16[2,2,2,2,16,4096]{5,4,3,2,1,0:T(8,128)(2,1)S(1)}, bf16[2,2,2,2,2,16,2048]{6,5,4,3,2,1,0:T(8,128)(2,1)S(1)}) custom-call(bf16[2,2,2,2,2,16,4096]{6,5,4,3,2,1,0:T(8,128)(2,1)S(1)} %bitcast.49, f32[16,4096]{1,0:T(8,128)S(1)} %get-tuple-element.22.resid, f32[16,128]{1,0:T(8,128)S(1)} %get-tuple-element.23.scale, f32[1,4096]{1,0:T(1,128)S(1)} %bitcast.53), custom_call_target="tpu_custom_call" | custom-call | flops 1000000 | bytes 100000000 | tf_op jit(solution)/shard_map/backward_plane/pallas_call | solution.py:332
  198.4 6.5 %collective-permute-done.5 = bf16[256,448]{0,1:T(8,128)(2,1)S(1)} collective-permute-done((bf16[256,448]{0,1:T(8,128)(2,1)S(1)}, bf16[256,448]{0,1:T(8,128)(2,1)S(1)}, u32[]{:S(2)}, u32[]{:S(2)}) %collective-permute-start.5) | collective-permute-done | bytes 229408 | tf_op jit(solution)/shard_map/ppermute | solution.py:453
  204.9 2.4 convolution_convert_fusion.4
  207.3 2.2 pad_maximum_fusion
  212.3 48.8 %reduce-scatter.5.cloned.1.call-done = bf16[256,896]{0,1:T(8,128)(2,1)} async-done(((bf16[2048,896]{0,1:T(8,128)(2,1)}), bf16[256,896]{0,1:T(8,128)(2,1)}) %reduce-scatter.5.cloned.1.call-update) | async-done | bytes 458768 | tf_op jit(solution)/shard_map/reduce_scatter | solution.py:461
  261.1 1.7 slice.26
  (70 shorter events, 16.9 us)
Async XLA Ops:
  7.2 11.2 %copy-start.10 = (s32[256]{0:T(256)S(1)}, s32[256]{0:T(256)}, u32[]{:S(2)}) copy-start(s32[256]{0:T(256)} %param.10) | copy-start | bytes 3076
  7.2 15.0 %copy-start.7 = (bf16[4096,64]{0,1:T(8,128)(2,1)S(1)}, bf16[4096,64]{0,1:T(8,128)(2,1)}, u32[]{:S(2)}) copy-start(bf16[4096,64]{0,1:T(8,128)(2,1)} %param.12) | copy-start | bytes 1572868
  7.2 15.5 %copy-start.9 = (s32[4096]{0:T(1024)S(1)}, s32[4096]{0:T(1024)}, u32[]{:S(2)}) copy-start(s32[4096]{0:T(1024)} %param.11) | copy-start | bytes 49156
  7.2 113.6 %all-gather.2.cloned.1.call-start = ((), (), s32[]{:S(2)}) async-start(), calls=%async_computation.3 | async-start | bytes 4718592 | tf_op jit(solution)/shard_map/all_gather | solution.py:397
  8.6 8.8 %collective-permute-start.3 = (bf16[256,512]{0,1:T(8,128)(2,1)S(1)}, bf16[256,512]{0,1:T(8,128)(2,1)S(1)}, u32[]{:S(2)}, u32[]{:S(2)}) collective-permute-start(bf16[256,512]{0,1:T(8,128)(2,1)S(1)} %bitcast.69), channel_id=1, source_target_pairs={{0,1},{1,0},{2,3},{3,2},{4,5},{5,4},{6,7},{7,6},{8,9},{9,8},{10,11... | collective-permute-start | bytes 786440 | tf_op jit(solution)/shard_map/ppermute | solution.py:396
  18.4 102.1 %collective-permute-start.2 = (s32[256]{0:T(256)S(1)}, s32[256]{0:T(256)S(1)}, u32[]{:S(2)}, u32[]{:S(2)}) collective-permute-start(s32[256]{0:T(256)S(1)} %copy-done.10), channel_id=1, source_target_pairs={{0,1},{1,0},{2,3},{3,2},{4,5},{5,4},{6,7},{7,6},{8,9},{9,8},{10,11... | collective-permute-start | bytes 3080 | tf_op jit(solution)/shard_map/ppermute | solution.py:416
  34.8 9.5 %copy-start = (bf16[256,4096]{1,0:T(8,128)(2,1)S(1)}, bf16[256,4096]{1,0:T(8,128)(2,1)}, u32[]{:S(2)}) copy-start(bf16[256,4096]{1,0:T(8,128)(2,1)} %param.9) | copy-start | bytes 6291460
  35.9 13.1 %copy-start.8 = (f32[4096]{0:T(1024)S(1)}, f32[4096]{0:T(1024)}, u32[]{:S(2)}) copy-start(f32[4096]{0:T(1024)} %param.13) | copy-start | bytes 49156
  35.9 84.5 %all-to-all-start = ((bf16[8,512,64]{1,2,0:T(8,128)(2,1)}), bf16[8,512,64]{1,2,0:T(8,128)(2,1)S(1)}, u32[]{:S(2)}, u32[]{:S(2)}) async-start(bf16[8,512,64]{1,2,0:T(8,128)(2,1)} %copy.23), calls=%async_computation | async-start | bytes 1048576 | tf_op jit(solution)/shard_map/all_to_all | solution.py:415
  44.3 165.3 %reduce-scatter.3.cloned.1.call-start = ((), (), s32[]{:S(2)}) async-start(), calls=%async_computation.4 | async-start | bytes 4718592 | tf_op jit(solution)/shard_map/reduce_scatter | solution.py:442
  49.0 3.7 %copy-start.11 = (bf16[4096,448]{0,1:T(8,128)(2,1)S(1)}, bf16[4096,448]{0,1:T(8,128)(2,1)}, u32[]{:S(2)}) copy-start(bf16[4096,448]{0,1:T(8,128)(2,1)} %param.15) | copy-start | bytes 11010052
  52.6 4.9 %copy-start.4 = (bf16[448,4096]{1,0:T(8,128)(2,1)S(1)}, bf16[448,4096]{1,0:T(8,128)(2,1)}, u32[]{:S(2)}) copy-start(bf16[448,4096]{1,0:T(8,128)(2,1)} %param.16) | copy-start | bytes 11010052
  52.6 67.8 %collective-permute-start = (bf16[256,2048]{0,1:T(8,128)(2,1)}, bf16[256,2048]{0,1:T(8,128)(2,1)}, u32[]{:S(2)}, u32[]{:S(2)}) collective-permute-start(bf16[256,2048]{0,1:T(8,128)(2,1)} %bitcast.5), channel_id=1, source_target_pairs={{0,1},{1,0},{2,3},{3,2},{4,5},{5,4},{6,7},{7,6},{8,9},{9,8},{10,11... | collective-permute-start | bytes 3145736 | tf_op jit(solution)/shard_map/ppermute | solution.py:410
  54.6 4.2 %copy-start.2 = (f32[4096]{0:T(1024)S(1)}, f32[4096]{0:T(1024)}, u32[]{:S(2)}) copy-start(f32[4096]{0:T(1024)} %param.14) | copy-start | bytes 49156
  54.6 65.9 %collective-permute-start.1 = (bf16[256,448]{0,1:T(8,128)(2,1)S(1)}, bf16[256,448]{0,1:T(8,128)(2,1)S(1)}, u32[]{:S(2)}, u32[]{:S(2)}) collective-permute-start(bf16[256,448]{0,1:T(8,128)(2,1)S(1)} %get-tuple-element.43), channel_id=1, source_target_pairs={{0,1},{1,0},{2,3},{3,2},{4,5},{5,4},{6,7},{7,6},{8,9},{9,8},{10,11... | collective-permute-start | bytes 688136 | tf_op jit(solution)/shard_map/ppermute | solution.py:411
  58.8 1.6 copy-start.1
  118.5 2.0 copy-start.3
  143.3 117.8 %reduce-scatter.5.cloned.1.call-start = ((), (), s32[]{:S(2)}) async-start(), calls=%async_computation.5 | async-start | bytes 4128768 | tf_op jit(solution)/shard_map/reduce_scatter | solution.py:461
  148.1 46.5 %copy-start.5 = (bf16[448,4096]{1,0:T(8,128)(2,1)S(1)}, bf16[448,4096]{1,0:T(8,128)(2,1)}, u32[]{:S(2)}) copy-start(bf16[448,4096]{1,0:T(8,128)(2,1)} %param.16) | copy-start | bytes 11010052
  148.1 46.5 %copy-start.12 = (f32[256,448]{0,1:T(8,128)S(1)}, f32[256,448]{0,1:T(8,128)}, u32[]{:S(2)}) copy-start(f32[256,448]{0,1:T(8,128)} %get-tuple-element.44) | copy-start | bytes 1376260
  195.8 9.2 %copy-start.6 = (bf16[256,8,1,256]{0,3,2,1:T(8,128)(2,1)S(1)}, bf16[256,8,1,256]{0,3,2,1:T(8,128)(2,1)}, u32[]{:S(2)}) copy-start(bf16[256,8,1,256]{0,3,2,1:T(8,128)(2,1)} %get-tuple-element.33) | copy-start | bytes 3145732
  195.8 9.2 %collective-permute-start.5 = (bf16[256,448]{0,1:T(8,128)(2,1)S(1)}, bf16[256,448]{0,1:T(8,128)(2,1)S(1)}, u32[]{:S(2)}, u32[]{:S(2)}) collective-permute-start(bf16[256,448]{0,1:T(8,128)(2,1)S(1)} %fusion.7), channel_id=1, source_target_pairs={{0,1},{1,0},{2,3},{3,2},{4,5},{5,4},{6,7},{7,6},{8,9},{9,8},{10,11... | collective-permute-start | bytes 688136 | tf_op jit(solution)/shard_map/ppermute | solution.py:453
  210.8 54.0 %collective-permute-start.4 = (bf16[256,512]{0,1:T(8,128)(2,1)S(1)}, bf16[256,512]{0,1:T(8,128)(2,1)S(1)}, u32[]{:S(2)}, u32[]{:S(2)}) collective-permute-start(bf16[256,512]{0,1:T(8,128)(2,1)S(1)} %bitcast.70), channel_id=1, source_target_pairs={{0,1},{1,0},{2,3},{3,2},{4,5},{5,4},{6,7},{7,6},{8,9},{9,8},{10,11... | collective-permute-start | bytes 786440 | tf_op jit(solution)/shard_map/ppermute | solution.py:443
Sparse Core Ops, SparseCore 0:
  18.5 70.6 all-gather.1
  143.4 55.7 reduce-scatter.2
  209.7 51.3 reduce-scatter.4

commit v4 on v3

v4 whole, which is shorter than its diff:
```python
import functools
import jax
import jax.numpy as jnp
from jax import lax
from jax.experimental import pallas as pl
from jax.experimental.pallas import tpu as pltpu
from jax.sharding import Mesh, PartitionSpec as P

EPS = 1e-05
HARD = 0.5
MESH = pl.DeviceIdType.MESH
LEAD = ("YB", "core", "XA", "YA", "XB")
REST = ("YB", "XA", "YA", "XB")
ICI3 = ("XA", "YA", "XB")
ICI4 = ("XA", "YA", "XB", "YB")
CUBE = (2,) * 5
BLK = 16
F32 = jnp.float32
BF16 = jnp.bfloat16


def place():
    x, ylo, yhi, core, z = (lax.axis_index(n) for n in ("x", "ylo", "yhi", "core", "z"))
    nz = lax.axis_size("z")
    y = 2 * yhi + ylo
    odd = lax.rem(x, 2)
    bits = {
        "core": core,
        "XA": lax.rem(lax.div(x + 1, 2), 2),
        "XB": lax.div(x, 2),
        "YA": lax.rem(lax.div(y + 1, 2), 2),
        "YB": yhi,
    }
    to = {
        "core": {"core": 1 - core},
        "XA": {"x": x + 1 - 2 * odd},
        "XB": {"x": lax.rem(x + 3 + 2 * odd, 4)},
        "YA": {"ylo": 1 - ylo},
        "YB": {"ylo": 1 - ylo, "yhi": 1 - yhi},
        "pair": {"yhi": 1 - yhi},
        "up": {"z": lax.rem(z + 1, nz)},
        "down": {"z": lax.rem(z + nz - 1, nz)},
    }
    for i in range(1, nz):
        to[i] = {"z": lax.rem(z + i, nz)}
    return bits, to, z, nz


def at(names, fixed, cols=None):
    where = tuple(fixed.get(n, slice(None)) for n in names)
    return where + (slice(None), slice(None) if cols is None else pl.ds(*cols))


def corners(names):
    out = [{}]
    for n in names:
        out = [dict(o, **{n: v}) for o in out for v in (0, 1)]
    return out


class Sender:
    def __init__(self, send_sem, recv_sem, to):
        self.send_sem, self.recv_sem, self.to = send_sem, recv_sem, to
        self.all = []

    def go(self, src, dst, dim):
        n = len(self.all)
        c = pltpu.make_async_remote_copy(
            src_ref=src,
            dst_ref=dst,
            send_sem=self.send_sem.at[n],
            recv_sem=self.recv_sem.at[n],
            device_id=self.to[dim],
            device_id_type=MESH,
        )
        c.start()
        self.all.append(c)
        return c

    def drain(self):
        for c in self.all:
            c.wait_send()


class Local:
    def __init__(self, sem):
        self.sem = sem
        self.n = 0

    def go(self, src, dst):
        c = pltpu.make_async_copy(src, dst, self.sem.at[self.n])
        c.start()
        self.n += 1
        return c


def colours(n, width):
    tiles = width // 128
    edges = [128 * (tiles * k // n) for k in range(n + 1)]
    return [(edges[k], edges[k + 1] - edges[k]) for k in range(n)]


def meet(to, dims):
    barrier = pltpu.get_barrier_semaphore()
    for d in dims:
        pl.semaphore_signal(barrier, inc=1, device_id=to[d], device_id_type=MESH)
    pl.semaphore_wait(barrier, len(dims))


def step(thread):
    return next(thread, None)


def finish(thread):
    for _ in thread:
        pass


def reduce_cube(send, bits, names, dims, width, part, total, landed):
    rest = tuple(n for n in names if n != "core")
    n = len(dims)
    cuts = colours(n, width)
    first, second = [], []
    for keep, held in ((1, first), (0, second)):
        for k in range(n):
            d = dims[k]
            bit = 1 - bits[d] if keep else bits[d]
            src = part.at[at(names, {"core": 1 - bits["core"], d: bit}, cuts[k])]
            dst = total.at[at(rest, {d: bit}, cuts[k])]
            held.append(send.go(src, dst, "core"))

    def merge(k, bit):
        d = dims[k]
        for f in corners([m for m in rest if m != d]):
            f = dict(f, **{d: bit})
            w = at(rest, f, cuts[k])
            total[w] = total[w] + part[at(names, dict(f, core=bits["core"]), cuts[k])]

    def start(k, j):
        d = dims[(k + j) % n]
        fixed = {dims[(k + i) % n]: bits[dims[(k + i) % n]] for i in range(j)}
        fixed[d] = 1 - bits[d]
        return send.go(total.at[at(rest, fixed, cuts[k])], landed[k * n + j], d)

    yield
    flying = []
    for k in range(n):
        first[k].wait_recv()
        merge(k, 1 - bits[dims[k]])
        flying.append(start(k, 0))
    yield
    for k in range(n):
        second[k].wait_recv()
        merge(k, bits[dims[k]])
    for j in range(n):
        yield
        for k in range(n):
            flying[k].wait_recv()
            done = [dims[(k + i) % n] for i in range(j + 1)]
            fixed = {m: bits[m] for m in done}
            left = [m for m in rest if m not in done]
            for f in corners(left):
                w = at(rest, dict(f, **fixed), cuts[k])
                total[w] = total[w] + landed[k * n + j][tuple(f[m] for m in left)]
            if j + 1 < n:
                flying[k] = start(k, j + 1)


def gather_cube(send, bits, dims, width, full):
    n = len(dims)
    cuts = colours(n, width)
    arriving = []
    for j in range(n):
        flying = []
        for k in range(n):
            d = dims[(k + j) % n]
            done = [dims[(k + i) % n] for i in range(j)]
            piece = full.at[at(LEAD, {m: bits[m] for m in LEAD if m not in done}, cuts[k])]
            flying.append(send.go(piece, piece, d))
        if j == 0:
            arriving.append(send.go(full.at[at(LEAD, bits)], full.at[at(LEAD, bits)], "core"))
        yield
        for k in range(n):
            flying[k].wait_recv()
            d = dims[(k + j) % n]
            done = [dims[(k + i) % n] for i in range(j)]
            fixed = {m: bits[m] for m in LEAD if m not in done}
            fixed[d] = 1 - bits[d]
            piece = full.at[at(LEAD, fixed, cuts[k])]
            arriving.append(send.go(piece, piece, "core"))
    for c in arriving:
        c.wait_recv()


def ring_gather(send, z, nz, slots, full, late):
    half = nz // 2

    def block(i, q):
        return full.at[lax.rem(z + nz + i, nz), slots[q]]

    ups, downs = [None, None], [None, None]
    for q in range(2):
        if q:
            late.wait_recv()
        if half > 1 or q == 0:
            ups[q] = send.go(block(0, q), block(0, q), "up")
        if half > 1 or q == 1:
            downs[q] = send.go(block(0, q), block(0, q), "down")
        yield
    for s in range(1, half + 1):
        for q in range(2):
            if s < half or q == 0:
                ups[q].wait_recv()
                if s + 1 < half or (s + 1 == half and q == 0):
                    ups[q] = send.go(block(-s, q), block(-s, q), "up")
            if s < half or q == 1:
                downs[q].wait_recv()
                if s + 1 < half or (s + 1 == half and q == 1):
                    downs[q] = send.go(block(s, q), block(s, q), "down")
            yield


def ring_scatter(send, z, nz, part, ups, downs):
    half = nz // 2
    rows = part.shape[1] // 2
    cut = [pl.ds(0, rows), pl.ds(rows, rows)]

    def mine(i, q):
        return part.at[lax.rem(z + nz + i, nz), cut[q]]

    flying = {}
    for way, landed, sign, q in (("up", ups, 1, 0), ("down", downs, -1, 1)):
        flying[way, 0, q] = send.go(mine(sign * half, q), landed[0].at[cut[q]], way)
        if half > 1:
            q = 1 - q
            flying[way, 1, q] = send.go(mine(sign * (half - 1), q), landed[1].at[cut[q]], way)
    yield
    order = [(0, 0)] + [(s, q) for s in range(1, half) for q in (1, 0)]
    for s, lead in order:
        for way, landed, sign in (("up", ups, 1), ("down", downs, -1)):
            q = lead if way == "up" else 1 - lead
            flying[way, s, q].wait_recv()
            if s + 1 < half:
                ref = landed[s].at[cut[q]]
                ref[...] = ref[...] + mine(sign * (half - 1 - s), q)[...]
                flying[way, s + 1, q] = send.go(ref, landed[s + 1].at[cut[q]], way)
        yield


def ring_result(z, part, ups, downs):
    own = part[z].astype(F32)
    if len(ups) > 1:
        return own + ups[-1][...].astype(F32) + downs[-1][...].astype(F32)
    rows = part.shape[1] // 2
    return own + jnp.concatenate([ups[0][:rows], downs[0][rows:]], 0).astype(F32)


def landing(dims, width):
    n = len(dims)
    cuts = colours(n, width)
    return [
        pltpu.VMEM((2,) * (n - 1 - j) + (BLK, cuts[k][1]), BF16) for k in range(n) for j in range(n)
    ]


def forward_kernel(
    feats, gain_in, w_in, w_out, gain, hw, buf, pos, toks,
    final_out, head_out, resid_out, scale_out, normed_out, pre_out, target_out, toks_out,
    fv, w1, w2, bv, pv, normed, pre, part, total, full, head, ordered, target,
    send_sem, recv_sem, local_sem, *landed,
):
    bits, to, z, nz = place()
    yhi = bits["YB"]
    width = fv.shape[1]
    tok = fv.shape[0]
    run = head.shape[2]
    units = pre.shape[1]
    local = Local(local_sem)
    got_head = local.go(hw.at[yhi], head.at[z, yhi])
    got_f = local.go(feats, fv)
    got_w1 = local.go(w_in, w1)
    got_w2 = local.go(w_out, w2)
    got_p = local.go(pos, pv)
    got_b = local.go(buf, bv)
    meet(to, LEAD + ("pair", "up", "down") + tuple(range(2, nz - 1)))
    send = Sender(send_sem, recv_sem, to)
    late = send.go(hw.at[1 - yhi], head.at[z, yhi], "pair")
    got_head.wait()
    ring = ring_gather(send, z, nz, (yhi, 1 - yhi), head, late)
    step(ring)
    swapped = [send.go(toks, toks_out.at[yhi], "pair")]
    kept = [local.go(toks, toks_out.at[yhi])]

    got_f.wait()
    chunk = 32

    def norm_rows(i, _):
        rows = pl.ds(pl.multiple_of(i * chunk, chunk), chunk)
        x = fv[rows, :].astype(F32)
        r = lax.rsqrt(jnp.mean(x * x, -1, keepdims=True) + EPS)
        normed[rows, :] = (x * r * gain_in[...]).astype(BF16)
        return 0

    lax.fori_loop(0, tok // chunk, norm_rows, 0)
    for b in range(width // (2 * run)):
        there = pl.multiple_of((2 * b + 1 - yhi) * run, run)
        here = pl.multiple_of((2 * b + yhi) * run, run)
        cols = pl.ds(b * run, run)
        swapped.append(
            send.go(normed.at[:, pl.ds(there, run)], normed_out.at[yhi, :, cols], "pair")
        )
        kept.append(local.go(normed.at[:, pl.ds(here, run)], normed_out.at[yhi, :, cols]))
    got_w1.wait()
    deep = width // 4
    for c in range(4):
        k = pl.ds(c * deep, deep)
        prod = jnp.dot(normed[:, k], w1[k, :], preferred_element_type=F32)
        pre[...] = prod if c == 0 else pre[...] + prod
    swapped.append(send.go(pre, pre_out.at[yhi], "pair"))
    kept.append(local.go(pre, pre_out.at[yhi]))
    step(ring)
    v = pre[...]
    act = (v * jax.nn.sigmoid(v)).astype(BF16)
    got_w2.wait()
    wide = width // 8
    names = LEAD[1:]
    for c in range(8):
        cols = (c * wide, wide)
        block = jnp.dot(act, w2[:, pl.ds(*cols)], preferred_element_type=F32).astype(BF16)
        for i, f in enumerate(corners(names)):
            part[at(names, f, cols)] = block[i * BLK : (i + 1) * BLK]

    got_p.wait()
    got_b.wait()
    n_buf = bv.shape[0]
    piece = 512 if n_buf % 512 == 0 else n_buf

    def ordered_rows(i):
        dest = lax.rem(z + i, nz)

        def inner(t, sums):
            start = pl.multiple_of(t * piece, piece)
            rows = bv[pl.ds(start, piece), :]
            out = []
            for h in range(2):
                there = pv[dest, h] - start
                lane = lax.broadcasted_iota(jnp.int32, (tok, piece), 1)
                hot = jnp.where(there == lane, 1.0, 0.0).astype(BF16)
                out.append(sums[h] + jnp.dot(hot, rows, preferred_element_type=F32))
            return tuple(out)

        zero = jnp.zeros((tok, bv.shape[1]), F32)
        a, b = lax.fori_loop(0, n_buf // piece, inner, (zero, zero))
        return jnp.concatenate([a, b], 1).astype(BF16)

    def gather_target():
        for i in range(1, nz):
            ordered[i] = ordered_rows(i)
            way = "up" if i == 1 else "down" if i == nz - 1 else i
            swapped.append(send.go(ordered.at[i], target.at[z], way))
            yield
        target[z] = ordered_rows(0)
        yield

    rows16 = fv.at[pl.ds(pl.multiple_of(own_row(bits), BLK), BLK)]
    side = gather_target()
    for _ in reduce_cube(send, bits, names, ICI3, width, part, total, landed):
        step(side)
        step(ring)
    hidden = total[at(ICI3, bits)].astype(F32)
    resid = rows16[...].astype(F32) + hidden
    rscale = lax.rsqrt(jnp.mean(resid * resid, -1, keepdims=True) + EPS)
    resid_out[...] = resid
    scale_out[...] = jnp.broadcast_to(rscale, scale_out.shape)
    full[at(LEAD, bits)] = (resid * rscale * gain[...]).astype(BF16)
    for _ in gather_cube(send, bits, ICI4, width, full):
        step(side)
        step(ring)
    put = [local.go(full, final_out)]
    finish(side)
    finish(ring)
    put.append(local.go(head, head_out))
    for c in swapped:
        c.wait_recv()
    put.append(local.go(target, target_out))
    for c in kept + put:
        c.wait()
    send.drain()


def own_row(bits):
    r = bits["core"]
    for n in ("XA", "YA", "XB"):
        r = 2 * r + bits[n]
    return r * BLK


def backward_kernel(
    run, part, resid, scale, gain, gh, dresid_out, half_out, gh_out,
    total, full, gh_sum, send_sem, recv_sem, local_sem, *landed,
):
    bits, to, z, nz = place()
    width = part.shape[-1]
    h = nz // 2
    landed, ups, downs = landed[: -2 * h], landed[-2 * h : -h], landed[-h:]
    meet(to, LEAD + ("up", "down"))
    send = Sender(send_sem, recv_sem, to)
    local = Local(local_sem)
    ring = ring_scatter(send, z, nz, gh, ups, downs)
    step(ring)
    for i, _ in enumerate(reduce_cube(send, bits, LEAD, ICI4, width, part, total, landed)):
        if i >= 2:
            step(ring)
    dfinal = total[at(REST, bits)].astype(F32)
    r = resid[...]
    rscale = scale[...][:, :1]
    scaled = dfinal * gain[...]
    inner = jnp.sum(scaled * r, -1, keepdims=True)
    full[at(LEAD, bits)] = (rscale * scaled - r * (rscale * rscale * rscale / width * inner)).astype(
        BF16
    )
    for i, _ in enumerate(gather_cube(send, bits, ICI4, width, full)):
        step(ring)
    put = [local.go(full, dresid_out)]
    for b in range(width // (2 * run)):
        col = pl.multiple_of((2 * b + bits["YB"]) * run, run)
        put.append(local.go(full.at[at(LEAD, {}, (col, run))], half_out.at[at(LEAD, {}, (b * run, run))]))
    finish(ring)
    gh_sum[...] = ring_result(z, gh, ups, downs).astype(BF16)
    put.append(local.go(gh_sum, gh_out))
    for c in put:
        c.wait()
    send.drain()


def finish_kernel(gf, gh, gi_out, go_out, gh_out, send_sem, recv_sem, local_sem, *landed):
    bits, to, z, nz = place()
    yhi = bits["YB"]
    h = nz // 2
    ups, downs = landed[:h], landed[h:]
    meet(to, ("pair", "up", "down"))
    send = Sender(send_sem, recv_sem, to)
    ring = ring_scatter(send, z, nz, gf, ups, downs)
    step(ring)
    cross = send.go(gh.at[1 - yhi], gh_out.at[yhi], "pair")
    kept = pltpu.make_async_copy(gh.at[yhi], gh_out.at[yhi], local_sem.at[0])
    kept.start()
    finish(ring)
    total = ring_result(z, gf, ups, downs)
    units = gi_out.shape[1]
    gi_out[...] = total[:, :units]
    go_out[...] = total[:, units:]
    cross.wait_recv()
    kept.wait()
    send.drain()


def stats_kernel(stats, out, near, far, held, send_sem, recv_sem):
    x, ylo, yhi, core = (lax.axis_index(n) for n in ("x", "ylo", "yhi", "core"))
    row = [
        {"x": lax.rem(x + i, 4), "core": lax.rem(core + c, 2)}
        for i in range(4) for c in range(2) if i or c
    ]
    column = [
        {"ylo": lax.rem(ylo + a, 2), "yhi": lax.rem(yhi + b, 2)}
        for a in range(2) for b in range(2) if a or b
    ]
    barrier = pltpu.get_barrier_semaphore()
    for d in row + column:
        pl.semaphore_signal(barrier, inc=1, device_id=d, device_id_type=MESH)
    pl.semaphore_wait(barrier, len(row) + len(column))

    def exchange(src, slots, peers, base):
        flying = []
        for i, d in enumerate(peers):
            c = pltpu.make_async_remote_copy(
                src_ref=src,
                dst_ref=slots.at[i],
                send_sem=send_sem.at[base + i],
                recv_sem=recv_sem.at[base + i],
                device_id=d,
                device_id_type=MESH,
            )
            c.start()
            flying.append(c)
        for c in flying:
            c.wait_recv()
        parts = [src[...]] + [slots[i] for i in range(len(peers))]
        tops = [p[0:2] for p in parts]
        top = functools.reduce(jnp.maximum, tops)
        total = functools.reduce(
            jnp.add, [p[2:4] * jnp.exp(t - top) for p, t in zip(parts, tops)]
        )
        return flying, top, total

    one, top, total = exchange(stats, near, row, 0)
    held[0:2] = top
    held[2:4] = total
    held[4:8] = jnp.zeros((4, held.shape[1]), F32)
    two, top, total = exchange(held, far, column, len(row))
    out[0:2] = top
    out[2:4] = total
    out[4:8] = jnp.zeros((4, out.shape[1]), F32)
    for c in one + two:
        c.wait_send()


VM = pl.BlockSpec(memory_space=pltpu.VMEM)
ANY = pl.BlockSpec(memory_space=pl.ANY)
SD = jax.ShapeDtypeStruct


def params(cid):
    return pltpu.CompilerParams(
        collective_id=cid, has_side_effects=True, vmem_limit_bytes=56 * 1024 * 1024
    )


def sems(remote, local):
    dma = pltpu.SemaphoreType.DMA
    return [dma((remote,)), dma((remote,)), dma((local,))]


def call_forward(feats, gain_in, w_in, w_out, gain, hw, buf, pos, toks):
    tok, width = feats.shape
    units = w_in.shape[1]
    _, rows, cols = hw.shape
    nz = lax.axis_size("z")
    tw = buf.shape[1]
    scratch = [
        pltpu.VMEM((tok, width), BF16),
        pltpu.VMEM((width, units), BF16),
        pltpu.VMEM((units, width), BF16),
        pltpu.VMEM(buf.shape, BF16),
        pltpu.VMEM(pos.shape, jnp.int32),
        pltpu.VMEM((tok, width), BF16),
        pltpu.VMEM((tok, units), F32),
        pltpu.VMEM(CUBE[1:] + (BLK, width), BF16),
        pltpu.VMEM(CUBE[2:] + (BLK, width), BF16),
        pltpu.VMEM(CUBE + (BLK, width), BF16),
        pltpu.VMEM((nz, 2, rows, cols), BF16),
        pltpu.VMEM((nz, tok, 2 * tw), BF16),
        pltpu.VMEM((nz, tok, 2 * tw), BF16),
    ]
    return pl.pallas_call(
        forward_kernel,
        out_shape=(
            SD(CUBE + (BLK, width), BF16),
            SD((nz, 2, rows, cols), BF16),
            SD((BLK, width), F32),
            SD((BLK, 128), F32),
            SD((2, tok, width // 2), BF16),
            SD((2, tok, units), F32),
            SD((nz, tok, 2 * tw), BF16),
            SD((2,) + toks.shape, jnp.int32),
        ),
        in_specs=[ANY, VM, ANY, ANY, VM, ANY, ANY, ANY, ANY],
        out_specs=(ANY, ANY, VM, VM, ANY, ANY, ANY, ANY),
        scratch_shapes=scratch + sems(96, 48) + landing(ICI3, width),
        compiler_params=params(1),
        cost_estimate=pl.CostEstimate(flops=10**10, bytes_accessed=10**8, transcendentals=0),
        name="forward_plane",
    )(feats, gain_in[None], w_in, w_out, gain[None], hw, buf, pos, toks)


def call_backward(part, resid, scale, gain, gh, run):
    width = resid.shape[1]
    nz, rows, cols = gh.shape
    ring = [pltpu.VMEM((rows, cols), BF16) for _ in range(nz)]
    return pl.pallas_call(
        functools.partial(backward_kernel, run),
        out_shape=(
            SD(CUBE + (BLK, width), BF16),
            SD(CUBE + (BLK, width // 2), BF16),
            SD((rows, cols), BF16),
        ),
        in_specs=[VM] * 5,
        out_specs=(ANY, ANY, ANY),
        scratch_shapes=[
            pltpu.VMEM((2,) * 4 + (BLK, width), BF16),
            pltpu.VMEM(CUBE + (BLK, width), BF16),
            pltpu.VMEM((rows, cols), BF16),
        ]
        + sems(80, 2 + width // run)
        + landing(ICI4, width)
        + ring,
        compiler_params=params(3),
        cost_estimate=pl.CostEstimate(flops=10**6, bytes_accessed=10**8, transcendentals=0),
        name="backward_plane",
    )(part.reshape(CUBE + (BLK, width)), resid, scale, gain[None], gh)


def call_finish(gf, gh):
    nz, rows, cols = gf.shape
    return pl.pallas_call(
        finish_kernel,
        out_shape=(SD((rows, cols // 2), F32), SD((rows, cols // 2), F32), SD(gh.shape, BF16)),
        in_specs=[VM, ANY],
        out_specs=(VM, VM, ANY),
        scratch_shapes=sems(24, 1) + [pltpu.VMEM((rows, cols), BF16) for _ in range(nz)],
        compiler_params=params(4),
        name="finish_ring",
    )(gf, gh)


def call_stats(stats):
    n = stats.shape[1]
    return pl.pallas_call(
        stats_kernel,
        out_shape=SD((8, n), F32),
        in_specs=[VM],
        out_specs=VM,
        scratch_shapes=[
            pltpu.VMEM((7, 8, n), F32),
            pltpu.VMEM((3, 8, n), F32),
            pltpu.VMEM((8, n), F32),
            pltpu.SemaphoreType.DMA((10,)),
            pltpu.SemaphoreType.DMA((10,)),
        ],
        compiler_params=params(2),
        name="softmax_stats",
    )(stats)


def body(
    features, token_ids, positions, target_buffer, norm_gain, final_gain, w_in, w_out, head_weight
):
    yhi = lax.axis_index("yhi")
    vocab = lax.axis_index(("ylo", "x", "core"))
    nz = lax.axis_size("z")
    backward = (((1,), (1,)), ((), ()))
    contract = (((0,), (0,)), ((), ()))
    rows, cols = head_weight.shape
    tok, width = features.shape
    units = w_in.shape[1]
    tw = target_buffer.shape[1]

    hw = head_weight.reshape(rows, nz, 2, tw).transpose(2, 0, 1, 3).reshape(2, rows, cols // 2)
    pos = positions.reshape(nz, 2, tok, 1)
    toks = jnp.zeros((8, 128), jnp.int32).at[: tok // 128].set(token_ids.reshape(tok // 128, 128))
    final, head, resid, scale, normed, pre, target, toks = call_forward(
        features, norm_gain, w_in, w_out, final_gain, hw, target_buffer, pos, toks
    )
    final = final.reshape(2 * tok, width)
    head = head.reshape(width, cols // 2)
    normed = normed.reshape(2 * tok, width // 2)
    pre = pre.reshape(2 * tok, units)
    target = target.reshape(nz, tok, 2, tw).transpose(2, 1, 0, 3).reshape(2 * tok, cols // 2)
    toks = toks[:, : tok // 128].reshape(2 * tok)

    logits = jnp.dot(final, head, preferred_element_type=F32)
    tfloat = target.astype(F32)
    top_q = jnp.max(logits, -1)
    top_p = jnp.max(tfloat, -1)
    qexp = jnp.exp(logits - top_q[:, None])
    pexp = jnp.exp(tfloat - top_p[:, None])
    zero = jnp.zeros_like(top_q)
    stats = jnp.stack([top_q, top_p, jnp.sum(qexp, -1), jnp.sum(pexp, -1), zero, zero, zero, zero])
    every = call_stats(stats)
    qprob = qexp * (jnp.exp(top_q - every[0]) / every[2])[:, None]
    pprob = pexp * (jnp.exp(top_p - every[1]) / every[3])[:, None]
    lane = jnp.arange(cols // 2, dtype=jnp.int32)
    columns_here = vocab * cols + (lane // tw) * (2 * tw) + yhi * tw + lane % tw
    onehot = (columns_here[None, :] == toks[:, None]).astype(F32)
    dlogits = (qprob - pprob + HARD * (qprob - onehot)).astype(BF16)

    gh = lax.dot_general(final, dlogits, contract, preferred_element_type=F32).astype(BF16)
    part = lax.dot_general(dlogits, head, backward, preferred_element_type=F32).astype(BF16)
    dresid, dresid_half, gh = call_backward(
        part, resid, scale, final_gain, gh.reshape(nz, 2 * rows, cols // 2), rows
    )
    dresid = dresid.reshape(2 * tok, width)
    dresid_half = dresid_half.reshape(2 * tok, width // 2)

    sig = jax.nn.sigmoid(pre)
    act = (pre * sig).astype(BF16)
    dact = lax.dot_general(dresid, w_out, backward, preferred_element_type=F32)
    dpre = (dact * sig * (1.0 + pre * (1.0 - sig))).astype(BF16)
    gf = jnp.concatenate(
        [
            lax.dot_general(normed, dpre, contract, preferred_element_type=F32),
            lax.dot_general(dresid_half, act, contract, preferred_element_type=F32),
        ],
        1,
    ).astype(BF16)
    gi, go, gh = call_finish(
        gf.reshape(nz, rows, 2 * units), gh.reshape(2, rows, cols // 2)
    )
    gh = gh.reshape(2, rows, nz, tw).transpose(1, 2, 0, 3).reshape(rows, cols).astype(F32)
    return (gh, gi, go.T)


def solution(mesh):
    names = ("ylo", "x", "core", "z", "yhi")
    fine = Mesh(mesh.devices.reshape(2, 4, 2, -1, 2), names)
    v = ("ylo", "x", "core")
    d = ("z", "yhi")
    return jax.shard_map(
        body,
        mesh=fine,
        in_specs=(
            P(d, None),
            P(d),
            P(),
            P(None, v + d),
            P(),
            P(),
            P(None, v),
            P(v, None),
            P(d, v),
        ),
        out_specs=(P(d, v), P(d, v), P(v, d)),
        check_vma=False,
    )
```

time: 273 us -> 279 us (1.022)
  Pallas kernels: 114 us -> 208 us
  waiting for transfers between devices: 60.4 us -> 0 us
  starting transfers between devices: 22.2 us -> 0 us
  between operations: 14.1 us -> 0.87 us
  local copies, waits for them, and re-layouts: 28 us -> 35.6 us
  other arithmetic: 9.79 us -> 6.2 us
    pallas_call x3 -> x4, Pallas kernels: 114 us -> 208 us  [the longest x1 97.2 us: call_forward(): pl.pallas_call(forward_kernel, out_shape=(SD(CUBE + (BLK, width), BF16),...]
    reduce_scatter x2 -> x0, waiting for transfers between devices: 48.8 us -> none  [the longest x1 48.8 us: body(): gf = scatter(gf).astype(f32)]
    ppermute x6 -> x0, starting transfers between devices: 13.5 us -> none  [the longest x1 3.83 us: body(): head_pair = swap(pick(hw, 2, 1 - yhi).reshape(rows, cols // 2))]
    gather x1 -> x0, local copies, waits for them, and re-layouts: 12.1 us -> none  [body(): ordered = target_buffer[positions].reshape(8, -1, tw)]
    ppermute x6 -> x0, waiting for transfers between devices: 11.5 us -> none  [the longest x1 6.54 us: body(): dpre2 = jnp.concatenate([dpre, swap(dpre)], 0)]
    all_to_all x1 -> x0, starting transfers between devices: 8.32 us -> none  [body(): lax.all_to_all(ordered, 'z', split_axis=0, concat_axis=2, tiled=True)[0]]
    another operation x0 -> x2, local copies, waits for them, and re-layouts: none -> 6.61 us
    dot_general x0 -> x2, local copies, waits for them, and re-layouts: none -> 6.43 us  [the longest x1 3.93 us: body(): lax.dot_general(dresid_half, act, contract, preferred_element_type=F32)]
  transfers between devices with their start and end apart: 10 -> 0, of which waited for: 3 -> 0; matrix products, arithmetic and copies ran while one was open for 15% -> 0% of each run, Pallas kernels for 38% -> 0%
where the time goes in v4:
time: 279 us; the launch traced here: 278 us
  Pallas kernels  208 us (75%)
  local copies, waits for them, and re-layouts  35.6 us (13%)
  matrix products  27.3 us (10%)
  other arithmetic  6.2 us (2%)
    pallas_call x1, Pallas kernels, call_forward(): pl.pallas_call(forward_kernel, out_shape=(SD(CUBE + (BLK, width), BF16),...  97.2 us
    pallas_call x1, Pallas kernels, call_backward(): pl.pallas_call(functools.partial(backward_kernel, run), out_shape=(SD(CUB...  61 us
    pallas_call x1, Pallas kernels, call_finish(): pl.pallas_call(finish_kernel, out_shape=(SD((rows, cols // 2), F32), SD((...  40.1 us
    unnamed x32, local copies, waits for them, and re-layouts  11.3 us
    pallas_call x1, Pallas kernels, call_stats(): pl.pallas_call(stats_kernel, out_shape=SD((8, n), F32), in_specs=[VM], ou...  9.9 us
    dot_general x1, matrix products, body(): lax.dot_general(normed, dpre, contract, preferred_element_type=F32)  8.55 us
    another operation x2, local copies, waits for them, and re-layouts  6.61 us
    dot_general x1, matrix products, body(): logits = jnp.dot(final, head, preferred_element_type=F32)  5.9 us

profile of v4, /device:TPU:1, one launch (start us, length us, event | category | flops | bytes accessed | tf_op | source)
XLA Modules:
  0.0 278.2 jit_solution(4196607007887083593)
XLA Ops:
  0.7 6.5 %copy.49.w_in = bf16[4096,448]{1,0:T(8,128)(2,1)} copy(bf16[4096,448]{0,1:T(8,128)(2,1)} %param.17) | data formatting | bytes 7340032 | tf_op args[6]
  7.2 3.3 %reshape.193.pos = s32[8,2,256,1]{3,2,1,0:T(8,128)} reshape(s32[4096]{0:T(1024)S(1)} %copy-done.7) | data formatting | bytes 32768 | tf_op jit(solution)/shard_map/reshape | solution.py:639
  10.7 1.0 copy.50.hw
  11.7 1.3 copy.51.buf
  13.6 97.2 %forward_plane.1 = (bf16[2,2,2,2,2,16,4096]{6,5,4,3,2,1,0:T(8,128)(2,1)}, bf16[8,2,256,512]{3,2,1,0:T(8,128)(2,1)}, f32[16,4096]{1,0:T(8,128)}, f32[16,128]{1,0:...) custom-call(bf16[256,4096]{1,0:T(8,128)(2,1)} %feats.1, ...), custom_call_target="tpu_custom_call" | custom-call | flops 10000000000 | bytes 100000000 | tf_op jit(solution)/shard_map/forward_plane/pallas_call | solution.py:545
  110.8 5.9 %fusion.18 = (f32[512]{0:T(512)S(1)}, f32[512,512]{0,1:T(8,128)S(1)}) fusion(bf16[512,4096]{1,0:T(8,128)(2,1)} %bitcast.108, bf16[4096,512]{1,0:T(8,128)(2,1)} %bitcast.106), kind=kOutput, calls=%fused_computation.37 | convolution fusion | flops 2147745280 | bytes 9439232 | tf_op jit(solution)/shard_map/dot_general | solution.py:651
  118.1 9.9 %softmax_stats.1 = f32[8,512]{1,0:T(8,128)} custom-call(f32[8,512]{1,0:T(8,128)} %stack.20.stats), custom_call_target="tpu_custom_call" | custom-call | tf_op jit(solution)/shard_map/softmax_stats/pallas_call | solution.py:608
  130.0 1.1 slice.35
  131.6 4.5 %convolution_convert_fusion = bf16[4096,512]{1,0:T(8,128)(2,1)} fusion(bf16[512,4096]{1,0:T(8,128)(2,1)S(1)} %bitcast.109, bf16[512,512]{0,1:T(8,128)(2,1)S(1)} %add_convert_fusion), kind=kOutput, calls=%fused_computation | convolution fusion | flops 2149580800 | bytes 8912896 | tf_op jit(solution)/shard_map/dot_general | solution.py:667
  136.0 4.4 %convolution_convert_fusion.1 = bf16[512,4096]{1,0:T(8,128)(2,1)} fusion(bf16[512,512]{0,1:T(8,128)(2,1)S(1)} %add_convert_fusion, bf16[4096,512]{1,0:T(8,128)(2,1)S(1)} %bitcast.107), kind=kOutput, calls=%fused_computation.1 | convolution fusion | flops 2149580800 | bytes 8912896 | tf_op jit(solution)/shard_map/dot_general | solution.py:668
  140.4 61.0 %backward_plane.1 = (bf16[2,2,2,2,2,16,4096]{6,5,4,3,2,1,0:T(8,128)(2,1)}, bf16[2,2,2,2,2,16,2048]{6,5,4,3,2,1,0:T(8,128)(2,1)}, bf16[512,512]{1,0:T(8,128)(2,1)}) custom-call(bf16[2,2,2,2,2,16,4096]{6,5,4,3,2,1,0:T(8,128)(2,1)} %bitcast.74, f32[16,4096]{1,0:T(8,128)} %get-tuple-element.34.resid, f32[16,128]{1,0:T(8,128)} %get-tuple-element.35.scale, ...), custom_call_target="tpu_custom_call" | custom-call | flops 1000000 | bytes 100000000 | tf_op jit(solution)/shard_map/backward_plane/pallas_call | solution.py:570
  201.5 1.2 copy.56
  202.7 2.5 copy.53
  205.2 8.6 %convolution_convert_fusion.3 = bf16[8,256,448]{1,2,0:T(8,128)(2,1)} fusion(bf16[8,256,512]{2,1,0:T(8,128)(2,1)} %bitcast.82, bf16[512,4096]{1,0:T(8,128)(2,1)} %bitcast.104, bf16[448,4096]{1,0:T(8,128)(2,1)} %w_out.1, f32[512,448]{0,1:T(8,128)} %copy.56), kind=kOutput, calls=%fused_computation.4 | convolution fusion | flops 2821554176 | bytes 12713984 | tf_op jit(solution)/shard_map/dot_general | solution.py:681
  213.8 2.8 %copy.60 = bf16[8,256,448]{2,1,0:T(8,128)(2,1)S(1)} copy(bf16[8,256,448]{1,2,0:T(8,128)(2,1)} %convolution_convert_fusion.3) | data formatting | bytes 3670016 | tf_op jit(solution)/shard_map/convert.25
  216.6 3.9 %copy.58 = bf16[2048,512]{1,0:T(8,128)(2,1)} copy(bf16[2048,512]{0,1:T(8,128)(2,1)} %bitcast.81) | data formatting | bytes 4194304 | tf_op jit(solution)/shard_map/dot_general | solution.py:682
  220.8 4.0 %convolution_convert_fusion.2 = bf16[8,256,448]{1,2,0:T(8,128)(2,1)} fusion(bf16[8,256,512]{2,1,0:T(8,128)(2,1)} %bitcast.83, bf16[512,448,1]{1,0,2:T(8,128)(2,1)S(1)} %bitcast.86), kind=kOutput, calls=%fused_computation.3 | convolution fusion | flops 940441600 | bytes 4390912 | tf_op jit(solution)/shard_map/dot_general | solution.py:682
  224.8 3.8 %copy.61 = bf16[8,256,448]{2,1,0:T(8,128)(2,1)} copy(bf16[8,256,448]{1,2,0:T(8,128)(2,1)} %convolution_convert_fusion.2) | data formatting | bytes 3670016 | tf_op jit(solution)/shard_map/convert.26
  228.6 4.8 %pad_maximum_fusion.gf = bf16[8,256,896]{2,1,0:T(8,128)(2,1)} fusion(bf16[8,256,448]{2,1,0:T(8,128)(2,1)} %copy.61, bf16[8,256,448]{2,1,0:T(8,128)(2,1)S(1)} %copy.60), kind=kLoop, calls=%fused_computation.2 | loop fusion | flops 7340032 | bytes 7340032 | tf_op jit(solution)/shard_map/concatenate | solution.py:679
  233.4 40.1 %finish_ring.1 = (f32[256,448]{1,0:T(8,128)}, f32[256,448]{1,0:T(8,128)}, bf16[2,256,512]{2,1,0:T(8,128)(2,1)}) custom-call(bf16[8,256,896]{2,1,0:T(8,128)(2,1)} %pad_maximum_fusion.gf, bf16[2,256,512]{2,1,0:T(8,128)(2,1)} %bitcast.88), custom_call_target="tpu_custom_call" | custom-call | tf_op jit(solution)/shard_map/finish_ring/pallas_call | solution.py:595
  273.6 1.3 copy.62
  275.0 1.3 copy.64
  276.3 1.0 copy.65
  277.3 1.0 copy.66
  (44 shorter events, 5.0 us)
Async XLA Ops:
  0.6 6.5 %copy-start.7 = (s32[4096]{0:T(1024)S(1)}, s32[4096]{0:T(1024)}, u32[]{:S(2)}) copy-start(s32[4096]{0:T(1024)} %param.13) | copy-start | bytes 49156
  0.6 9.8 %copy-start.3 = (bf16[256,1024]{1,0:T(8,128)(2,1)S(1)}, bf16[256,1024]{1,0:T(8,128)(2,1)}, u32[]{:S(2)}) copy-start(bf16[256,1024]{1,0:T(8,128)(2,1)} %param.19) | copy-start | bytes 1572868
  7.1 4.6 %copy-start.2 = (bf16[4096,64]{0,1:T(8,128)(2,1)S(1)}, bf16[4096,64]{0,1:T(8,128)(2,1)}, u32[]{:S(2)}) copy-start(bf16[4096,64]{0,1:T(8,128)(2,1)} %param.14) | copy-start | bytes 1572868
  7.2 5.9 %copy-start.8 = (s32[256]{0:T(256)S(1)}, s32[256]{0:T(256)}, u32[]{:S(2)}) copy-start(s32[256]{0:T(256)} %param.12) | copy-start | bytes 3076
  110.8 6.1 %copy-start.4 = (bf16[8,256,128]{2,1,0:T(8,128)(2,1)S(1)}, bf16[8,256,128]{2,1,0:T(8,128)(2,1)}, u32[]{:S(2)}) copy-start(bf16[8,256,128]{2,1,0:T(8,128)(2,1)} %get-tuple-element.32) | copy-start | bytes 1572868
  129.1 2.5 copy-start.10
  131.6 4.5 %copy-start.9 = (bf16[8,2,256,512]{3,2,1,0:T(8,128)(2,1)S(1)}, bf16[8,2,256,512]{3,2,1,0:T(8,128)(2,1)}, u32[]{:S(2)}) copy-start(bf16[8,2,256,512]{3,2,1,0:T(8,128)(2,1)} %get-tuple-element.31) | copy-start | bytes 12582916
  140.4 61.0 %copy-start = (f32[2,256,448]{2,1,0:T(8,128)S(1)}, f32[2,256,448]{2,1,0:T(8,128)}, u32[]{:S(2)}) copy-start(f32[2,256,448]{2,1,0:T(8,128)} %get-tuple-element.37) | copy-start | bytes 2752516
  140.4 62.3 %copy-start.1 = (bf16[2,256,2048]{2,1,0:T(8,128)(2,1)S(1)}, bf16[2,256,2048]{2,1,0:T(8,128)(2,1)}, u32[]{:S(2)}) copy-start(bf16[2,256,2048]{2,1,0:T(8,128)(2,1)} %get-tuple-element.29) | copy-start | bytes 6291460
  273.5 2.8 copy-start.6
  273.5 3.7 %copy-start.5 = (f32[256,448]{1,0:T(8,128)S(1)}, f32[256,448]{1,0:T(8,128)}, u32[]{:S(2)}) copy-start(f32[256,448]{1,0:T(8,128)} %get-tuple-element.42) | copy-start | bytes 1376260

commit v5 on v4

v5 whole, which is shorter than its diff:
```python
import functools
import jax
import jax.numpy as jnp
from jax import lax
from jax.experimental import pallas as pl
from jax.experimental.pallas import tpu as pltpu
from jax.sharding import Mesh, PartitionSpec as P

EPS = 1e-05
HARD = 0.5
MESH = pl.DeviceIdType.MESH
LEAD = ("YB", "core", "XA", "YA", "XB")
REST = ("YB", "XA", "YA", "XB")
ICI3 = ("XA", "YA", "XB")
ICI4 = ("XA", "YA", "XB", "YB")
CUBE = (2,) * 5
BLK = 16
F32 = jnp.float32
BF16 = jnp.bfloat16


SCHED = ((1, 2, 4), (1, 2, 3), (0, 2, 4, 5), (0, 1, 2, 3))


def place():
    x, ylo, yhi, core, z = (lax.axis_index(n) for n in ("x", "ylo", "yhi", "core", "z"))
    nz = lax.axis_size("z")
    y = 2 * yhi + ylo
    odd = lax.rem(x, 2)
    bits = {
        "core": core,
        "XA": lax.rem(lax.div(x + 1, 2), 2),
        "XB": lax.div(x, 2),
        "YA": lax.rem(lax.div(y + 1, 2), 2),
        "YB": yhi,
    }
    to = {
        "core": {"core": 1 - core},
        "XA": {"x": x + 1 - 2 * odd},
        "XB": {"x": lax.rem(x + 3 + 2 * odd, 4)},
        "YA": {"ylo": 1 - ylo},
        "YB": {"ylo": 1 - ylo, "yhi": 1 - yhi},
        "pair": {"yhi": 1 - yhi},
        "up": {"z": lax.rem(z + 1, nz)},
        "down": {"z": lax.rem(z + nz - 1, nz)},
    }
    for i in range(1, nz):
        to[i] = {"z": lax.rem(z + i, nz)}
    for i in range(4):
        for c in range(2):
            to["row", i, c] = {"x": lax.rem(x + i, 4), "core": lax.rem(core + c, 2)}
    for a in range(2):
        for b in range(2):
            to["col", a, b] = {"ylo": lax.rem(ylo + a, 2), "yhi": lax.rem(yhi + b, 2)}
    return bits, to, z, nz


def at(names, fixed, cols=None):
    where = tuple(fixed.get(n, slice(None)) for n in names)
    return where + (slice(None), slice(None) if cols is None else pl.ds(*cols))


def corners(names):
    out = [{}]
    for n in names:
        out = [dict(o, **{n: v}) for o in out for v in (0, 1)]
    return out


class Sender:
    def __init__(self, send_sem, recv_sem, to):
        self.send_sem, self.recv_sem, self.to = send_sem, recv_sem, to
        self.all = []

    def go(self, src, dst, dim):
        n = len(self.all)
        c = pltpu.make_async_remote_copy(
            src_ref=src,
            dst_ref=dst,
            send_sem=self.send_sem.at[n],
            recv_sem=self.recv_sem.at[n],
            device_id=self.to[dim],
            device_id_type=MESH,
        )
        c.start()
        self.all.append(c)
        return c

    def drain(self):
        for c in self.all:
            c.wait_send()


class Local:
    def __init__(self, sem):
        self.sem = sem
        self.n = 0

    def go(self, src, dst):
        c = pltpu.make_async_copy(src, dst, self.sem.at[self.n])
        c.start()
        self.n += 1
        return c


def colours(n, width):
    tiles = width // 128
    edges = [128 * (tiles * k // n) for k in range(n + 1)]
    return [(edges[k], edges[k + 1] - edges[k]) for k in range(n)]


def greet(to, dims):
    barrier = pltpu.get_barrier_semaphore()
    for d in dims:
        pl.semaphore_signal(barrier, inc=1, device_id=to[d], device_id_type=MESH)
    return lambda: pl.semaphore_wait(barrier, len(dims))


def meet(to, dims):
    greet(to, dims)()


def step(thread):
    return next(thread, None)


def finish(thread):
    for _ in thread:
        pass


def reduce_cube(send, bits, names, dims, width, part, total, landed):
    rest = tuple(n for n in names if n != "core")
    n = len(dims)
    cuts = colours(n, width)
    first, second = [], []
    for keep, held in ((1, first), (0, second)):
        for k in range(n):
            d = dims[k]
            bit = 1 - bits[d] if keep else bits[d]
            src = part.at[at(names, {"core": 1 - bits["core"], d: bit}, cuts[k])]
            dst = total.at[at(rest, {d: bit}, cuts[k])]
            held.append(send.go(src, dst, "core"))

    def merge(k, bit):
        d = dims[k]
        for f in corners([m for m in rest if m != d]):
            f = dict(f, **{d: bit})
            w = at(rest, f, cuts[k])
            total[w] = total[w] + part[at(names, dict(f, core=bits["core"]), cuts[k])]

    def start(k, j):
        d = dims[(k + j) % n]
        fixed = {dims[(k + i) % n]: bits[dims[(k + i) % n]] for i in range(j)}
        fixed[d] = 1 - bits[d]
        return send.go(total.at[at(rest, fixed, cuts[k])], landed[k * n + j], d)

    yield
    flying = []
    for k in range(n):
        first[k].wait_recv()
        merge(k, 1 - bits[dims[k]])
        flying.append(start(k, 0))
    yield
    for k in range(n):
        second[k].wait_recv()
        merge(k, bits[dims[k]])
    for j in range(n):
        yield
        for k in range(n):
            flying[k].wait_recv()
            done = [dims[(k + i) % n] for i in range(j + 1)]
            fixed = {m: bits[m] for m in done}
            left = [m for m in rest if m not in done]
            for f in corners(left):
                w = at(rest, dict(f, **fixed), cuts[k])
                total[w] = total[w] + landed[k * n + j][tuple(f[m] for m in left)]
            if j + 1 < n:
                flying[k] = start(k, j + 1)


def gather_cube(send, bits, dims, width, full, names=LEAD):
    n = len(dims)
    cuts = colours(n, width)
    arriving = []
    for j in range(n):
        flying = []
        for k in range(n):
            d = dims[(k + j) % n]
            done = [dims[(k + i) % n] for i in range(j)]
            piece = full.at[at(names, {m: bits[m] for m in names if m not in done}, cuts[k])]
            flying.append(send.go(piece, piece, d))
        if j == 0:
            arriving.append(send.go(full.at[at(names, bits)], full.at[at(names, bits)], "core"))
        yield
        for k in range(n):
            flying[k].wait_recv()
            d = dims[(k + j) % n]
            done = [dims[(k + i) % n] for i in range(j)]
            fixed = {m: bits[m] for m in names if m not in done}
            fixed[d] = 1 - bits[d]
            piece = full.at[at(names, fixed, cuts[k])]
            arriving.append(send.go(piece, piece, "core"))
    for c in arriving:
        c.wait_recv()


def ring_gather(send, z, nz, slots, full, late):
    half = nz // 2

    def block(i, q):
        return full.at[lax.rem(z + nz + i, nz), slots[q]]

    ups, downs = [None, None], [None, None]
    for q in range(2):
        if q:
            late.wait_recv()
        if half > 1 or q == 0:
            ups[q] = send.go(block(0, q), block(0, q), "up")
        if half > 1 or q == 1:
            downs[q] = send.go(block(0, q), block(0, q), "down")
        yield
    for s in range(1, half + 1):
        for q in range(2):
            if s < half or q == 0:
                ups[q].wait_recv()
                if s + 1 < half or (s + 1 == half and q == 0):
                    ups[q] = send.go(block(-s, q), block(-s, q), "up")
            if s < half or q == 1:
                downs[q].wait_recv()
                if s + 1 < half or (s + 1 == half and q == 1):
                    downs[q] = send.go(block(s, q), block(s, q), "down")
            yield


def ring_scatter(send, z, nz, part, ups, downs, prepare):
    half = nz // 2
    rows = part.shape[1] // 2
    cut = [pl.ds(0, rows), pl.ds(rows, rows)]

    def block(i):
        return lax.rem(z + nz + i, nz)

    def mine(i, q):
        return part.at[block(i), cut[q]]

    flying = {}
    ways = (("up", ups, 1), ("down", downs, -1))
    prepare(block(half))
    for way, landed, sign in ways:
        q = 0 if way == "up" else 1
        flying[way, 0, q] = send.go(mine(sign * half, q), landed[0].at[cut[q]], way)
    if half > 1:
        for way, landed, sign in ways:
            q = 1 if way == "up" else 0
            prepare(block(sign * (half - 1)))
            flying[way, 1, q] = send.go(mine(sign * (half - 1), q), landed[1].at[cut[q]], way)
    yield
    for s in range(half):
        if half - 1 - s > 0 and s > 0:
            prepare(block(half - 1 - s))
            prepare(block(s + 1 - half))
        elif s == half - 1:
            prepare(block(0))
        for lead in (1, 0) if s else (0,):
            for way, landed, sign in ways:
                q = lead if way == "up" else 1 - lead
                flying[way, s, q].wait_recv()
                if s + 1 < half:
                    ref = landed[s].at[cut[q]]
                    ref[...] = ref[...] + mine(sign * (half - 1 - s), q)[...]
                    flying[way, s + 1, q] = send.go(ref, landed[s + 1].at[cut[q]], way)
            yield


def ring_result(z, part, ups, downs):
    own = part[z].astype(F32)
    if len(ups) > 1:
        return own + ups[-1][...].astype(F32) + downs[-1][...].astype(F32)
    rows = part.shape[1] // 2
    return own + jnp.concatenate([ups[0][:rows], downs[0][rows:]], 0).astype(F32)


def landing(dims, width):
    n = len(dims)
    cuts = colours(n, width)
    return [
        pltpu.VMEM((2,) * (n - 1 - j) + (BLK, cuts[k][1]), BF16) for k in range(n) for j in range(n)
    ]


def forward_kernel(
    feats, gain_in, w_in, w_out, gain, hw, buf, pos, toks,
    final_out, head_out, resid_out, scale_out, normed_out, pre_out, target_out, toks_out,
    fv, w1, w2, bv, bn, normed, other, pre, part, total, full, head, ordered, target,
    send_sem, recv_sem, local_sem, *landed,
):
    bits, to, z, nz = place()
    yhi = bits["YB"]
    tok, width = fv.shape
    run = head.shape[2]
    names = LEAD[1:]
    greeted = greet(to, LEAD + ("pair", "up", "down") + tuple(range(2, nz - 1)))
    local = Local(local_sem)
    got_f = local.go(feats, fv)
    got_head = local.go(hw.at[yhi], head.at[z, yhi])
    got_w1 = local.go(w_in, w1)
    got_w2 = local.go(w_out, w2)
    got_b = local.go(buf, bv)
    got_f.wait()
    chunk = 64

    def norm_rows(i, _):
        rows = pl.ds(pl.multiple_of(i * chunk, chunk), chunk)
        x = fv[rows, :].astype(F32)
        r = lax.rsqrt(jnp.mean(x * x, -1, keepdims=True) + EPS)
        normed[rows, :] = (x * r * gain_in[...]).astype(BF16)
        return 0

    lax.fori_loop(0, tok // chunk, norm_rows, 0)
    greeted()
    send = Sender(send_sem, recv_sem, to)
    late = send.go(hw.at[1 - yhi], head.at[z, yhi], "pair")
    got_head.wait()
    ring = ring_gather(send, z, nz, (yhi, 1 - yhi), head, late)
    step(ring)
    swapped = [send.go(toks, toks_out.at[yhi], "pair")]
    kept = [local.go(toks, toks_out.at[yhi])]
    mine = pl.ds(pl.multiple_of(own_row(bits), BLK), BLK)
    crossed = send.go(normed.at[mine], other.at[at(names, bits)], "YB")

    def project(rows):
        deep = width // 4
        for c in range(4):
            k = pl.ds(c * deep, deep)
            prod = lax.dot_general(
                rows[:, k], w1[:, k], (((1,), (1,)), ((), ())), preferred_element_type=F32
            )
            pre[...] = prod if c == 0 else pre[...] + prod

    got_w1.wait()
    project(normed)
    pre_out[yhi] = pre[...]
    step(ring)
    v = pre[...]
    act = (v * jax.nn.sigmoid(v)).astype(BF16)
    got_w2.wait()
    wide = width // 8
    for c in range(8):
        cols = (c * wide, wide)
        block = jnp.dot(act, w2[:, pl.ds(*cols)], preferred_element_type=F32).astype(BF16)
        for i, f in enumerate(corners(names)):
            part[at(names, f, cols)] = block[i * BLK : (i + 1) * BLK]

    got_b.wait()
    n_buf = bv.shape[1]
    piece = 1024 if n_buf % 1024 == 0 else n_buf
    pos_t = pos[...].T

    def ordered_rows(i):
        dest = lax.rem(z + i, nz)
        lane = lax.broadcasted_iota(jnp.int32, pos_t.shape, 1)
        there = [
            jnp.sum(jnp.where(lane == 2 * dest + h, pos_t, 0.0), 1, keepdims=True) for h in range(2)
        ]
        cols = lax.broadcasted_iota(jnp.int32, (tok, piece), 1).astype(F32)

        def inner(t, sums):
            rows = bn[pl.ds(pl.multiple_of(t * piece, piece), piece), :]
            out = []
            for h in range(2):
                hot = jnp.where(there[h] - (t * piece).astype(F32) == cols, 1.0, 0.0).astype(BF16)
                out.append(sums[h] + jnp.dot(hot, rows, preferred_element_type=F32))
            return tuple(out)

        zero = jnp.zeros((tok, bv.shape[0]), F32)
        a, b = lax.fori_loop(0, n_buf // piece, inner, (zero, zero))
        return jnp.concatenate([a, b], 1).astype(BF16)

    def gather_target():
        for i in range(1, nz):
            ordered[i] = ordered_rows(i)
            way = "up" if i == 1 else "down" if i == nz - 1 else i
            swapped.append(send.go(ordered.at[i], target.at[z], way))
            yield
        target[z] = ordered_rows(0)
        yield

    def gather_other():
        crossed.wait_recv()
        yield from gather_cube(send, bits, ICI3, width, other, names)

    side = gather_target()
    cross = gather_other()
    for i, _ in enumerate(reduce_cube(send, bits, names, ICI3, width, part, total, landed)):
        if i == 0:
            bn[...] = bv[...].T
        step(side)
        if i in SCHED[0]:
            step(ring)
        if i >= 1:
            step(cross)
    hidden = total[at(ICI3, bits)].astype(F32)
    resid = fv[mine, :].astype(F32) + hidden
    rscale = lax.rsqrt(jnp.mean(resid * resid, -1, keepdims=True) + EPS)
    resid_out[...] = resid
    scale_out[...] = jnp.broadcast_to(rscale, scale_out.shape)
    full[at(LEAD, bits)] = (resid * rscale * gain[...]).astype(BF16)
    for i, _ in enumerate(gather_cube(send, bits, ICI4, width, full)):
        step(side)
        if i in SCHED[1]:
            step(ring)
    put = [local.go(full, final_out)]
    finish(side)
    step(ring)
    finish(cross)
    for i, f in enumerate(corners(names)):
        fv[i * BLK : (i + 1) * BLK, :] = other[at(names, f)]
    for src, slot in ((normed, yhi), (fv, 1 - yhi)):
        for b in range(width // (2 * run)):
            here = pl.ds(pl.multiple_of((2 * b + yhi) * run, run), run)
            put.append(local.go(src.at[:, here], normed_out.at[slot, :, pl.ds(b * run, run)]))
    project(fv)
    pre_out[1 - yhi] = pre[...]
    finish(ring)
    put.append(local.go(head, head_out))
    for c in swapped:
        c.wait_recv()
    put.append(local.go(target, target_out))
    for c in kept + put:
        c.wait()
    send.drain()


def own_row(bits):
    r = bits["core"]
    for n in ("XA", "YA", "XB"):
        r = 2 * r + bits[n]
    return r * BLK


def exchange_stats(send, own, near, held, far, out):
    def merge(src, slots, peers, dst):
        flying = [send.go(src, slots.at[i], p) for i, p in enumerate(peers)]
        for c in flying:
            c.wait_recv()
        parts = [src[...]] + [slots[i] for i in range(len(peers))]
        tops = [p[0:2] for p in parts]
        top = functools.reduce(jnp.maximum, tops)
        total = functools.reduce(
            jnp.add, [p[2:4] * jnp.exp(t - top) for p, t in zip(parts, tops)]
        )
        dst[0:2] = top
        dst[2:4] = total

    held[4:8] = jnp.zeros((4, held.shape[1]), F32)
    merge(own, near, [("row", i, c) for i in range(4) for c in range(2) if i or c], held)
    merge(held, far, [("col", a, b) for a in range(2) for b in range(2) if a or b], out)


NT = (((1,), (1,)), ((), ()))
TN = (((0,), (0,)), ((), ()))


def backward_kernel(
    run, first_col, final, head, target, w_out, normed, pre, toks, resid, scale, gain,
    gh_out, gi_out, go_out,
    fin, hv, tv, w2, nv, pexp, lg, own, near, held, far, back, dl, part, total, full,
    ghp, ghs, ghx, ghv, gfp, da, act, dpre,
    send_sem, recv_sem, local_sem, *landed,
):
    bits, to, z, nz = place()
    yhi = bits["YB"]
    n_tok, width = fin.shape
    n_col = hv.shape[1]
    units = w2.shape[0]
    tok, tw = tv.shape[1], tv.shape[2] // 2
    h = nz // 2
    rings, landed = landed[: 4 * h], landed[4 * h :]
    peers = [("row", i, c) for i in range(4) for c in range(2) if i or c]
    peers += [("col", a, b) for a in range(2) for b in range(2) if a or b]
    greeted = greet(to, peers + ["up", "down"])
    local = Local(local_sem)
    got_t = local.go(target, tv)
    got_fin = local.go(final, fin)
    got_hv = local.go(head, hv)
    got_w2 = local.go(w_out, w2)
    got_nv = local.go(normed, nv)
    send = Sender(send_sem, recv_sem, to)

    got_t.wait()
    for k in range(nz // 2):
        for s in range(2):
            lanes = slice(s * tw, (s + 1) * tw)
            two = [tv[2 * k + i].astype(F32)[:, lanes] for i in range(2)]
            pexp[s * tok : (s + 1) * tok, k * 2 * tw : (k + 1) * 2 * tw] = jnp.concatenate(two, 1)
    t = pexp[...]
    top_p = jnp.max(t, -1, keepdims=True)
    t = jnp.exp(t - top_p)
    pexp[...] = t
    sum_p = jnp.sum(t, -1, keepdims=True)

    got_fin.wait()
    got_hv.wait()
    deep = width // 4
    for c in range(4):
        k = pl.ds(c * deep, deep)
        prod = jnp.dot(fin[:, k], hv[k, :], preferred_element_type=F32)
        lg[...] = prod if c == 0 else lg[...] + prod
    t = lg[...]
    top_q = jnp.max(t, -1, keepdims=True)
    t = jnp.exp(t - top_q)
    lg[...] = t
    sum_q = jnp.sum(t, -1, keepdims=True)
    lane = lax.broadcasted_iota(jnp.int32, (n_tok, 128), 1)
    columns = jnp.where(
        lane == 0, top_q, jnp.where(lane == 1, top_p, jnp.where(lane == 2, sum_q, sum_p))
    )
    own[...] = columns.T[0:8]
    greeted()
    back[...] = jnp.zeros(back.shape, F32)
    back[8:16] = toks[...]
    exchange_stats(send, own, near, held, far, back)
    columns = back[...].T
    all_q, all_p, tot_q, tot_p, token = (columns[:, i : i + 1] for i in (0, 1, 2, 3, 8))
    q = lg[...] * (jnp.exp(top_q - all_q) / tot_q)
    p = pexp[...] * (jnp.exp(top_p - all_p) / tot_p)
    lane = lax.broadcasted_iota(jnp.int32, (n_tok, n_col), 1)
    shift = tw.bit_length() - 1
    here = first_col() + lane + jnp.left_shift(jnp.right_shift(lane, shift), shift)
    onehot = jnp.where(token.astype(jnp.int32) == here, 1.0, 0.0)
    dl[...] = (q - p + HARD * (q - onehot)).astype(BF16)

    wide = width // 8
    for c in range(8):
        cols = (c * wide, wide)
        block = lax.dot_general(
            dl[...], hv[pl.ds(*cols), :], NT, preferred_element_type=F32
        ).astype(BF16)
        for i, f in enumerate(corners(LEAD)):
            part[at(LEAD, f, cols)] = block[i * BLK : (i + 1) * BLK]

    def make_gh(b):
        cols = pl.ds(pl.multiple_of(b * 2 * run, 2 * run), 2 * run)
        ghp[b] = lax.dot_general(dl[...], fin[:, cols], TN, preferred_element_type=F32).astype(BF16)

    ring = ring_scatter(send, z, nz, ghp, rings[:h], rings[h : 2 * h], make_gh)
    for i, _ in enumerate(reduce_cube(send, bits, LEAD, ICI4, width, part, total, landed)):
        if i in SCHED[2]:
            step(ring)
    dfinal = total[at(REST, bits)].astype(F32)
    r = resid[...]
    rscale = scale[...][:, :1]
    scaled = dfinal * gain[...]
    inner = jnp.sum(scaled * r, -1, keepdims=True)
    full[at(LEAD, bits)] = (rscale * scaled - r * (rscale * rscale * rscale / width * inner)).astype(
        BF16
    )
    for i, _ in enumerate(gather_cube(send, bits, ICI4, width, full)):
        if i in SCHED[3]:
            step(ring)

    def dresid(start, size):
        return full[at(LEAD, {}, (start, size))].reshape(n_tok, size)

    got_w2.wait()
    for c in range(4):
        k = pl.ds(c * deep, deep)
        prod = lax.dot_general(dresid(c * deep, deep), w2[:, k], NT, preferred_element_type=F32)
        da[...] = prod if c == 0 else da[...] + prod
    v = pre[...]
    sig = jax.nn.sigmoid(v)
    act[...] = (v * sig).astype(BF16)
    dpre[...] = (da[...] * sig * (1.0 + v * (1.0 - sig))).astype(BF16)
    got_nv.wait()

    def make_gf(b):
        cols = pl.ds(pl.multiple_of(b * run, run), run)
        gfp[b, 0:units] = lax.dot_general(
            dpre[...], nv[:, cols], TN, preferred_element_type=F32
        ).astype(BF16)
        there = pl.multiple_of((2 * b + yhi) * run, run)
        gfp[b, units:] = lax.dot_general(
            act[...], dresid(there, run), TN, preferred_element_type=F32
        ).astype(BF16)

    last = ring_scatter(send, z, nz, gfp, rings[2 * h : 3 * h], rings[3 * h :], make_gf)
    step(last)
    finish(ring)
    ghs[...] = ring_result(z, ghp, rings[:h], rings[h : 2 * h]).astype(BF16)
    halves = [pl.ds(pl.multiple_of(i * run, run), run) for i in (yhi, 1 - yhi)]
    crossed = send.go(ghs.at[:, halves[1]], ghx, ("col", 0, 1))
    step(last)
    step(last)
    step(last)
    crossed.wait_recv()
    for k in range(nz):
        src = slice(k * tw, (k + 1) * tw)
        for value, half in ((ghs[src, halves[0]], yhi), (ghx[src, :], 1 - yhi)):
            ghv[pl.ds(pl.multiple_of(k * 2 * tw + half * tw, tw), tw), :] = value.astype(F32)
    gh_out[...] = ghv[...].T
    finish(last)
    result = ring_result(z, gfp, rings[2 * h : 3 * h], rings[3 * h :])
    gi_out[...] = result[:units]
    go_out[...] = result[units:]
    send.drain()


VM = pl.BlockSpec(memory_space=pltpu.VMEM)
ANY = pl.BlockSpec(memory_space=pl.ANY)
SD = jax.ShapeDtypeStruct


def params(cid):
    return pltpu.CompilerParams(
        collective_id=cid, has_side_effects=True, vmem_limit_bytes=56 * 1024 * 1024
    )


def sems(remote, local):
    dma = pltpu.SemaphoreType.DMA
    return [dma((remote,)), dma((remote,)), dma((local,))]


def call_forward(feats, gain_in, w_in, w_out, gain, hw, buf, pos, toks):
    tok, width = feats.shape
    units = w_in.shape[0]
    _, rows, cols = hw.shape
    nz = lax.axis_size("z")
    tw = buf.shape[0]
    scratch = [
        pltpu.VMEM((tok, width), BF16),
        pltpu.VMEM(w_in.shape, BF16),
        pltpu.VMEM((units, width), BF16),
        pltpu.VMEM(buf.shape, BF16),
        pltpu.VMEM(buf.shape[::-1], BF16),
        pltpu.VMEM((tok, width), BF16),
        pltpu.VMEM(CUBE[1:] + (BLK, width), BF16),
        pltpu.VMEM((tok, units), F32),
        pltpu.VMEM(CUBE[1:] + (BLK, width), BF16),
        pltpu.VMEM(CUBE[2:] + (BLK, width), BF16),
        pltpu.VMEM(CUBE + (BLK, width), BF16),
        pltpu.VMEM((nz, 2, rows, cols), BF16),
        pltpu.VMEM((nz, tok, 2 * tw), BF16),
        pltpu.VMEM((nz, tok, 2 * tw), BF16),
    ]
    return pl.pallas_call(
        forward_kernel,
        out_shape=(
            SD(CUBE + (BLK, width), BF16),
            SD((nz, 2, rows, cols), BF16),
            SD((BLK, width), F32),
            SD((BLK, 128), F32),
            SD((2, tok, width // 2), BF16),
            SD((2, tok, units), F32),
            SD((nz, tok, 2 * tw), BF16),
            SD((2,) + toks.shape, jnp.int32),
        ),
        in_specs=[ANY, VM, ANY, ANY, VM, ANY, ANY, VM, ANY],
        out_specs=(ANY, ANY, VM, VM, ANY, VM, ANY, ANY),
        scratch_shapes=scratch + sems(96, 48) + landing(ICI3, width),
        compiler_params=params(1),
        cost_estimate=pl.CostEstimate(flops=10**10, bytes_accessed=10**8, transcendentals=0),
        name="forward_plane",
    )(feats, gain_in[None], w_in, w_out, gain[None], hw, buf, pos, toks)


def call_backward(first_col, final, head, target, w_out, normed, pre, toks, resid, scale, gain, run):
    n_tok, width = final.shape
    n_col = head.shape[1]
    units = w_out.shape[0]
    nz = lax.axis_size("z")
    vm = pltpu.VMEM
    scratch = [
        vm((n_tok, width), BF16),
        vm((width, n_col), BF16),
        vm(target.shape, BF16),
        vm(w_out.shape, BF16),
        vm(normed.shape, BF16),
        vm((n_tok, n_col), F32),
        vm((n_tok, n_col), F32),
        vm((8, n_tok), F32),
        vm((7, 8, n_tok), F32),
        vm((8, n_tok), F32),
        vm((3, 8, n_tok), F32),
        vm((128, n_tok), F32),
        vm((n_tok, n_col), BF16),
        vm(CUBE + (BLK, width), BF16),
        vm((2,) * 4 + (BLK, width), BF16),
        vm(CUBE + (BLK, width), BF16),
        vm((nz, n_col, 2 * run), BF16),
        vm((n_col, 2 * run), BF16),
        vm((n_col, run), BF16),
        vm((2 * n_col, run), F32),
        vm((nz, 2 * units, run), BF16),
        vm((n_tok, units), F32),
        vm((n_tok, units), BF16),
        vm((n_tok, units), BF16),
    ]
    rings = [vm((n_col, 2 * run), BF16) for _ in range(nz)]
    rings += [vm((2 * units, run), BF16) for _ in range(nz)]
    return pl.pallas_call(
        functools.partial(backward_kernel, run, first_col),
        out_shape=(SD((run, 2 * n_col), F32), SD((units, run), F32), SD((units, run), F32)),
        in_specs=[ANY] * 5 + [VM] * 5,
        out_specs=(VM, VM, VM),
        scratch_shapes=scratch + sems(120, 8) + rings + landing(ICI4, width),
        compiler_params=params(3),
        cost_estimate=pl.CostEstimate(flops=10**10, bytes_accessed=10**8, transcendentals=0),
        name="backward_plane",
    )(final, head, target, w_out, normed, pre, toks, resid, scale, gain[None])


def body(
    features, token_ids, positions, target_buffer, norm_gain, final_gain, w_in, w_out, head_weight
):
    nz = lax.axis_size("z")
    rows, cols = head_weight.shape
    tok, width = features.shape
    units = w_in.shape[1]
    tw = target_buffer.shape[1]

    hw = head_weight.reshape(rows, nz, 2, tw).transpose(2, 0, 1, 3).reshape(2, rows, cols // 2)
    pos = jnp.zeros((128, tok), F32).at[: 2 * nz].set(positions.reshape(2 * nz, tok).astype(F32))
    toks = jnp.zeros((8, 128), jnp.int32).at[: tok // 128].set(token_ids.reshape(tok // 128, 128))
    final, head, resid, scale, normed, pre, target, toks = call_forward(
        features, norm_gain, w_in.T, w_out, final_gain, hw, target_buffer.T, pos, toks
    )
    tokens = jnp.zeros((8, 2 * tok), F32).at[0].set(
        toks[:, : tok // 128].reshape(2 * tok).astype(F32)
    )

    def first_col():
        block = (lax.axis_index("ylo") * 4 + lax.axis_index("x")) * 2 + lax.axis_index("core")
        return block * cols + lax.axis_index("yhi") * tw

    gh, gi, go = call_backward(
        first_col,
        final.reshape(2 * tok, width),
        head.reshape(width, cols // 2),
        target,
        w_out,
        normed.reshape(2 * tok, width // 2),
        pre.reshape(2 * tok, units),
        tokens,
        resid,
        scale,
        final_gain,
        rows,
    )
    return (gh, gi.T, go)


def solution(mesh):
    names = ("ylo", "x", "core", "z", "yhi")
    fine = Mesh(mesh.devices.reshape(2, 4, 2, -1, 2), names)
    v = ("ylo", "x", "core")
    d = ("z", "yhi")
    return jax.shard_map(
        body,
        mesh=fine,
        in_specs=(
            P(d, None),
            P(d),
            P(),
            P(None, v + d),
            P(),
            P(),
            P(None, v),
            P(v, None),
            P(d, v),
        ),
        out_specs=(P(d, v), P(d, v), P(v, d)),
        check_vma=False,
    )
```

time: 279 us -> 193 us (0.69)
  Pallas kernels: 208 us -> 179 us
  matrix products: 27.3 us -> 0 us
  local copies, waits for them, and re-layouts: 35.6 us -> 10.8 us
  other arithmetic: 6.2 us -> 1.42 us
    dot_general x5 -> x0, matrix products: 27.3 us -> none  [the longest x1 8.55 us: body(): lax.dot_general(normed, dpre, contract, preferred_element_type=F32)]
    pallas_call x1, Pallas kernels: 97.2 us -> 72.3 us  [call_forward(): pl.pallas_call(forward_kernel, out_shape=(SD(CUBE + (BLK, width), BF16),...]
    another operation x4 -> x0, local copies, waits for them, and re-layouts: 7.25 us -> none
    dot_general x2 -> x0, local copies, waits for them, and re-layouts: 6.43 us -> none  [the longest x1 3.93 us: body(): lax.dot_general(dresid_half, act, contract, preferred_element_type=F32)]
    concatenate x1 -> x0, other arithmetic: 4.77 us -> none  [body(): jnp.concatenate([lax.dot_general(normed, dpre, contract, preferred_elemen...]
    reshape x2 -> x0, local copies, waits for them, and re-layouts: 4.51 us -> none  [the longest x1 3.27 us: body(): pos = positions.reshape(nz, 2, tok, 1)]
    unnamed x32 -> x4, local copies, waits for them, and re-layouts: 11.3 us -> 7.18 us
    pallas_call x3 -> x1, Pallas kernels: 111 us -> 107 us  [call_backward(): pl.pallas_call(functools.partial(backward_kernel, run, first_col), out_sh...]
where the time goes in v5:
time: 193 us; the launch traced here: 192 us
  Pallas kernels  179 us (93%)
  local copies, waits for them, and re-layouts  10.8 us (6%)
    pallas_call x1, Pallas kernels, call_backward(): pl.pallas_call(functools.partial(backward_kernel, run, first_col), out_sh...  107 us
    pallas_call x1, Pallas kernels, call_forward(): pl.pallas_call(forward_kernel, out_shape=(SD(CUBE + (BLK, width), BF16),...  72.3 us
    unnamed x4, local copies, waits for them, and re-layouts  7.18 us

profile of v5, /device:TPU:1, one launch (start us, length us, event | category | flops | bytes accessed | tf_op | source)
XLA Modules:
  0.0 192.2 jit_solution(4905681882993266592)
XLA Ops:
  0.6 1.3 scatter.11.toks
  1.9 0.7 convert_element_type.17
  2.6 0.7 scatter.10.pos
  3.3 1.2 copy.13
  4.6 1.0 copy.15.hw
  5.6 72.3 %forward_plane.1 = (bf16[2,2,2,2,2,16,4096]{6,5,4,3,2,1,0:T(8,128)(2,1)}, bf16[8,2,256,512]{3,2,1,0:T(8,128)(2,1)}, f32[16,4096]{1,0:T(8,128)}, f32[16,128]{1,0:...) custom-call(bf16[256,4096]{1,0:T(8,128)(2,1)} %feats.1, ...), custom_call_target="tpu_custom_call" | custom-call | flops 10000000000 | bytes 100000000 | tf_op jit(solution)/shard_map/forward_plane/pallas_call | solution.py:647
  77.9 0.7 slice_convert_fusion
  78.6 0.6 scatter.14.toks
  79.2 107.0 %backward_plane.1 = (f32[256,1024]{1,0:T(8,128)}, f32[448,256]{1,0:T(8,128)}, f32[448,256]{1,0:T(8,128)}) custom-call(bf16[512,4096]{1,0:T(8,128)(2,1)} %bitcast.25, bf16[4096,512]{1,0:T(8,128)(2,1)} %bitcast.26, bf16[8,256,128]{2,1,0:T(8,128)(2,1)} %get-tuple-element.52.target, bf16[448,4096]{1,0:T(8,128)(2,1)} %w_out.3, bf16[512,2048]{1,0:T(8,128)(2,1)} %bitcast.27, ...), custom_call_target="tpu_custom_call" | custom-call | flops 10000000000 | bytes 100000000 | tf_op jit(solution)/shard_map/backward_plane/pallas_call | solution.py:702
  186.3 2.3 %copy.19 = f32[256,1024]{1,0:T(8,128)} copy(f32[256,1024]{1,0:T(8,128)} %get-tuple-element.64) | data formatting | bytes 2097152
  188.6 1.8 copy.20
  190.4 1.8 copy.21
  (2 shorter events, 0.1 us)

commit v6 on v1

v6 whole, which is shorter than its diff:
```python
import functools
import jax
import jax.numpy as jnp
from jax import lax
from jax.experimental import pallas as pl
from jax.experimental.pallas import tpu as pltpu
from jax.sharding import Mesh, PartitionSpec as P

EPS = 1e-05
HARD = 0.5
MESH = pl.DeviceIdType.MESH
LEAD = ("YB", "core", "XA", "YA", "XB")
REST = ("YB", "XA", "YA", "XB")
ICI3 = ("XA", "YA", "XB")
ICI4 = ("XA", "YA", "XB", "YB")
CUBE = (2,) * 5
BLK = 16
F32 = jnp.float32
BF16 = jnp.bfloat16


FORWARD_STEPS = ((1, 0, 2, 0, 1), (1, 0, 1, 1))
BACKWARD_STEPS = ((0, 0, 1, 1, 0, 1), (0, 1, 1, 1))


def place():
    x, ylo, yhi, core, z = (lax.axis_index(n) for n in ("x", "ylo", "yhi", "core", "z"))
    nz = lax.axis_size("z")
    y = 2 * yhi + ylo
    odd = lax.rem(x, 2)
    bits = {
        "core": core,
        "XA": lax.rem(lax.div(x + 1, 2), 2),
        "XB": lax.div(x, 2),
        "YA": lax.rem(lax.div(y + 1, 2), 2),
        "YB": yhi,
    }
    to = {
        "core": {"core": 1 - core},
        "XA": {"x": x + 1 - 2 * odd},
        "XB": {"x": lax.rem(x + 3 + 2 * odd, 4)},
        "YA": {"ylo": 1 - ylo},
        "YB": {"ylo": 1 - ylo, "yhi": 1 - yhi},
        "pair": {"yhi": 1 - yhi},
        "up": {"z": lax.rem(z + 1, nz)},
        "down": {"z": lax.rem(z + nz - 1, nz)},
    }
    for i in range(1, nz):
        to[i] = {"z": lax.rem(z + i, nz)}
    for i in range(4):
        for c in range(2):
            to["row", i, c] = {"x": lax.rem(x + i, 4), "core": lax.rem(core + c, 2)}
    for a in range(2):
        for b in range(2):
            to["col", a, b] = {"ylo": lax.rem(ylo + a, 2), "yhi": lax.rem(yhi + b, 2)}
    return bits, to, z, nz


def at(names, fixed, cols=None):
    where = tuple(fixed.get(n, slice(None)) for n in names)
    return where + (slice(None), slice(None) if cols is None else pl.ds(*cols))


def corners(names):
    out = [{}]
    for n in names:
        out = [dict(o, **{n: v}) for o in out for v in (0, 1)]
    return out


class Sender:
    def __init__(self, send_sem, recv_sem, to):
        self.send_sem, self.recv_sem, self.to = send_sem, recv_sem, to
        self.n = 0
        self.open = []

    def go(self, src, dst, dim):
        n = self.n
        c = pltpu.make_async_remote_copy(
            src_ref=src,
            dst_ref=dst,
            send_sem=self.send_sem.at[n],
            recv_sem=self.recv_sem.at[n],
            device_id=self.to[dim],
            device_id_type=MESH,
        )
        c.start()
        self.n += 1
        self.open.append(c)
        return c

    def drain(self):
        for c in self.open:
            c.wait_send()
        self.open = []


class Local:
    def __init__(self, sem):
        self.sem = sem
        self.n = 0

    def go(self, src, dst):
        c = pltpu.make_async_copy(src, dst, self.sem.at[self.n])
        c.start()
        self.n += 1
        return c


def colours(n, width):
    tiles = width // 128
    edges = [128 * (tiles * k // n) for k in range(n + 1)]
    return [(edges[k], edges[k + 1] - edges[k]) for k in range(n)]


def greet(to, dims):
    barrier = pltpu.get_barrier_semaphore()
    for d in dims:
        pl.semaphore_signal(barrier, inc=1, device_id=to[d], device_id_type=MESH)
    return lambda: pl.semaphore_wait(barrier, len(dims))


def meet(to, dims):
    greet(to, dims)()


def step(thread):
    return next(thread, None)


def finish(thread):
    for _ in thread:
        pass


def region(names, order, bits, j, core):
    fixed = {m: bits[m] for m in order[:j]}
    if j < len(order):
        fixed[order[j]] = 1 - bits[order[j]]
    if core:
        fixed["core"] = bits["core"]
    return fixed, [m for m in names if m not in fixed]


def reduce_cube(send, bits, names, dims, width, part, total, landed):
    rest = tuple(n for n in names if n != "core")
    n = len(dims)
    cuts = colours(n, width)
    orders = [[dims[(k + i) % n] for i in range(n)] for k in range(n)]
    first, second = [], []
    for keep, held in ((1, first), (0, second)):
        for k in range(n):
            d = dims[k]
            bit = 1 - bits[d] if keep else bits[d]
            src = part.at[at(names, {"core": 1 - bits["core"], d: bit}, cuts[k])]
            dst = total.at[at(rest, {d: bit}, cuts[k])]
            held.append(send.go(src, dst, "core"))

    def merge(k, bit):
        d = dims[k]
        for f in corners([m for m in rest if m != d]):
            f = dict(f, **{d: bit})
            w = at(rest, f, cuts[k])
            total[w] = total[w] + part[at(names, dict(f, core=bits["core"]), cuts[k])]

    slots = iter(landed)
    coming = {}

    def start(k, i):
        o = orders[k]
        for j in range(i + 1, n + 1):
            fixed = region(rest, o, bits, j, False)[0]
            fixed[o[i]] = 1 - bits[o[i]]
            slot = next(slots)
            src = total.at[at(rest, fixed, cuts[k])]
            coming[k, i, j] = (send.go(src, slot, o[i]), slot)

    yield
    for k in range(n):
        first[k].wait_recv()
        merge(k, 1 - bits[dims[k]])
        start(k, 0)
    yield
    for k in range(n):
        second[k].wait_recv()
        merge(k, bits[dims[k]])
    for j in range(1, n + 1):
        yield
        for k in range(n):
            fixed, free = region(rest, orders[k], bits, j, False)
            got = [coming[k, i, j] for i in range(j)]
            for c, _ in got:
                c.wait_recv()
            for f in corners(free):
                w = at(rest, dict(f, **fixed), cuts[k])
                value = total[w]
                for _, slot in got:
                    value = value + slot[tuple(f[m] for m in free)]
                total[w] = value
            if j < n:
                start(k, j)


def landing(dims, width):
    n = len(dims)
    cuts = colours(n, width)

    def room(k, i):
        return [
            pltpu.VMEM((2,) * (n - 1 - j) + (BLK, cuts[k][1]), BF16) for j in range(i + 1, n + 1)
        ]

    return [slot for i in range(n) for k in range(n) for slot in room(k, i)]


def gather_cube(send, bits, dims, width, full, names=LEAD):
    n = len(dims)
    cuts = colours(n, width)
    orders = [[dims[(k + i) % n] for i in range(n)] for k in range(n)]
    own = full.at[at(names, bits)]
    direct = {d: send.go(own, own, d) for d in dims}
    arriving = [send.go(own, own, "core")]
    coming = {(k, j): [] for k in range(n) for j in range(n)}
    for i in range(n):
        yield
        for k in range(n):
            o = orders[k]
            if i == 0:
                direct[o[0]].wait_recv()
            for c in coming[k, i]:
                c.wait_recv()
            fixed = {m: bits[m] for m in names if m not in o[:i]}
            fixed[o[i]] = 1 - bits[o[i]]
            piece = full.at[at(names, fixed, cuts[k])]
            for j in range(i + 1, n):
                coming[k, j].append(send.go(piece, piece, o[j]))
            arriving.append(send.go(piece, piece, "core"))
    for c in arriving:
        c.wait_recv()


def ring_gather(send, z, nz, full, own, other, late):
    half = nz // 2
    rows = (own, other)

    def block(i, q):
        return full.at[lax.rem(z + nz + i, nz), rows[q]]

    flying = {}

    def hop(s, q):
        for way, sign, short in (("up", -1, 0), ("down", 1, 1)):
            if s and (s < half or q == short):
                flying[way, q].wait_recv()
            if s + 1 < half or (s + 1 == half and q == short):
                flying[way, q] = send.go(block(sign * s, q), block(sign * s, q), way)

    hop(0, 0)
    yield None
    hop(1, 0)
    yield None
    late.wait_recv()
    hop(0, 1)
    yield 0
    for s in range(1, half + 1):
        if s + 1 <= half:
            hop(s + 1, 0)
            yield None
        hop(s, 1)
        yield s


def ring_scatter(send, z, nz, part, ups, downs, cut, prepare):
    half = nz // 2
    made = set()

    def mine(i, q):
        b = lax.rem(z + nz + i, nz)
        if (i % nz, q) not in made:
            made.add((i % nz, q))
            prepare(b, q)
        return part.at[(b,) + cut[q]]

    flying = {}
    ways = (("up", ups, 1), ("down", downs, -1))
    for q in (1, 0):
        for way, landed, sign in ways:
            s = 0 if q == (0 if way == "up" else 1) else 1
            if s < half:
                flying[way, s, q] = send.go(mine(sign * (half - s), q), landed[s].at[cut[q]], way)
        yield
    for s in range(half):
        for lead in (1, 0) if s else (0,):
            for way, landed, sign in ways:
                q = lead if way == "up" else 1 - lead
                own = mine(sign * (half - 1 - s), q)
                flying[way, s, q].wait_recv()
                if s + 1 < half:
                    ref = landed[s].at[cut[q]]
                    ref[...] = ref[...] + own[...]
                    flying[way, s + 1, q] = send.go(ref, landed[s + 1].at[cut[q]], way)
            yield
    for q in range(2):
        mine(0, q)


def ring_result(z, part, ups, downs, cut, q):
    total = part[(z,) + cut[q]].astype(F32)
    sides = (ups, downs) if len(ups) > 1 else ((ups, downs)[q],)
    for side in sides:
        total = total + side[-1][cut[q]].astype(F32)
    return total


def runs_of(value, parity, tw):
    out = []
    for k in range(value.shape[1] // (4 * tw)):
        starts = [(2 * (2 * k + i) + parity) * tw for i in range(2)]
        out.append(jnp.concatenate([value[:, s : s + tw] for s in starts], 1))
    return jnp.concatenate(out, 1)


def own_row(bits):
    r = bits["core"]
    for n in ("XA", "YA", "XB"):
        r = 2 * r + bits[n]
    return r * BLK


def exchange_stats(send, own, near, held, far, out):
    def merge(src, slots, peers, dst):
        flying = [send.go(src, slots.at[i], p) for i, p in enumerate(peers)]
        for c in flying:
            c.wait_recv()
        parts = [src[...]] + [slots[i] for i in range(len(peers))]
        tops = [p[0:2] for p in parts]
        top = functools.reduce(jnp.maximum, tops)
        total = functools.reduce(
            jnp.add, [p[2:4] * jnp.exp(t - top) for p, t in zip(parts, tops)]
        )
        dst[0:2] = top
        dst[2:4] = total

    held[4:8] = jnp.zeros((4, held.shape[1]), F32)
    merge(own, near, [("row", i, c) for i in range(4) for c in range(2) if i or c], held)
    merge(held, far, [("col", a, b) for a in range(2) for b in range(2) if a or b], out)


NT = (((1,), (1,)), ((), ()))
TN = (((0,), (0,)), ((), ()))


def kernel(
    run, first_col,
    feats, gain_in, w_in, w_out, gain, hw, buf, pos, toks,
    gh_out, gf_out,
    fv, hs, pp, tk, tk2, w1, w2, bv, bn, normed, other, pre, part, total, full, head, ordered, target,
    pexp, lg, own, near, held, far, back, dl, dres, ghp, ghx, gfp, act, dpre,
    send_sem, recv_sem, local_sem, *landed,
):
    bits, to, z, nz = place()
    yhi = bits["YB"]
    tok, width = fv.shape
    n_tok = 2 * tok
    n_col = head.shape[2]
    units = w1.shape[0]
    tw = bv.shape[0]
    half = nz // 2
    names = LEAD[1:]
    gh_rings, landed = landed[:nz], landed[nz:]
    n_forward = len(landing(ICI3, width))
    peers = [("row", i, c) for i in range(4) for c in range(2) if i or c]
    peers += [("col", a, b) for a in range(2) for b in range(2) if a or b]
    greeted = greet(to, peers + ["up", "down"] + list(range(2, nz - 1)))
    local = Local(local_sem)
    got_f = local.go(feats, fv)
    got_w1 = local.go(w_in, w1)
    got_w2 = local.go(w_out, w2)
    got_b = local.go(buf, bv)

    here = pl.ds(pl.multiple_of(yhi * run, run), run)
    there = pl.ds(pl.multiple_of((1 - yhi) * run, run), run)
    both = hw[...].astype(F32)
    both = [runs_of(both, p, tw) for p in range(2)]
    head[z, here] = jnp.where(yhi == 0, both[0], both[1]).astype(BF16)
    hs[...] = jnp.where(yhi == 0, both[1], both[0]).astype(BF16)
    tk[...] = jnp.zeros(tk.shape, jnp.int32)
    tk[0 : toks.shape[0]] = toks[...]
    pp[...] = jnp.zeros(pp.shape, F32)
    pp[0 : pos.shape[0]] = pos[...].astype(F32)

    got_f.wait()
    chunk = 64

    def norm_rows(i, _):
        rows = pl.ds(pl.multiple_of(i * chunk, chunk), chunk)
        x = fv[rows, :].astype(F32)
        r = lax.rsqrt(jnp.mean(x * x, -1, keepdims=True) + EPS)
        normed[rows, :] = (x * r * gain_in[...]).astype(BF16)
        return 0

    lax.fori_loop(0, tok // chunk, norm_rows, 0)
    greeted()
    send = Sender(send_sem, recv_sem, to)
    late = send.go(hs, head.at[z, here], "pair")
    ring = ring_gather(send, z, nz, head, here, there, late)
    step(ring)
    swapped = [send.go(tk, tk2, "pair")]
    mine = pl.ds(pl.multiple_of(own_row(bits), BLK), BLK)
    crossed = send.go(normed.at[mine], other.at[at(names, bits)], "YB")

    deep = width // 4

    def project(slot, rows):
        for c in range(4):
            k = pl.ds(c * deep, deep)
            prod = lax.dot_general(rows(k), w1[:, k], NT, preferred_element_type=F32)
            pre[slot] = prod if c == 0 else pre[slot] + prod

    got_w1.wait()
    project(0, lambda k: normed[:, k])
    v = pre[0]
    forward_act = (v * jax.nn.sigmoid(v)).astype(BF16)
    got_w2.wait()
    wide = width // 8
    first_part, first_total = part.at[0], total.at[0]
    for c in range(8):
        cols = (c * wide, wide)
        block = jnp.dot(forward_act, w2[:, pl.ds(*cols)], preferred_element_type=F32).astype(BF16)
        for i, f in enumerate(corners(names)):
            first_part[at(names, f, cols)] = block[i * BLK : (i + 1) * BLK]

    got_b.wait()
    n_buf = bv.shape[1]
    piece = 1024 if n_buf % 1024 == 0 else n_buf
    pos_t = pp[...].T

    def ordered_rows(i):
        dest = lax.rem(z + i, nz)
        lane = lax.broadcasted_iota(jnp.int32, pos_t.shape, 1)
        each = tok // 128
        there = [
            jnp.concatenate(
                [
                    jnp.sum(
                        jnp.where(lane == (2 * dest + h) * each + e, pos_t, 0.0), 1, keepdims=True
                    )
                    for e in range(each)
                ],
                0,
            )
            for h in range(2)
        ]
        cols = lax.broadcasted_iota(jnp.int32, (tok, piece), 1).astype(F32)

        def inner(t, sums):
            rows = bn[pl.ds(pl.multiple_of(t * piece, piece), piece), :]
            out = []
            for h in range(2):
                hot = jnp.where(there[h] - (t * piece).astype(F32) == cols, 1.0, 0.0).astype(BF16)
                out.append(sums[h] + jnp.dot(hot, rows, preferred_element_type=F32))
            return tuple(out)

        zero = jnp.zeros((tok, bv.shape[0]), F32)
        a, b = lax.fori_loop(0, n_buf // piece, inner, (zero, zero))
        return jnp.concatenate([a, b], 1).astype(BF16)

    def gather_target():
        for i in range(1, nz):
            ordered[i] = ordered_rows(i)
            way = "up" if i == 1 else "down" if i == nz - 1 else i
            swapped.append(send.go(ordered.at[i], target.at[z], way))
            yield
        target[z] = ordered_rows(0)
        yield

    def gather_other():
        crossed.wait_recv()
        yield from gather_cube(send, bits, ICI3, width, other, names)

    side = gather_target()
    cross = gather_other()
    ready = []

    def advance(count):
        for _ in range(count):
            s = step(ring)
            if s is not None:
                ready.extend([s] if s in (0, half) else [s, -s])

    reduce = reduce_cube(send, bits, names, ICI3, width, first_part, first_total, landed[:n_forward])
    for i, _ in enumerate(reduce):
        if i == 0:
            bn[...] = bv[...].T
        step(side)
        advance(FORWARD_STEPS[0][i])
        if i >= 1:
            step(cross)
    hidden = first_total[at(ICI3, bits)].astype(F32)
    resid = fv[mine, :].astype(F32) + hidden
    rscale = lax.rsqrt(jnp.mean(resid * resid, -1, keepdims=True) + EPS)
    full[at(LEAD, bits)] = (resid * rscale * gain[...]).astype(BF16)
    for i, _ in enumerate(gather_cube(send, bits, ICI4, width, full)):
        step(side)
        advance(FORWARD_STEPS[1][i])
    finish(side)
    finish(cross)
    project(1, lambda k: other[at(names, {}, (k.start, k.size))].reshape(tok, k.size))

    started = []

    def add_logits():
        while ready:
            b = lax.rem(z + nz + ready.pop(0), nz)
            cols = (pl.multiple_of(b * 2 * run, 2 * run), 2 * run)
            rows = full[at(LEAD, {}, cols)].reshape(n_tok, 2 * run)
            prod = jnp.dot(rows, head[b], preferred_element_type=F32)
            lg[...] = lg[...] + prod if started else prod
            started.append(b)

    add_logits()
    for c in swapped:
        c.wait_recv()
    for k in range(nz // 2):
        for s in range(2):
            lanes = slice(s * tw, (s + 1) * tw)
            two = [target[2 * k + i].astype(F32)[:, lanes] for i in range(2)]
            pexp[s * tok : (s + 1) * tok, k * 2 * tw : (k + 1) * 2 * tw] = jnp.concatenate(two, 1)
    t = pexp[...]
    top_p = jnp.max(t, -1, keepdims=True)
    t = jnp.exp(t - top_p)
    pexp[...] = t
    sum_p = jnp.sum(t, -1, keepdims=True)
    for s in ring:
        if s is not None:
            ready.extend([s] if s in (0, half) else [s, -s])
            add_logits()
    t = lg[...]
    top_q = jnp.max(t, -1, keepdims=True)
    t = jnp.exp(t - top_q)
    lg[...] = t
    sum_q = jnp.sum(t, -1, keepdims=True)
    lane = lax.broadcasted_iota(jnp.int32, (n_tok, 128), 1)
    columns = jnp.where(
        lane == 0, top_q, jnp.where(lane == 1, top_p, jnp.where(lane == 2, sum_q, sum_p))
    )
    own[...] = columns.T[0:8]
    back[...] = jnp.zeros(back.shape, F32)
    for i in range(n_tok // 128):
        e = i % (tok // 128)
        line = jnp.where(yhi == i // (tok // 128), tk[e : e + 1], tk2[e : e + 1])
        back[8:9, i * 128 : (i + 1) * 128] = line.astype(F32)
    send.drain()
    exchange_stats(send, own, near, held, far, back)
    columns = back[...].T
    all_q, all_p, tot_q, tot_p, token = (columns[:, i : i + 1] for i in (0, 1, 2, 3, 8))
    q = lg[...] * (jnp.exp(top_q - all_q) / tot_q)
    p = pexp[...] * (jnp.exp(top_p - all_p) / tot_p)
    lane = lax.broadcasted_iota(jnp.int32, (n_tok, n_col), 1)
    shift = tw.bit_length() - 1
    column = first_col() + lane + jnp.left_shift(jnp.right_shift(lane, shift), shift)
    onehot = jnp.where(token.astype(jnp.int32) == column, 1.0, 0.0)
    dl[...] = (q - p + HARD * (q - onehot)).astype(BF16)

    split = n_col // 2
    rows_cut = [(pl.ds(i * split, split), slice(None)) for i in range(2)]

    def make_gh(b, q):
        cols = (pl.multiple_of(b * 2 * run, 2 * run), 2 * run)
        rows = full[at(LEAD, {}, cols)].reshape(n_tok, 2 * run)
        ghp[(b,) + rows_cut[q]] = lax.dot_general(
            dl[:, q * split : (q + 1) * split], rows, TN, preferred_element_type=F32
        ).astype(BF16)

    gh_ups, gh_downs = gh_rings[:half], gh_rings[half:]
    ring = ring_scatter(send, z, nz, ghp, gh_ups, gh_downs, rows_cut, make_gh)
    step(ring)
    step(ring)
    block_rows = head.shape[1]
    for c in range(nz):
        cols = (c * block_rows, block_rows)
        block = lax.dot_general(dl[...], head[c], NT, preferred_element_type=F32).astype(BF16)
        for i, f in enumerate(corners(LEAD)):
            part[at(LEAD, f, cols)] = block[i * BLK : (i + 1) * BLK]
    reduce = reduce_cube(send, bits, LEAD, ICI4, width, part, total, landed[n_forward:])
    for i, _ in enumerate(reduce):
        for _ in range(BACKWARD_STEPS[0][i]):
            step(ring)
    dfinal = total[at(REST, bits)].astype(F32)
    scaled = dfinal * gain[...]
    inner = jnp.sum(scaled * resid, -1, keepdims=True)
    dres[at(LEAD, bits)] = (
        rscale * scaled - resid * (rscale * rscale * rscale / width * inner)
    ).astype(BF16)
    for i, _ in enumerate(gather_cube(send, bits, ICI4, width, dres)):
        for _ in range(BACKWARD_STEPS[1][i]):
            step(ring)
    finish(ring)

    def dresid(start, size):
        return dres[at(LEAD, {}, (start, size))].reshape(n_tok, size)

    def by_half(a, b):
        return jnp.where(yhi == 0, a, b), jnp.where(yhi == 0, b, a)

    v = jnp.concatenate(by_half(pre[0], pre[1]), 0)
    sig = jax.nn.sigmoid(v)
    act[...] = (v * sig).astype(BF16)
    lanes_cut = [(slice(None), pl.ds(i * run, run)) for i in range(2)]

    def make_gf(b, q):
        start = pl.multiple_of((2 * b + yhi) * run, run)
        if q:
            left, right = act[...], dresid(start, run)
        else:
            rows = other[at(names, {}, (start, run))].reshape(tok, run)
            left = dpre[...]
            right = jnp.concatenate(by_half(normed[:, pl.ds(start, run)], rows), 0)
        gfp[(b,) + lanes_cut[q]] = lax.dot_general(
            left, right, TN, preferred_element_type=F32
        ).astype(BF16)

    gf_ups = [head.at[i, 0:units] for i in range(half)]
    gf_downs = [head.at[half + i, 0:units] for i in range(half)]
    last = ring_scatter(send, z, nz, gfp, gf_ups, gf_downs, lanes_cut, make_gf)
    step(last)
    for c in range(4):
        k = pl.ds(c * deep, deep)
        prod = lax.dot_general(dresid(c * deep, deep), w2[:, k], NT, preferred_element_type=F32)
        lg[:, 0:units] = prod if c == 0 else lg[:, 0:units] + prod
    dpre[...] = (lg[:, 0:units] * sig * (1.0 + v * (1.0 - sig))).astype(BF16)
    step(last)

    for i in range(2):
        dl[rows_cut[i]] = ring_result(z, ghp, gh_ups, gh_downs, rows_cut, i).astype(BF16)
    crossed = send.go(dl.at[:, there], ghx, ("col", 0, 1))
    for _ in range(3):
        step(last)
    crossed.wait_recv()
    for k in range(nz):
        src = slice(k * tw, (k + 1) * tw)
        for value, side in ((dl[src, here], yhi), (ghx[src, :], 1 - yhi)):
            gh_out[pl.ds(pl.multiple_of(k * 2 * tw + side * tw, tw), tw), :] = value
    finish(last)
    for i in range(2):
        gf_out[lanes_cut[i]] = ring_result(z, gfp, gf_ups, gf_downs, lanes_cut, i).astype(BF16)
    send.drain()


VM = pl.BlockSpec(memory_space=pltpu.VMEM)
ANY = pl.BlockSpec(memory_space=pl.ANY)
SD = jax.ShapeDtypeStruct


def params(cid):
    return pltpu.CompilerParams(
        collective_id=cid, has_side_effects=True, vmem_limit_bytes=62 * 1024 * 1024
    )


def sems(remote, local):
    dma = pltpu.SemaphoreType.DMA
    return [dma((remote,)), dma((remote,)), dma((local,))]


def call_step(first_col, feats, gain_in, w_in, w_out, gain, hw, buf, pos, toks):
    tok, width = feats.shape
    units = w_in.shape[0]
    run, n_col = hw.shape[0], hw.shape[1] // 2
    nz = lax.axis_size("z")
    tw = buf.shape[0]
    n_tok = 2 * tok
    vm = pltpu.VMEM
    scratch = [
        vm((tok, width), BF16),
        vm((run, n_col), BF16),
        vm((128, 128), F32),
        vm((8, 128), jnp.int32),
        vm((8, 128), jnp.int32),
        vm(w_in.shape, BF16),
        vm(w_out.shape, BF16),
        vm(buf.shape, BF16),
        vm(buf.shape[::-1], BF16),
        vm((tok, width), BF16),
        vm(CUBE[1:] + (BLK, width), BF16),
        vm((2, tok, units), F32),
        vm(CUBE + (BLK, width), BF16),
        vm(CUBE[1:] + (BLK, width), BF16),
        vm(CUBE + (BLK, width), BF16),
        vm((nz, 2 * run, n_col), BF16),
        vm((nz, tok, 2 * tw), BF16),
        vm((nz, tok, 2 * tw), BF16),
        vm((n_tok, n_col), F32),
        vm((n_tok, n_col), F32),
        vm((8, n_tok), F32),
        vm((7, 8, n_tok), F32),
        vm((8, n_tok), F32),
        vm((3, 8, n_tok), F32),
        vm((128, n_tok), F32),
        vm((n_tok, n_col), BF16),
        vm(CUBE + (BLK, width), BF16),
        vm((nz, n_col, 2 * run), BF16),
        vm((n_col, run), BF16),
        vm((nz, units, 2 * run), BF16),
        vm((n_tok, units), BF16),
        vm((n_tok, units), BF16),
    ]
    rings = [vm((n_col, 2 * run), BF16) for _ in range(nz)]
    return pl.pallas_call(
        functools.partial(kernel, run, first_col),
        out_shape=(SD((2 * n_col, run), BF16), SD((units, 2 * run), BF16)),
        in_specs=[ANY, VM, ANY, ANY, VM, VM, ANY, VM, VM],
        out_specs=(VM, VM),
        scratch_shapes=scratch
        + sems(256, 4)
        + rings
        + landing(ICI3, width)
        + landing(ICI4, width),
        compiler_params=params(1),
        cost_estimate=pl.CostEstimate(flops=10**10, bytes_accessed=10**8, transcendentals=0),
        name="distill_step",
    )(feats, gain_in[None], w_in, w_out, gain[None], hw, buf, pos, toks)


def write_kernel(gh, gf, gh_out, gi_out, go_out):
    run = gi_out.shape[1]
    gh_out[...] = gh[...].astype(F32).T
    gi_out[...] = gf[:, 0:run].astype(F32)
    go_out[...] = gf[:, run:].astype(F32)


def call_write(gh, gf):
    run = gh.shape[1]
    half = SD((gf.shape[0], run), F32)
    return pl.pallas_call(
        write_kernel,
        out_shape=(SD((run, gh.shape[0]), F32), half, half),
        in_specs=[VM, VM],
        out_specs=(VM, VM, VM),
        compiler_params=pltpu.CompilerParams(vmem_limit_bytes=32 * 1024 * 1024),
        name="write_out",
    )(gh, gf)


def body(
    features, token_ids, positions, target_buffer, norm_gain, final_gain, w_in, w_out, head_weight
):
    cols = head_weight.shape[1]
    tw = target_buffer.shape[1]

    def first_col():
        block = (lax.axis_index("ylo") * 4 + lax.axis_index("x")) * 2 + lax.axis_index("core")
        return block * cols + lax.axis_index("yhi") * tw

    gh, gf = call_step(
        first_col,
        features,
        norm_gain,
        w_in.T,
        w_out,
        final_gain,
        head_weight,
        target_buffer.T,
        positions.reshape(-1, 128),
        token_ids.reshape(-1, 128),
    )
    gh, gi, go = call_write(gh, gf)
    return (gh, gi.T, go)


def solution(mesh):
    names = ("ylo", "x", "core", "z", "yhi")
    fine = Mesh(mesh.devices.reshape(2, 4, 2, -1, 2), names)
    v = ("ylo", "x", "core")
    d = ("z", "yhi")
    return jax.shard_map(
        body,
        mesh=fine,
        in_specs=(
            P(d, None),
            P(d),
            P(),
            P(None, v + d),
            P(),
            P(),
            P(None, v),
            P(v, None),
            P(d, v),
        ),
        out_specs=(P(d, v), P(d, v), P(v, d)),
        check_vma=False,
    )
```

time: 542 us -> 177 us (0.33)
  waiting for transfers between devices: 394 us -> 0 us
  Pallas kernels: 0 us -> 174 us
  blocking collectives: 40.5 us -> 0 us
  matrix products: 34.4 us -> 0 us
  local copies, waits for them, and re-layouts: 26.2 us -> 2.05 us
  starting transfers between devices: 15.3 us -> 0 us
  between operations: 15.8 us -> 0.65 us
  other arithmetic: 14.4 us -> 0 us
    reduce_scatter x4 -> x0, waiting for transfers between devices: 246 us -> none  [the longest x2 160 us: body(): lax.psum_scatter(part, PLANE, scatter_dimension=0, tiled=True).astype(f32)]
    pallas_call x0 -> x2, Pallas kernels: none -> 174 us  [the longest x1 173 us: call_step(): pl.pallas_call(functools.partial(kernel, run, first_col), out_shape=(SD((...]
    all_gather x4 -> x0, waiting for transfers between devices: 132 us -> none  [the longest x1 69 us: body(): feats = lax.all_gather(features, 'yhi', axis=0, tiled=True)]
    dot_general x7 -> x0, matrix products: 34.4 us -> none  [the longest x1 7.89 us: body(): lax.dot_general(normed, dpre, contract, preferred_element_type=f32)]
    all_gather x2 -> x0, blocking collectives: 29.2 us -> none  [the longest x1 24.6 us: body(): every = lax.all_gather(stats, PLANE, axis=0)]
    all_to_all x3 -> x0, waiting for transfers between devices: 15.2 us -> none  [the longest x1 10.2 us: body(): lax.all_to_all(ordered, 'z', split_axis=0, concat_axis=2, tiled=True)[0]]
    all_to_all x3 -> x0, starting transfers between devices: 14.7 us -> none  [the longest x1 6.73 us: body(): lax.all_to_all(ordered, 'z', split_axis=0, concat_axis=2, tiled=True)[0]]
    gather x1 -> x0, local copies, waits for them, and re-layouts: 12.1 us -> none  [body(): ordered = target_buffer[positions].reshape(8, -1, tw)]
  transfers between devices with their start and end apart: 11 -> 0, of which waited for: 9 -> 0; matrix products, arithmetic and copies ran while one was open for 9% -> 0% of each run, Pallas kernels for 0% -> 0%
where the time goes in v6:
time: 177 us
  Pallas kernels  174 us (98%)
  local copies, waits for them, and re-layouts  2.05 us (1%)
    pallas_call x1, Pallas kernels, call_step(): pl.pallas_call(functools.partial(kernel, run, first_col), out_shape=(SD((...  173 us

profile of v6, /device:TPU:1, one launch (start us, length us, event | category | flops | bytes accessed | tf_op | source)
XLA Modules:
  0.0 177.1 jit_solution(16938228612065435579)
XLA Ops:
  0.6 172.9 %distill_step.1 = (bf16[1024,256]{1,0:T(8,128)(2,1)}, bf16[448,512]{1,0:T(8,128)(2,1)}) custom-call(bf16[256,4096]{1,0:T(8,128)(2,1)} %feats.1, f32[1,4096]{1,0:T(1,128)} %bitcast.10, bf16[448,4096]{1,0:T(8,128)(2,1)} %bitcast.7, bf16[448,4096]{1,0:T(8,128)(2,1)} %w_out.1, f32[1,4096]{1,0:T(1,128)} %bitcast.11, bf16[256,1024]{1,0:T(8,128)(2,1)} %hw.1, ...), custom_call_target="tpu_custom_call" | custom-call | flops 10000000000 | bytes 100000000 | tf_op jit(solution)/shard_map/distill_step/pallas_call | solution.py:709
  173.6 0.0 copy-start
  173.6 1.0 copy-done
  174.6 0.0 copy-start.1
  174.6 1.0 copy-done.1
  175.6 1.4 write_out.1
Async XLA Ops:
  173.6 1.0 copy-start
  174.6 1.0 copy-start.1

commit v7 on v6

--- a/solution.py
+++ b/solution.py
@@ -19,8 +19,8 @@
 BF16 = jnp.bfloat16
 
 
-FORWARD_STEPS = ((1, 0, 2, 0, 1), (1, 0, 1, 1))
-BACKWARD_STEPS = ((0, 0, 1, 1, 0, 1), (0, 1, 1, 1))
+FORWARD_STEPS = ((1, 1, 1, 0, 1), (1, 1, 1, 1))
+BACKWARD_STEPS = ((0, 1, 1, 0, 1, 0), (1, 1, 0, 1))
 
 
 def place():
@@ -289,17 +289,18 @@
             if s < half:
                 flying[way, s, q] = send.go(mine(sign * (half - s), q), landed[s].at[cut[q]], way)
         yield
-    for s in range(half):
-        for lead in (1, 0) if s else (0,):
-            for way, landed, sign in ways:
-                q = lead if way == "up" else 1 - lead
-                own = mine(sign * (half - 1 - s), q)
-                flying[way, s, q].wait_recv()
-                if s + 1 < half:
-                    ref = landed[s].at[cut[q]]
-                    ref[...] = ref[...] + own[...]
-                    flying[way, s + 1, q] = send.go(ref, landed[s + 1].at[cut[q]], way)
-            yield
+    up = [(1, 1), (0, 0)] + [t for s in range(2, half) for t in ((s, 1), (s - 1, 0))] + [(half - 1, 0)]
+    order = [t for t in dict.fromkeys(up) if t[0] < half]
+    down = [(0, 1)] + [t for s in range(1, half) for t in ((s, 0), (s, 1))]
+    for event in zip(order, down):
+        for (way, landed, sign), (s, q) in zip(ways, event):
+            own = mine(sign * (half - 1 - s), q)
+            flying[way, s, q].wait_recv()
+            if s + 1 < half:
+                ref = landed[s].at[cut[q]]
+                ref[...] = ref[...] + own[...]
+                flying[way, s + 1, q] = send.go(ref, landed[s + 1].at[cut[q]], way)
+        yield
     for q in range(2):
         mine(0, q)
 
@@ -592,7 +593,16 @@
     dres[at(LEAD, bits)] = (
         rscale * scaled - resid * (rscale * rscale * rscale / width * inner)
     ).astype(BF16)
+    def by_half(a, b):
+        return jnp.where(yhi == 0, a, b), jnp.where(yhi == 0, b, a)
+
+    def in_order():
+        return jnp.concatenate(by_half(pre[0], pre[1]), 0)
+
     for i, _ in enumerate(gather_cube(send, bits, ICI4, width, dres)):
+        if i == 0:
+            v = in_order()
+            act[...] = (v * jax.nn.sigmoid(v)).astype(BF16)
         for _ in range(BACKWARD_STEPS[1][i]):
             step(ring)
     finish(ring)
@@ -600,12 +610,6 @@
     def dresid(start, size):
         return dres[at(LEAD, {}, (start, size))].reshape(n_tok, size)
 
-    def by_half(a, b):
-        return jnp.where(yhi == 0, a, b), jnp.where(yhi == 0, b, a)
-
-    v = jnp.concatenate(by_half(pre[0], pre[1]), 0)
-    sig = jax.nn.sigmoid(v)
-    act[...] = (v * sig).astype(BF16)
     lanes_cut = [(slice(None), pl.ds(i * run, run)) for i in range(2)]
 
     def make_gf(b, q):
@@ -628,6 +632,8 @@
         k = pl.ds(c * deep, deep)
         prod = lax.dot_general(dresid(c * deep, deep), w2[:, k], NT, preferred_element_type=F32)
         lg[:, 0:units] = prod if c == 0 else lg[:, 0:units] + prod
+    v = in_order()
+    sig = jax.nn.sigmoid(v)
     dpre[...] = (lg[:, 0:units] * sig * (1.0 + v * (1.0 - sig))).astype(BF16)
     step(last)
 

time: 177 us -> 173 us (0.977)
  Pallas kernels: 174 us -> 171 us
    pallas_call x1, Pallas kernels: 173 us -> 169 us  [call_step(): pl.pallas_call(functools.partial(kernel, run, first_col), out_shape=(SD((...]
where the time goes in v7:
time: 173 us
  Pallas kernels  171 us (99%)
  local copies, waits for them, and re-layouts  2.05 us (1%)
    pallas_call x1, Pallas kernels, call_step(): pl.pallas_call(functools.partial(kernel, run, first_col), out_shape=(SD((...  169 us

profile of v7, /device:TPU:1, one launch (start us, length us, event | category | flops | bytes accessed | tf_op | source)
XLA Modules:
  0.0 173.3 jit_solution(5081974677490472050)
XLA Ops:
  0.6 169.1 %distill_step.1 = (bf16[1024,256]{1,0:T(8,128)(2,1)}, bf16[448,512]{1,0:T(8,128)(2,1)}) custom-call(bf16[256,4096]{1,0:T(8,128)(2,1)} %feats.1, f32[1,4096]{1,0:T(1,128)} %bitcast.10, bf16[448,4096]{1,0:T(8,128)(2,1)} %bitcast.7, bf16[448,4096]{1,0:T(8,128)(2,1)} %w_out.1, f32[1,4096]{1,0:T(1,128)} %bitcast.11, bf16[256,1024]{1,0:T(8,128)(2,1)} %hw.1, ...), custom_call_target="tpu_custom_call" | custom-call | flops 10000000000 | bytes 100000000 | tf_op jit(solution)/shard_map/distill_step/pallas_call | solution.py:715
  169.8 0.0 copy-start
  169.8 1.0 copy-done
  170.8 0.0 copy-start.1
  170.8 1.0 copy-done.1
  171.8 1.4 write_out.1
Async XLA Ops:
  169.8 1.0 copy-start
  170.8 1.0 copy-start.1

commit v8 on v7

--- a/solution.py
+++ b/solution.py
@@ -390,6 +390,12 @@
     pp[...] = jnp.zeros(pp.shape, F32)
     pp[0 : pos.shape[0]] = pos[...].astype(F32)
 
+    greeted()
+    send = Sender(send_sem, recv_sem, to)
+    late = send.go(hs, head.at[z, here], "pair")
+    ring = ring_gather(send, z, nz, head, here, there, late)
+    step(ring)
+    swapped = [send.go(tk, tk2, "pair")]
     got_f.wait()
     chunk = 64
 
@@ -401,12 +407,6 @@
         return 0
 
     lax.fori_loop(0, tok // chunk, norm_rows, 0)
-    greeted()
-    send = Sender(send_sem, recv_sem, to)
-    late = send.go(hs, head.at[z, here], "pair")
-    ring = ring_gather(send, z, nz, head, here, there, late)
-    step(ring)
-    swapped = [send.go(tk, tk2, "pair")]
     mine = pl.ds(pl.multiple_of(own_row(bits), BLK), BLK)
     crossed = send.go(normed.at[mine], other.at[at(names, bits)], "YB")
 
@@ -433,7 +433,7 @@
 
     got_b.wait()
     n_buf = bv.shape[1]
-    piece = 1024 if n_buf % 1024 == 0 else n_buf
+    piece = 2048 if n_buf % 2048 == 0 else n_buf
     pos_t = pp[...].T
 
     def ordered_rows(i):

time: 173 us -> 173 us (level)
  no operation moved by 1% of the time
where the time goes in v8:
time: 173 us
  Pallas kernels  170 us (98%)
  local copies, waits for them, and re-layouts  2.05 us (1%)
    pallas_call x1, Pallas kernels, call_step(): pl.pallas_call(functools.partial(kernel, run, first_col), out_shape=(SD((...  169 us

profile of v8, /device:TPU:1, one launch (start us, length us, event | category | flops | bytes accessed | tf_op | source)
XLA Modules:
  0.0 172.8 jit_solution(2632983936272957132)
XLA Ops:
  0.6 168.7 %distill_step.1 = (bf16[1024,256]{1,0:T(8,128)(2,1)}, bf16[448,512]{1,0:T(8,128)(2,1)}) custom-call(bf16[256,4096]{1,0:T(8,128)(2,1)} %feats.1, f32[1,4096]{1,0:T(1,128)} %bitcast.10, bf16[448,4096]{1,0:T(8,128)(2,1)} %bitcast.7, bf16[448,4096]{1,0:T(8,128)(2,1)} %w_out.1, f32[1,4096]{1,0:T(1,128)} %bitcast.11, bf16[256,1024]{1,0:T(8,128)(2,1)} %hw.1, ...), custom_call_target="tpu_custom_call" | custom-call | flops 10000000000 | bytes 100000000 | tf_op jit(solution)/shard_map/distill_step/pallas_call | solution.py:715
  169.3 0.0 copy-start
  169.3 1.0 copy-done
  170.4 0.0 copy-start.1
  170.4 1.0 copy-done.1
  171.4 1.4 write_out.1
Async XLA Ops:
  169.3 1.0 copy-start
  170.4 1.0 copy-start.1
